TPU v7x, 32 devices: a whole 2x2x4 slice. The times are simulated.
32 devices in a mesh: fsdp: 8 (over z, x), tp: 4 (over y, core).
Axes of the slice: x: 2, y: 2, z: 4, core: 2. Of those that a mesh axis runs over, the one named last changes fastest.
Arguments:
- inputs: bfloat16 [4096, 2048], P(('fsdp', 'tp')), may hold values from -6 to 6
- out_grad: bfloat16 [4096, 2048], P(('fsdp', 'tp')), may hold values from -6 to 6
- segments: int32 [4096], P('fsdp'), may hold values from 0 to 4095, as said below
- routes: int32 [4096, 8], P(('fsdp', 'tp')), may hold values from 0 to 31, all different within a row; in each aligned block of 128 rows (0 to 127, 128 to 255, ...) at most 48 rows name the same one
- attn_gain: float32 [2048], replicated, may hold values from 0.25 to 1.75
- w_query: bfloat16 [2048, 2048], P('fsdp', 'tp'), may hold values from -0.125 to 0.125
- w_key: bfloat16 [2048, 2048], P('fsdp', 'tp'), may hold values from -0.125 to 0.125
- w_value: bfloat16 [2048, 2048], P('fsdp', 'tp'), may hold values from -0.125 to 0.125
- w_output: bfloat16 [2048, 2048], P('tp', 'fsdp'), may hold values from -0.75 to 0.75
- moe_gain: float32 [2048], replicated, may hold values from 0.25 to 1.75
- router: bfloat16 [2048, 32], replicated, may hold values from -0.0625 to 0.0625
- w_gate: bfloat16 [32, 2048, 1024], P('fsdp', None, 'tp'), may hold values from -0.125 to 0.125
- w_up: bfloat16 [32, 2048, 1024], P('fsdp', None, 'tp'), may hold values from -0.125 to 0.125
- w_down: bfloat16 [32, 1024, 2048], P('fsdp', 'tp'), may hold values from -0.5 to 0.5
Outputs:
- output: bfloat16 [4096, 2048], P(('fsdp', 'tp'))
- input_grad: float32 [4096, 2048], P(('fsdp', 'tp'))
- attn_gain_grad: float32 [2048], P(('fsdp', 'tp'))
- w_query_grad: float32 [2048, 2048], P('fsdp', 'tp')
- w_key_grad: float32 [2048, 2048], P('fsdp', 'tp')
- w_value_grad: float32 [2048, 2048], P('fsdp', 'tp')
- w_output_grad: float32 [2048, 2048], P('tp', 'fsdp')
- moe_gain_grad: float32 [2048], P(('fsdp', 'tp'))
- router_grad: float32 [2048, 32], P(('fsdp', 'tp'))
- w_gate_grad: float32 [32, 2048, 1024], P('fsdp', None, 'tp')
- w_up_grad: float32 [32, 2048, 1024], P('fsdp', None, 'tp')
- w_down_grad: float32 [32, 1024, 2048], P('fsdp', 'tp')
Inputs may be any that keep to these rules, and one draw needn't show every extreme that they name: `routes`: each row names 8 different experts; in the rows of one device no expert is named more than 48 times. `segments`: numbers never fall along the tokens; a document's tokens are consecutive and lie within one sequence of 512 tokens; sequence i carries numbers from i * 512 to (i + 1) * 512 - 1, its last token the highest of them.
All inputs are finite; a program needn't handle non-finite values.
Results may differ from a plain program's by a relative error of at most 0.025.
Values may be sent and summed in bfloat16 or wider, within the bound.
A program may use at most 320 MiB of HBM per device.

v0:
```python
import math

import jax
import jax.numpy as jnp
from jax import lax
from jax.sharding import PartitionSpec as P

HEAD = 128


EPSILON = 1e-05
HIGHEST = lax.Precision.HIGHEST


def norm_rows(values, gain):
    inverse = lax.rsqrt(jnp.mean(values * values, axis=-1, keepdims=True) + EPSILON)
    return (values * inverse * gain, inverse)


def norm_back(values, inverse, gain, grad):
    scaled = gain * grad
    gain_grad = jnp.sum(grad * values * inverse, axis=0)
    cubed = inverse * inverse * inverse
    values_grad = inverse * scaled - values * cubed * jnp.mean(
        values * scaled, axis=-1, keepdims=True
    )
    return (values_grad, gain_grad)


def contract_last(left, right):
    return lax.dot_general(
        left, right, (((1,), (1,)), ((), ())), preferred_element_type=jnp.float32
    )


def contract_first(left, right):
    return lax.dot_general(
        left, right, (((0,), (0,)), ((), ())), preferred_element_type=jnp.float32
    )


def send_rows(buffer):
    return lax.all_to_all(buffer, "fsdp", split_axis=1, concat_axis=1, tiled=True)


def per_device(
    inputs,
    out_grad,
    segments,
    routes,
    attn_gain,
    w_query,
    w_key,
    w_value,
    w_output,
    moe_gain,
    router,
    w_gate,
    w_up,
    w_down,
):
    tp_count = lax.axis_size("tp")
    fsdp_count = lax.axis_size("fsdp")
    rows_piece, width = inputs.shape
    head_size = HEAD
    full_query, full_key, full_value, full_output = (
        lax.all_gather(w_query, "fsdp", axis=0, tiled=True),
        lax.all_gather(w_key, "fsdp", axis=0, tiled=True),
        lax.all_gather(w_value, "fsdp", axis=0, tiled=True),
        lax.all_gather(w_output, "fsdp", axis=1, tiled=True),
    )
    whole_rows = lax.all_gather(inputs, "tp", axis=0, tiled=True)
    seq_len = whole_rows.shape[0]
    whole_float = whole_rows.astype(jnp.float32)
    normed_one, inverse_one = norm_rows(whole_float, attn_gain)
    act_one = normed_one.astype(jnp.bfloat16)
    local_heads = full_query.shape[1] // head_size
    query = (
        jnp.dot(act_one, full_query, preferred_element_type=jnp.float32)
        .astype(jnp.bfloat16)
        .reshape(seq_len, local_heads, head_size)
    )
    key_rows = (
        jnp.dot(act_one, full_key, preferred_element_type=jnp.float32)
        .astype(jnp.bfloat16)
        .reshape(seq_len, local_heads, head_size)
    )
    value_rows = (
        jnp.dot(act_one, full_value, preferred_element_type=jnp.float32)
        .astype(jnp.bfloat16)
        .reshape(seq_len, local_heads, head_size)
    )
    block_rows = min(512, seq_len)
    score_scale = 1.0 / math.sqrt(head_size)

    def block_scores(query_block):
        scores = (
            jnp.einsum("qhd,khd->hqk", query_block, key_rows, preferred_element_type=jnp.float32)
            * score_scale
        )
        same_doc = segments[:, None] == segments[None, :]
        return jnp.where(same_doc[None], scores, -1e30)

    scores = block_scores(query)
    peak = jnp.max(scores, axis=-1, keepdims=True)
    expo = jnp.exp(scores - peak)
    total = jnp.sum(expo, axis=-1, keepdims=True)
    softmax_rows = (expo / total).astype(jnp.bfloat16)
    block_outputs = jnp.einsum(
        "hqk,khd->qhd", softmax_rows, value_rows, preferred_element_type=jnp.float32
    )
    log_totals = [peak + jnp.log(total)]
    attended = block_outputs.reshape(seq_len, -1).astype(jnp.bfloat16)
    branch = lax.psum_scatter(
        jnp.dot(attended, full_output, preferred_element_type=jnp.float32).astype(jnp.bfloat16),
        "tp",
        scatter_dimension=0,
        tiled=True,
    ).astype(jnp.float32)
    resid = inputs.astype(jnp.float32) + branch
    normed_two, inverse_two = norm_rows(resid, moe_gain)
    act_two = normed_two.astype(jnp.bfloat16)
    local_experts = w_gate.shape[0]
    experts = local_experts * fsdp_count
    top_k = routes.shape[1]
    capacity = 3 * rows_piece * top_k // (2 * experts)
    logits = jnp.dot(act_two, router, preferred_element_type=jnp.float32)
    picks = (routes[:, :, None] == jnp.arange(experts, dtype=jnp.int32)[None, None, :]).astype(
        jnp.float32
    )
    chosen = jnp.einsum("tke,te->tk", picks, logits, precision=HIGHEST)
    gates = jax.nn.softmax(chosen, axis=-1)
    flat_routes = routes.reshape(-1)
    route_count = flat_routes.shape[0]
    hits = (flat_routes[:, None] == jnp.arange(experts, dtype=jnp.int32)[None, :]).astype(jnp.int32)
    ranks = jnp.sum((jnp.cumsum(hits, axis=0) - 1) * hits, axis=1)
    slots = flat_routes * capacity + ranks
    sources = (
        jnp.full((experts * capacity,), route_count, jnp.int32)
        .at[slots]
        .set(jnp.arange(route_count, dtype=jnp.int32))
    )
    padded_act = jnp.concatenate([act_two, jnp.zeros((1, width), jnp.bfloat16)], 0)
    send_buffer = padded_act[sources // top_k].reshape(
        1, fsdp_count, local_experts * capacity, width
    )
    gate_full, up_full, down_full = (
        lax.all_gather(w_gate, "tp", axis=2, tiled=True),
        lax.all_gather(w_up, "tp", axis=2, tiled=True),
        lax.all_gather(w_down, "tp", axis=1, tiled=True),
    )
    own_in = send_rows(send_buffer)
    own_rows = own_in.reshape(fsdp_count, local_experts, capacity, width)
    own_gate = jnp.einsum("secd,edf->secf", own_rows, gate_full, preferred_element_type=jnp.float32)
    own_up = jnp.einsum("secd,edf->secf", own_rows, up_full, preferred_element_type=jnp.float32)
    own_sigmoid = jax.nn.sigmoid(own_gate)
    own_silu = own_gate * own_sigmoid
    own_hidden = (own_silu * own_up).astype(jnp.bfloat16)
    own_out = jnp.einsum(
        "secf,efd->secd", own_hidden, down_full, preferred_element_type=jnp.float32
    )
    expert_out = own_out.reshape(1, fsdp_count, local_experts * capacity, width).astype(
        jnp.bfloat16
    )
    returned = lax.all_to_all(expert_out, "fsdp", split_axis=1, concat_axis=1, tiled=True).reshape(
        experts * capacity, width
    )
    routed = returned[slots].reshape(rows_piece, top_k, width).astype(jnp.float32)
    mixture = jnp.sum(gates[:, :, None] * routed, axis=1)
    output = (resid + mixture).astype(jnp.bfloat16)
    grad_float = out_grad.astype(jnp.float32)
    gate_grad = jnp.sum(routed * grad_float[:, None, :], axis=2)
    route_grad = (
        (gates[:, :, None] * grad_float[:, None, :])
        .astype(jnp.bfloat16)
        .reshape(route_count, width)
    )
    padded_grad = jnp.concatenate([route_grad, jnp.zeros((1, width), jnp.bfloat16)], 0)
    grad_buffer = padded_grad[sources].reshape(1, fsdp_count, local_experts * capacity, width)
    own_grads = send_rows(grad_buffer).reshape(fsdp_count, local_experts, capacity, width)
    own_hidden_grad = jnp.einsum(
        "secd,efd->secf", own_grads, down_full, preferred_element_type=jnp.float32
    )
    own_gate_low = (
        own_hidden_grad * own_up * own_sigmoid * (1.0 + own_gate * (1.0 - own_sigmoid))
    ).astype(jnp.bfloat16)
    own_up_low = (own_hidden_grad * own_silu).astype(jnp.bfloat16)
    down_term = jnp.einsum(
        "secf,secd->efd", own_hidden, own_grads, preferred_element_type=jnp.float32
    )
    gate_term = jnp.einsum(
        "secd,secf->edf", own_rows, own_gate_low, preferred_element_type=jnp.float32
    )
    up_term = jnp.einsum("secd,secf->edf", own_rows, own_up_low, preferred_element_type=jnp.float32)
    w_gate_grad, w_up_grad, w_down_grad = (
        lax.psum_scatter(
            gate_term.astype(jnp.bfloat16), "tp", scatter_dimension=2, tiled=True
        ).astype(jnp.float32),
        lax.psum_scatter(
            up_term.astype(jnp.bfloat16), "tp", scatter_dimension=2, tiled=True
        ).astype(jnp.float32),
        lax.psum_scatter(
            down_term.astype(jnp.bfloat16), "tp", scatter_dimension=1, tiled=True
        ).astype(jnp.float32),
    )
    own_back = jnp.einsum(
        "secf,edf->secd", own_gate_low, gate_full, preferred_element_type=jnp.float32
    )
    own_back = own_back + jnp.einsum(
        "secf,edf->secd", own_up_low, up_full, preferred_element_type=jnp.float32
    )
    expert_grad = own_back.reshape(1, fsdp_count, local_experts * capacity, width).astype(
        jnp.bfloat16
    )
    back_rows = lax.all_to_all(
        expert_grad, "fsdp", split_axis=1, concat_axis=1, tiled=True
    ).reshape(experts * capacity, width)
    act_two_grad = jnp.sum(
        back_rows[slots].reshape(rows_piece, top_k, width).astype(jnp.float32), axis=1
    )
    centered = gate_grad - jnp.sum(gates * gate_grad, axis=1, keepdims=True)
    chosen_grad = gates * centered
    logit_grad = jnp.einsum("tke,tk->te", picks, chosen_grad, precision=HIGHEST)
    router_float = router.astype(jnp.float32)
    act_two_grad = act_two_grad + lax.dot_general(
        logit_grad, router_float, (((1,), (1,)), ((), ())), precision=HIGHEST
    )
    router_part = lax.dot_general(
        act_two.astype(jnp.float32), logit_grad, (((0,), (0,)), ((), ())), precision=HIGHEST
    )
    resid_part, gain_two_part = norm_back(resid, inverse_two, moe_gain, act_two_grad)
    resid_grad = grad_float + resid_part
    branch_grad = lax.all_gather(resid_grad.astype(jnp.bfloat16), "tp", axis=0, tiled=True)
    attended_grad = (
        contract_last(branch_grad, full_output)
        .astype(jnp.bfloat16)
        .reshape(seq_len, local_heads, head_size)
    )
    w_output_part = contract_first(attended, branch_grad)
    query_parts = []
    key_grad = jnp.zeros((seq_len, local_heads, head_size), jnp.float32)
    value_grad = jnp.zeros((seq_len, local_heads, head_size), jnp.float32)
    for block_index, first_row in enumerate(range(0, seq_len, block_rows)):
        query_block = query
        scores = block_scores(query_block)
        softmax_rows = jnp.exp(scores - log_totals[block_index])
        prob_grad = jnp.einsum(
            "qhd,khd->hqk", attended_grad, value_rows, preferred_element_type=jnp.float32
        )
        inner = jnp.sum(softmax_rows * prob_grad, axis=-1, keepdims=True)
        score_grad = (softmax_rows * (prob_grad - inner) * score_scale).astype(jnp.bfloat16)
        query_parts.append(
            jnp.einsum("hqk,khd->qhd", score_grad, key_rows, preferred_element_type=jnp.float32)
        )
        key_grad = jnp.einsum(
            "hqk,qhd->khd", score_grad, query_block, preferred_element_type=jnp.float32
        )
        value_grad = jnp.einsum(
            "hqk,qhd->khd",
            softmax_rows.astype(jnp.bfloat16),
            attended_grad,
            preferred_element_type=jnp.float32,
        )
    query_low = query_parts[0].reshape(seq_len, -1).astype(jnp.bfloat16)
    key_low = key_grad.reshape(seq_len, -1).astype(jnp.bfloat16)
    value_low = value_grad.reshape(seq_len, -1).astype(jnp.bfloat16)
    w_query_part = contract_first(act_one, query_low)
    w_key_part = contract_first(act_one, key_low)
    w_value_part = contract_first(act_one, value_low)
    act_one_grad = (
        contract_last(query_low, full_query)
        + contract_last(key_low, full_key)
        + contract_last(value_low, full_value)
    )
    whole_part, gain_one_part = norm_back(whole_float, inverse_one, attn_gain, act_one_grad)

    def arrange(values):
        shaped = values.reshape((fsdp_count, tp_count, -1) + values.shape[1:])
        return jnp.swapaxes(shaped, 0, 1)

    input_part, gain_one_tp, gain_two_tp, router_tp = (
        lax.psum_scatter(
            whole_part.astype(jnp.bfloat16), "tp", scatter_dimension=0, tiled=True
        ).astype(jnp.float32),
        lax.psum_scatter(
            arrange(gain_one_part).astype(jnp.bfloat16), "tp", scatter_dimension=0, tiled=True
        ).astype(jnp.float32),
        lax.psum_scatter(
            arrange(gain_two_part).astype(jnp.bfloat16), "tp", scatter_dimension=0, tiled=True
        ).astype(jnp.float32),
        lax.psum_scatter(
            arrange(router_part).astype(jnp.bfloat16), "tp", scatter_dimension=0, tiled=True
        ).astype(jnp.float32),
    )
    input_grad = resid_grad + input_part
    query_sum, key_sum, value_sum, output_sum, gain_one_sum, gain_two_sum, router_sum = (
        lax.psum_scatter(
            w_query_part.astype(jnp.bfloat16), "fsdp", scatter_dimension=0, tiled=True
        ).astype(jnp.float32),
        lax.psum_scatter(
            w_key_part.astype(jnp.bfloat16), "fsdp", scatter_dimension=0, tiled=True
        ).astype(jnp.float32),
        lax.psum_scatter(
            w_value_part.astype(jnp.bfloat16), "fsdp", scatter_dimension=0, tiled=True
        ).astype(jnp.float32),
        lax.psum_scatter(
            w_output_part.astype(jnp.bfloat16), "fsdp", scatter_dimension=1, tiled=True
        ).astype(jnp.float32),
        lax.psum_scatter(
            gain_one_tp.astype(jnp.bfloat16), "fsdp", scatter_dimension=1, tiled=True
        ).astype(jnp.float32),
        lax.psum_scatter(
            gain_two_tp.astype(jnp.bfloat16), "fsdp", scatter_dimension=1, tiled=True
        ).astype(jnp.float32),
        lax.psum_scatter(
            router_tp.astype(jnp.bfloat16), "fsdp", scatter_dimension=1, tiled=True
        ).astype(jnp.float32),
    )
    return (
        output,
        input_grad,
        gain_one_sum.reshape(-1),
        query_sum,
        key_sum,
        value_sum,
        output_sum,
        gain_two_sum.reshape(-1),
        router_sum.reshape(-1, experts),
        w_gate_grad,
        w_up_grad,
        w_down_grad,
    )


def solution(mesh):
    return jax.shard_map(
        per_device,
        mesh=mesh,
        in_specs=(
            P(("fsdp", "tp"), None),
            P(("fsdp", "tp"), None),
            P("fsdp"),
            P(("fsdp", "tp"), None),
            P(),
            P("fsdp", "tp"),
            P("fsdp", "tp"),
            P("fsdp", "tp"),
            P("tp", "fsdp"),
            P(),
            P(),
            P("fsdp", None, "tp"),
            P("fsdp", None, "tp"),
            P("fsdp", "tp", None),
        ),
        out_specs=(
            P(("fsdp", "tp"), None),
            P(("fsdp", "tp"), None),
            P(("fsdp", "tp")),
            P("fsdp", "tp"),
            P("fsdp", "tp"),
            P("fsdp", "tp"),
            P("tp", "fsdp"),
            P(("fsdp", "tp")),
            P(("fsdp", "tp"), None),
            P("fsdp", None, "tp"),
            P("fsdp", None, "tp"),
            P("fsdp", "tp", None),
        ),
        check_vma=False,
    )
```

profile of v0, /device:TPU:2, one launch (start us, length us, event | category | flops | bytes accessed | tf_op | source)
XLA Modules:
  0.0 1763.7 jit_solution(13823056930193630111)
XLA Ops:
  11.6 21.8 %all-gather.10.cloned.1.call-done = bf16[512,2048]{1,0:T(8,128)(2,1)} async-done(((bf16[128,2048]{1,0:T(8,128)(2,1)}), bf16[512,2048]{1,0:T(8,128)(2,1)}) %all-gather.10.cloned.1.call-update) | async-done | bytes 2097168 | tf_op jit(solution)/shard_map/all_gather | solution.py:72
  36.1 47.9 %all-gather.14.cloned.1.call-done = bf16[2048,512]{1,0:T(8,128)(2,1)} async-done(((bf16[256,512]{1,0:T(8,128)(2,1)}), bf16[2048,512]{1,0:T(8,128)(2,1)}) %all-gather.14.cloned.1.call-update) | async-done | bytes 2097168 | tf_op jit(solution)/shard_map/all_gather | solution.py:67
  84.0 3.6 convolution_convert_fusion.8
  87.6 46.3 %all-gather.16.cloned.1.call-done = bf16[2048,512]{1,0:T(8,128)(2,1)} async-done(((bf16[256,512]{1,0:T(8,128)(2,1)}), bf16[2048,512]{1,0:T(8,128)(2,1)}) %all-gather.16.cloned.1.call-update) | async-done | bytes 2097168 | tf_op jit(solution)/shard_map/all_gather | solution.py:68
  133.9 3.0 convolution_convert_fusion.7
  140.6 43.1 %all-gather.12.cloned.1.call-done = bf16[2048,512]{1,0:T(8,128)(2,1)} async-done(((bf16[256,512]{1,0:T(8,128)(2,1)}), bf16[2048,512]{1,0:T(8,128)(2,1)}) %all-gather.12.cloned.1.call-update) | async-done | bytes 2097168 | tf_op jit(solution)/shard_map/all_gather | solution.py:69
  183.7 3.1 convolution_convert_fusion.9
  188.6 47.5 %all-gather.18.cloned.1.call-done = bf16[512,2048]{1,0:T(8,128)(2,1)} async-done(((bf16[512,256]{1,0:T(8,128)(2,1)}), bf16[512,2048]{1,0:T(8,128)(2,1)}) %all-gather.18.cloned.1.call-update) | async-done | bytes 2097168 | tf_op jit(solution)/shard_map/all_gather | solution.py:70
  236.1 4.2 convolution_convert_fusion.4
  243.1 9.0 reduce-window.6
  252.6 4.3 scatter_custom_fusion
  257.0 13.2 reduce-scatter.12.cloned.1.call-done
  273.3 7.0 gather_fusion
  280.3 6.4 all-to-all-start
  291.5 15.5 gather_fusion.2
  307.0 117.3 %all-to-all-done = bf16[1,8,192,2048]{3,2,0,1:T(8,128)(2,1)} async-done(((bf16[1,8,192,2048]{3,2,0,1:T(8,128)(2,1)}), bf16[1,8,192,2048]{3,2,0,1:T(8,128)(2,1)}, u32[]{:S(2)}, u32[]{:S(2)}) %all-to-all-start) | async-done | bytes 6291488 | tf_op jit(solution)/shard_map/all_to_all | solution.py:43
  424.3 5.2 all-to-all-start.2
  429.5 15.3 fusion.3
  444.8 45.0 %all-gather.20.cloned.1.call-done = bf16[4,2048,1024]{2,1,0:T(8,128)(2,1)} async-done(((bf16[4,2048,256]{2,1,0:T(8,128)(2,1)}), bf16[4,2048,1024]{2,1,0:T(8,128)(2,1)}) %all-gather.20.cloned.1.call-update) | async-done | bytes 16777232 | tf_op jit(solution)/shard_map/all_gather | solution.py:148
  489.8 15.3 fusion.7
  505.0 61.3 %all-to-all-done.2 = bf16[1,8,192,2048]{3,2,0,1:T(8,128)(2,1)} async-done(((bf16[1,8,192,2048]{3,2,0,1:T(8,128)(2,1)}), bf16[1,8,192,2048]{3,2,0,1:T(8,128)(2,1)}, u32[]{:S(2)}, u32[]{:S(2)}) %all-to-all-start.2) | async-done | bytes 6291488 | tf_op jit(solution)/shard_map/all_to_all | solution.py:43
  566.4 31.0 %all-gather.24.cloned.1.call-done = bf16[4,1024,2048]{2,1,0:T(8,128)(2,1)} async-done(((bf16[4,256,2048]{2,1,0:T(8,128)(2,1)}), bf16[4,1024,2048]{2,1,0:T(8,128)(2,1)}) %all-gather.24.cloned.1.call-update) | async-done | bytes 16777232 | tf_op jit(solution)/shard_map/all_gather | solution.py:150
  597.4 17.7 %fusion.19 = (bf16[8,4,48,1024]{3,2,0,1:T(8,128)(2,1)}, bf16[8,4,48,1024]{3,2,0,1:T(8,128)(2,1)S(1)}, bf16[8,4,48,1024]{3,2,0,1:T(8,128)(2,1)}) fusion(f32[4,8,48,1024]{3,2,1,0:T(8,128)} %fusion.3, f32[4,8,48,1024]{3,2,1,0:T(8,128)} %fusion.7, bf16[4,1024,2048]{2,1,0:T(8,128)(2,1)} %all-gather.24.cloned.1.call-done, bf16[8,4,48,2048]{3,2,1,0:T(8,128)(2,1)} %bitcast.31), kind=kOutput, calls=%fused_computation.39 | convolution fusion | flops 6466043904 | bytes 45088768 | tf_op jit(solution)/shard_map/secd,efd->secf/dot_general | solution.py:181
  615.1 14.1 convert_bitcast_fusion
  629.2 3.3 copy.71
  632.5 6.5 all-to-all-start.1
  639.0 13.9 fusion.1
  652.9 15.8 fusion.16
  668.7 6.6 copy.75
  675.3 101.7 %all-to-all-done.1 = bf16[1,8,192,2048]{3,2,0,1:T(8,128)(2,1)} async-done(((bf16[1,8,192,2048]{3,2,0,1:T(8,128)(2,1)}), bf16[1,8,192,2048]{3,2,0,1:T(8,128)(2,1)}, u32[]{:S(2)}, u32[]{:S(2)}) %all-to-all-start.1) | async-done | bytes 6291488 | tf_op jit(solution)/shard_map/all_to_all | solution.py:165
  777.0 5.2 all-to-all-start.3
  782.4 12.4 gather_fusion.1
  794.8 4.9 fusion.14
  801.1 118.5 %all-to-all-done.3 = bf16[1,8,192,2048]{3,2,0,1:T(8,128)(2,1)} async-done(((bf16[1,8,192,2048]{3,2,0,1:T(8,128)(2,1)}), bf16[1,8,192,2048]{3,2,0,1:T(8,128)(2,1)}, u32[]{:S(2)}, u32[]{:S(2)}) %all-to-all-start.3) | async-done | bytes 6291488 | tf_op jit(solution)/shard_map/all_to_all | solution.py:215
  919.5 12.4 gather_fusion.3
  932.0 5.1 convert_reduce_fusion
  940.1 3.0 fusion.103
  943.2 15.1 reduce-scatter.24.cloned.1.call-done
  958.7 24.5 %all-gather.26.cloned.1.call-done = bf16[512,2048]{1,0:T(8,128)(2,1)} async-done(((bf16[128,2048]{1,0:T(8,128)(2,1)}), bf16[512,2048]{1,0:T(8,128)(2,1)}) %all-gather.26.cloned.1.call-update) | async-done | bytes 2097168 | tf_op jit(solution)/shard_map/all_gather | solution.py:233
  983.1 4.3 convolution_convert_fusion
  987.6 3.0 convolution_convert_fusion.6
  992.2 2.8 convolution_convert_fusion.1
  995.1 3.8 fusion.106
  998.9 8.2 fusion.70
  1007.2 2.8 convolution_convert_fusion.3
  1010.0 9.1 fusion.73
  1019.1 3.9 convolution_convert_fusion.2
  1023.4 3.0 fusion.107
  1028.1 2.4 fusion.42
  1032.9 15.6 bitcast_convert_fusion
  1050.4 15.3 bitcast_convert_fusion.2
  1067.6 15.3 bitcast_convert_fusion.1
  1086.2 10.4 all-reduce.7
  1097.3 18.3 %all-reduce.6 = (bf16[1,8,64]{2,0,1:T(2,128)(2,1)S(1)}, bf16[1,8,64]{2,0,1:T(2,128)(2,1)S(1)}) all-reduce(bf16[1,8,64]{2,0,1:T(2,128)(2,1)S(1)} %copy.83, bf16[1,8,64]{2,0,1:T(2,128)(2,1)S(1)} %copy.85), channel_id=5, replica_groups=mesh['fsdp'=8,'tp'=4] {'fsdp'}, use_global_device_ids=true, to_apply=%region_21.22.clone | all-reduce | flops 1024 | bytes 4096
  1119.9 68.4 %reduce-scatter.20.cloned.1.call-done = bf16[256,512]{1,0:T(8,128)(2,1)} async-done(((bf16[2048,512]{1,0:T(8,128)(2,1)}), bf16[256,512]{1,0:T(8,128)(2,1)}) %reduce-scatter.20.cloned.1.call-update) | async-done | bytes 262160 | tf_op jit(solution)/shard_map/reduce_scatter | solution.py:303
  1190.1 69.1 %reduce-scatter.16.cloned.1.call-done = bf16[256,512]{1,0:T(8,128)(2,1)} async-done(((bf16[2048,512]{1,0:T(8,128)(2,1)}), bf16[256,512]{1,0:T(8,128)(2,1)}) %reduce-scatter.16.cloned.1.call-update) | async-done | bytes 262160 | tf_op jit(solution)/shard_map/reduce_scatter | solution.py:297
  1260.9 69.0 %reduce-scatter.18.cloned.1.call-done = bf16[256,512]{1,0:T(8,128)(2,1)} async-done(((bf16[2048,512]{1,0:T(8,128)(2,1)}), bf16[256,512]{1,0:T(8,128)(2,1)}) %reduce-scatter.18.cloned.1.call-update) | async-done | bytes 262160 | tf_op jit(solution)/shard_map/reduce_scatter | solution.py:300
  1331.8 32.3 %reduce-scatter.14.cloned.1.call-done = bf16[128,2048]{1,0:T(8,128)(2,1)} async-done(((bf16[512,2048]{1,0:T(8,128)(2,1)}), bf16[128,2048]{1,0:T(8,128)(2,1)}) %reduce-scatter.14.cloned.1.call-update) | async-done | bytes 524304 | tf_op jit(solution)/shard_map/reduce_scatter | solution.py:282
  1366.2 126.6 %reduce-scatter.32.cloned.1.call-done = bf16[4,256,2048]{2,1,0:T(8,128)(2,1)} async-done(((bf16[4,1024,2048]{2,1,0:T(8,128)(2,1)}), bf16[4,256,2048]{2,1,0:T(8,128)(2,1)}) %reduce-scatter.32.cloned.1.call-update) | async-done | bytes 4194320 | tf_op jit(solution)/shard_map/reduce_scatter | solution.py:202
  1492.9 6.7 convert_element_type.306
  1499.5 122.1 %reduce-scatter.28.cloned.1.call-done = bf16[4,2048,256]{2,1,0:T(8,128)(2,1)} async-done(((bf16[4,2048,1024]{2,1,0:T(8,128)(2,1)}), bf16[4,2048,256]{2,1,0:T(8,128)(2,1)}) %reduce-scatter.28.cloned.1.call-update) | async-done | bytes 4194320 | tf_op jit(solution)/shard_map/reduce_scatter | solution.py:196
  1621.6 6.4 convert_element_type.302
  1627.9 122.4 %reduce-scatter.30.cloned.1.call-done = bf16[4,2048,256]{2,1,0:T(8,128)(2,1)} async-done(((bf16[4,2048,1024]{2,1,0:T(8,128)(2,1)}), bf16[4,2048,256]{2,1,0:T(8,128)(2,1)}) %reduce-scatter.30.cloned.1.call-update) | async-done | bytes 4194320 | tf_op jit(solution)/shard_map/reduce_scatter | solution.py:199
  1750.3 6.3 convert_element_type.304
  (192 shorter events, 54.0 us)
Async XLA Ops:
  7.2 279.6 %copy-start = (bf16[2048,32]{0,1:T(8,128)(2,1)S(1)}, bf16[2048,32]{0,1:T(8,128)(2,1)}, u32[]{:S(2)}) copy-start(bf16[2048,32]{0,1:T(8,128)(2,1)} %param.24) | copy-start | bytes 393220
  7.2 26.2 %all-gather.10.cloned.1.call-start = ((), (), s32[]{:S(2)}) async-start(), calls=%async_computation.15 | async-start | bytes 2621440 | tf_op jit(solution)/shard_map/all_gather | solution.py:72
  7.9 76.0 %all-gather.14.cloned.1.call-start = ((), (), s32[]{:S(2)}) async-start(), calls=%async_computation.17 | async-start | bytes 2359296 | tf_op jit(solution)/shard_map/all_gather | solution.py:67
  8.7 125.2 %all-gather.16.cloned.1.call-start = ((), (), s32[]{:S(2)}) async-start(), calls=%async_computation.18 | async-start | bytes 2359296 | tf_op jit(solution)/shard_map/all_gather | solution.py:68
  9.4 174.3 %all-gather.12.cloned.1.call-start = ((), (), s32[]{:S(2)}) async-start(), calls=%async_computation.16 | async-start | bytes 2359296 | tf_op jit(solution)/shard_map/all_gather | solution.py:69
  10.0 226.1 %all-gather.18.cloned.1.call-start = ((), (), s32[]{:S(2)}) async-start(), calls=%async_computation.19 | async-start | bytes 2359296 | tf_op jit(solution)/shard_map/all_gather | solution.py:70
  10.6 259.6 %reduce-scatter.12.cloned.1.call-start = ((), (), s32[]{:S(2)}) async-start(), calls=%async_computation.20 | async-start | bytes 2621440 | tf_op jit(solution)/shard_map/reduce_scatter | solution.py:114
  35.5 98.4 %copy-start.5 = (bf16[512,2048]{1,0:T(8,128)(2,1)S(1)}, bf16[512,2048]{1,0:T(8,128)(2,1)}, u32[]{:S(2)}) copy-start(bf16[512,2048]{1,0:T(8,128)(2,1)} %all-gather.10.cloned.1.call-done) | copy-start | bytes 6291460
  35.5 98.4 %copy-start.22 = (f32[2048]{0:T(1024)S(1)}, f32[2048]{0:T(1024)}, u32[]{:S(2)}) copy-start(f32[2048]{0:T(1024)} %param.18) | copy-start | bytes 24580
  36.1 147.6 %copy-start.26 = (f32[512]{0:T(512)}, f32[512]{0:T(512)S(1)}, u32[]{:S(2)}) copy-start(f32[512]{0:T(512)S(1)} %get-tuple-element.31) | copy-start | bytes 6148
  87.6 50.3 %copy-start.16 = (bf16[512,512]{0,1:T(8,128)(2,1)}, bf16[512,512]{0,1:T(8,128)(2,1)S(1)}, u32[]{:S(2)}) copy-start(bf16[512,512]{0,1:T(8,128)(2,1)S(1)} %convolution_convert_fusion.8) | copy-start | bytes 1572868
  136.9 1.0 copy-start.17
  137.9 2.1 copy-start.2
  137.9 48.9 %copy-start.20 = (f32[4,512]{1,0:T(4,128)}, f32[4,512]{1,0:T(4,128)S(1)}, u32[]{:S(2)}) copy-start(f32[4,512]{1,0:T(4,128)S(1)} %get-tuple-element.34) | copy-start | bytes 24580
  140.6 48.0 %copy-start.24 = (f32[4,512]{1,0:T(4,128)}, f32[4,512]{1,0:T(4,128)S(1)}, u32[]{:S(2)}) copy-start(f32[4,512]{1,0:T(4,128)S(1)} %fusion.44) | copy-start | bytes 24580
  183.7 3.9 copy-start.3
  186.8 0.8 copy-start.15
  188.6 52.5 %copy-start.34 = (bf16[4,128,512]{2,1,0:T(8,128)(2,1)}, bf16[4,128,512]{2,1,0:T(8,128)(2,1)S(1)}, u32[]{:S(2)}) copy-start(bf16[4,128,512]{2,1,0:T(8,128)(2,1)S(1)} %fusion.69) | copy-start | bytes 1572868
  240.3 189.2 %all-gather.22.cloned.1.call-start = ((), (), s32[]{:S(2)}) async-start(), calls=%async_computation.22 | async-start | bytes 20971520 | tf_op jit(solution)/shard_map/all_gather | solution.py:149
  241.0 1.5 copy-start.28
  241.1 29.1 %copy-start.7 = (bf16[128,2048]{1,0:T(8,128)(2,1)S(1)}, bf16[128,2048]{1,0:T(8,128)(2,1)}, u32[]{:S(2)}) copy-start(bf16[128,2048]{1,0:T(8,128)(2,1)} %param.14) | copy-start | bytes 1572868
  241.1 248.7 %all-gather.20.cloned.1.call-start = ((), (), s32[]{:S(2)}) async-start(), calls=%async_computation.21 | async-start | bytes 20971520 | tf_op jit(solution)/shard_map/all_gather | solution.py:148
  241.8 30.2 %copy-start.18 = (f32[2048]{0:T(1024)S(1)}, f32[2048]{0:T(1024)}, u32[]{:S(2)}) copy-start(f32[2048]{0:T(1024)} %param.23) | copy-start | bytes 24580
  241.8 355.6 %all-gather.24.cloned.1.call-start = ((), (), s32[]{:S(2)}) async-start(), calls=%async_computation.23 | async-start | bytes 20971520 | tf_op jit(solution)/shard_map/all_gather | solution.py:150
  272.0 8.3 copy-start.30
  280.3 6.4 copy-start.12
  280.3 144.1 %all-to-all-start = ((bf16[1,8,192,2048]{3,2,0,1:T(8,128)(2,1)}), bf16[1,8,192,2048]{3,2,0,1:T(8,128)(2,1)}, u32[]{:S(2)}, u32[]{:S(2)}) async-start(bf16[1,8,192,2048]{3,2,0,1:T(8,128)(2,1)} %bitcast.209), calls=%async_computation.1 | async-start | bytes 12582912 | tf_op jit(solution)/shard_map/all_to_all | solution.py:43
  424.3 142.0 %all-to-all-start.2 = ((bf16[1,8,192,2048]{3,2,0,1:T(8,128)(2,1)}), bf16[1,8,192,2048]{3,2,0,1:T(8,128)(2,1)}, u32[]{:S(2)}, u32[]{:S(2)}) async-start(bf16[1,8,192,2048]{3,2,0,1:T(8,128)(2,1)} %bitcast.210), calls=%async_computation.3 | async-start | bytes 12582912 | tf_op jit(solution)/shard_map/all_to_all | solution.py:43
  615.1 14.1 copy-start.39
  632.5 144.6 %all-to-all-start.1 = ((bf16[1,8,192,2048]{3,2,0,1:T(8,128)(2,1)}), bf16[1,8,192,2048]{3,2,0,1:T(8,128)(2,1)}, u32[]{:S(2)}, u32[]{:S(2)}) async-start(bf16[1,8,192,2048]{3,2,0,1:T(8,128)(2,1)} %bitcast.208), calls=%async_computation.2 | async-start | bytes 12582912 | tf_op jit(solution)/shard_map/all_to_all | solution.py:165
  777.0 142.5 %all-to-all-start.3 = ((bf16[1,8,192,2048]{3,2,0,1:T(8,128)(2,1)}), bf16[1,8,192,2048]{3,2,0,1:T(8,128)(2,1)}, u32[]{:S(2)}, u32[]{:S(2)}) async-start(bf16[1,8,192,2048]{3,2,0,1:T(8,128)(2,1)} %bitcast.207), calls=%async_computation.4 | async-start | bytes 12582912 | tf_op jit(solution)/shard_map/all_to_all | solution.py:215
  782.2 176.1 %reduce-scatter.24.cloned.1.call-start = ((), (), s32[]{:S(2)}) async-start(), calls=%async_computation.30 | async-start | bytes 327680 | tf_op jit(solution)/shard_map/reduce_scatter | solution.py:291
  931.9 5.2 copy-start.8
  931.9 5.2 copy-start.9
  931.9 5.2 copy-start.19
  932.0 5.2 copy-start.31
  932.0 8.2 copy-start.32
  940.1 43.1 %all-gather.26.cloned.1.call-start = ((), (), s32[]{:S(2)}) async-start(), calls=%async_computation.24 | async-start | bytes 2621440 | tf_op jit(solution)/shard_map/all_gather | solution.py:233
  943.1 141.7 %reduce-scatter.26.cloned.1.call-start = ((), (), s32[]{:S(2)}) async-start(), calls=%async_computation.31 | async-start | bytes 73728 | tf_op jit(solution)/shard_map/reduce_scatter | solution.py:315
  958.4 29.2 %copy-start.21 = (f32[4,512]{1,0:T(4,128)S(1)}, f32[4,512]{1,0:T(4,128)}, u32[]{:S(2)}) copy-start(f32[4,512]{1,0:T(4,128)} %copy-done.20) | copy-start | bytes 24580
  958.4 29.2 %copy-start.25 = (f32[4,512]{1,0:T(4,128)S(1)}, f32[4,512]{1,0:T(4,128)}, u32[]{:S(2)}) copy-start(f32[4,512]{1,0:T(4,128)} %copy-done.24) | copy-start | bytes 24580
  958.4 29.2 %copy-start.33 = (bf16[512,2048]{1,0:T(8,128)(2,1)S(1)}, bf16[512,2048]{1,0:T(8,128)(2,1)}, u32[]{:S(2)}) copy-start(bf16[512,2048]{1,0:T(8,128)(2,1)} %all-gather.18.cloned.1.call-done) | copy-start | bytes 6291460
  958.4 159.7 %reduce-scatter.22.cloned.1.call-start = ((), (), s32[]{:S(2)}) async-start(), calls=%async_computation.29 | async-start | bytes 2359296 | tf_op jit(solution)/shard_map/reduce_scatter | solution.py:306
  987.5 200.8 %reduce-scatter.20.cloned.1.call-start = ((), (), s32[]{:S(2)}) async-start(), calls=%async_computation.28 | async-start | bytes 2359296 | tf_op jit(solution)/shard_map/reduce_scatter | solution.py:303
  987.6 3.1 copy-start.4
  990.6 1.6 copy-start.6
  990.6 1.6 copy-start.23
  990.6 1.6 copy-start.27
  995.0 264.1 %reduce-scatter.16.cloned.1.call-start = ((), (), s32[]{:S(2)}) async-start(), calls=%async_computation.26 | async-start | bytes 2359296 | tf_op jit(solution)/shard_map/reduce_scatter | solution.py:297
  1010.0 320.0 %reduce-scatter.18.cloned.1.call-start = ((), (), s32[]{:S(2)}) async-start(), calls=%async_computation.27 | async-start | bytes 2359296 | tf_op jit(solution)/shard_map/reduce_scatter | solution.py:300
  1023.0 341.1 %reduce-scatter.14.cloned.1.call-start = ((), (), s32[]{:S(2)}) async-start(), calls=%async_computation.25 | async-start | bytes 2621440 | tf_op jit(solution)/shard_map/reduce_scatter | solution.py:282
  1023.4 3.1 copy-start.13
  1023.4 3.1 copy-start.14
  1026.5 1.6 copy-start.11
  1028.1 2.4 copy-start.29
  1032.9 460.0 %reduce-scatter.32.cloned.1.call-start = ((), (), s32[]{:S(2)}) async-start(), calls=%async_computation.34 | async-start | bytes 20971520 | tf_op jit(solution)/shard_map/reduce_scatter | solution.py:202
  1048.5 1.9 copy-start.37
  1048.5 573.1 %reduce-scatter.28.cloned.1.call-start = ((), (), s32[]{:S(2)}) async-start(), calls=%async_computation.32 | async-start | bytes 20971520 | tf_op jit(solution)/shard_map/reduce_scatter | solution.py:196
  1065.7 1.9 copy-start.38
  1065.7 684.6 %reduce-scatter.30.cloned.1.call-start = ((), (), s32[]{:S(2)}) async-start(), calls=%async_computation.33 | async-start | bytes 20971520 | tf_op jit(solution)/shard_map/reduce_scatter | solution.py:199
  1082.9 0.7 copy-start.36
  1082.9 1.2 copy-start.35
  1082.9 281.2 %copy-start.10 = (f32[128,2048]{1,0:T(8,128)S(1)}, f32[128,2048]{1,0:T(8,128)}, u32[]{:S(2)}) copy-start(f32[128,2048]{1,0:T(8,128)} %get-tuple-element.23) | copy-start | bytes 3145732
  1621.6 135.1 %copy-start.1 = (bf16[2048,32]{0,1:T(8,128)(2,1)S(1)}, bf16[2048,32]{0,1:T(8,128)(2,1)}, u32[]{:S(2)}) copy-start(bf16[2048,32]{0,1:T(8,128)(2,1)} %param.24) | copy-start | bytes 393220
Sparse Core Ops, SparseCore 0:
  9.6 23.8 all-gather.9
  35.6 48.3 all-gather.13
  86.1 47.7 all-gather.15
  135.9 47.7 all-gather.11
  185.6 50.4 all-gather.17
  240.4 29.7 reduce-scatter.11
  271.8 108.1 all-gather.21
  381.6 108.1 all-gather.19
  491.4 105.9 all-gather.23
  940.2 18.1 reduce-scatter.23
  960.5 22.5 all-gather.25
  986.4 61.2 reduce-scatter.25
  1051.2 66.9 reduce-scatter.21
  1121.5 66.7 reduce-scatter.19
  1192.2 66.8 reduce-scatter.15
  1263.1 66.8 reduce-scatter.17
  1332.9 31.1 reduce-scatter.13
  1366.7 126.1 reduce-scatter.31
  1495.4 126.1 reduce-scatter.27
  1624.2 126.0 reduce-scatter.29
where the time goes:
time: 1780 us; the launch traced here: 1760 us
  waiting for transfers between devices  1350 us (76%)
  matrix products  203 us (11%)
  local copies, waits for them, and re-layouts  75.9 us (4%)
  other arithmetic  65.8 us (4%)
  blocking collectives  28.7 us (2%)
  starting transfers between devices  25 us (1%)
    all_to_all x2, waiting for transfers between devices, send_rows(): lax.all_to_all(buffer, 'fsdp', split_axis=1, concat_axis=1, tiled=True)  179 us
    reduce_scatter x1, waiting for transfers between devices, per_device(): lax.psum_scatter(down_term.astype(jnp.bfloat16), 'tp', scatter_dimension=...  127 us
    reduce_scatter x1, waiting for transfers between devices, per_device(): lax.psum_scatter(up_term.astype(jnp.bfloat16), 'tp', scatter_dimension=2,...  122 us
    reduce_scatter x1, waiting for transfers between devices, per_device(): lax.psum_scatter(gate_term.astype(jnp.bfloat16), 'tp', scatter_dimension=...  122 us
    all_to_all x1, waiting for transfers between devices, per_device(): lax.all_to_all(expert_grad, 'fsdp', split_axis=1, concat_axis=1, tiled=True)  118 us
    all_to_all x1, waiting for transfers between devices, per_device(): lax.all_to_all(expert_out, 'fsdp', split_axis=1, concat_axis=1, tiled=True)  102 us
    reduce_scatter x1, waiting for transfers between devices, per_device(): lax.psum_scatter(w_query_part.astype(jnp.bfloat16), 'fsdp', scatter_dimen...  69.1 us
    reduce_scatter x1, waiting for transfers between devices, per_device(): lax.psum_scatter(w_key_part.astype(jnp.bfloat16), 'fsdp', scatter_dimensi...  69 us
  transfers between devices with their start and end apart: 24, of which 22 were waited for; matrix products, arithmetic and copies ran while one was open for 15% of the time, Pallas kernels for 0%

commit v1 on v0

--- a/solution.py
+++ b/solution.py
@@ -1,15 +1,912 @@
+import functools
 import math
 
 import jax
 import jax.numpy as jnp
 from jax import lax
+from jax.experimental import pallas as pl
+from jax.experimental.pallas import tpu as pltpu
 from jax.sharding import PartitionSpec as P
 
 HEAD = 128
-
-
+LANES = 128
 EPSILON = 1e-05
 HIGHEST = lax.Precision.HIGHEST
+MESH = pl.DeviceIdType.MESH
+ANY = pl.BlockSpec(memory_space=pl.ANY)
+VMEM = pl.BlockSpec(memory_space=pltpu.VMEM)
+MIB = 1 << 20
+HBM_BUDGET = 300 * MIB
+BF16 = jnp.bfloat16
+F32 = jnp.float32
+
+
+class Place:
+    def __init__(self, depth):
+        self.depth = depth
+        f, t = lax.axis_index("fsdp"), lax.axis_index("tp")
+        self.f, self.t = f, t
+        self.z, self.x = lax.div(f, 2), lax.rem(f, 2)
+        self.y, self.c = lax.div(t, 2), lax.rem(t, 2)
+        self.to = {
+            "x": (self.z * 2 + 1 - self.x, t),
+            "y": (f, (1 - self.y) * 2 + self.c),
+            "c": (f, self.y * 2 + 1 - self.c),
+            "up": (f + 2, t),
+            "down": (f - 2, t),
+        }
+        self.can_up = self.z < depth - 1
+        self.can_down = self.z > 0
+        offs = [0]
+        for step in range(1, depth):
+            offs += [-step, step]
+        self.offs = offs
+
+    def valid(self, off):
+        if off == 0:
+            return None
+        return self.z + off >= 0 if off < 0 else self.z + off < self.depth
+
+
+def when(cond, body):
+    if cond is None:
+        body()
+    else:
+        pl.when(cond)(body)
+
+
+def both(first, second):
+    if first is None:
+        return second
+    if second is None:
+        return first
+    return jnp.logical_and(first, second)
+
+
+class Net:
+    def __init__(self, place, send_sems, recv_sems, local_sems):
+        self.place = place
+        self.send_sems, self.recv_sems, self.local_sems = send_sems, recv_sems, local_sems
+        self.keys, self.sent, self.locals_used = {}, [], 0
+
+    def slot(self, key):
+        return self.keys.setdefault(key, len(self.keys))
+
+    def put(self, src, dst, to, key, cond=None, guard=None):
+        copy = pltpu.make_async_remote_copy(
+            src_ref=src,
+            dst_ref=dst,
+            send_sem=self.send_sems.at[len(self.sent)],
+            recv_sem=self.recv_sems.at[self.slot(key)],
+            device_id=self.place.to[to],
+            device_id_type=MESH,
+        )
+        self.sent.append((both(cond, guard), copy))
+        when(cond, copy.start)
+
+    def got(self, dst, key):
+        pltpu.make_async_remote_copy(
+            src_ref=dst,
+            dst_ref=dst,
+            send_sem=self.send_sems.at[0],
+            recv_sem=self.recv_sems.at[self.slot(key)],
+            device_id=self.place.to["c"],
+            device_id_type=MESH,
+        ).wait_recv()
+
+    def local(self, src, dst):
+        copy = pltpu.make_async_copy(src, dst, self.local_sems.at[self.locals_used])
+        self.locals_used += 1
+        copy.start()
+        return copy
+
+    def finish(self):
+        for cond, copy in self.sent:
+            when(cond, copy.wait_send)
+
+
+def greet(place, links):
+    barrier = pltpu.get_barrier_semaphore()
+    count = 0
+    for link in links:
+        if link == "z":
+            for name, cond in (("up", place.can_up), ("down", place.can_down)):
+                target = place.to[name]
+                pl.when(cond)(
+                    lambda target=target: pl.semaphore_signal(
+                        barrier, inc=1, device_id=target, device_id_type=MESH
+                    )
+                )
+                count = count + cond.astype(jnp.int32)
+        else:
+            pl.semaphore_signal(barrier, inc=1, device_id=place.to[link], device_id_type=MESH)
+            count = count + 1
+    pl.semaphore_wait(barrier, count)
+
+
+SENDS, RECVS, LOCALS = 160, 160, 24
+
+
+def sems():
+    return [
+        pltpu.SemaphoreType.DMA((SENDS,)),
+        pltpu.SemaphoreType.DMA((RECVS,)),
+        pltpu.SemaphoreType.DMA((LOCALS,)),
+    ]
+
+
+def add_rows(dst, src, rows, step=16):
+    def body(i, carry):
+        at = pl.ds(pl.multiple_of(i * step, step), step)
+        dst[at, :] = (dst[at, :].astype(F32) + src[at, :].astype(F32)).astype(dst.dtype)
+        return carry
+
+    lax.fori_loop(0, rows // step, body, 0)
+
+
+def comm_params(ident, mib=None):
+    limit = None if mib is None else mib * MIB
+    return pltpu.CompilerParams(collective_id=ident, has_side_effects=True, vmem_limit_bytes=limit)
+
+
+def spread_zx(net, name, block, own):
+    p = net.place
+    offs = p.offs
+
+    def step(i):
+        if i >= len(offs):
+            return
+        off = offs[i]
+        zz = p.z + off
+        valid = p.valid(off)
+        ref = block(zz, p.x)
+
+        def body():
+            if off:
+                net.got(ref, (name, "z", off))
+
+        when(valid, body)
+        src = ref if off else own
+        if off <= 0:
+            net.put(src, ref, "up", (name, "z", off - 1), both(valid, p.can_up))
+        if off >= 0:
+            net.put(src, ref, "down", (name, "z", off + 1), both(valid, p.can_down))
+        net.put(src, ref, "x", (name, "x", off), valid)
+
+    def finish():
+        for off in offs:
+            ref = block(p.z + off, 1 - p.x)
+            when(p.valid(off), lambda: net.got(ref, (name, "x", off)))
+
+    return step, finish
+
+
+def spread_xz(net, name, block, pair, own, placed):
+    p = net.place
+    offs = p.offs
+
+    def step(i):
+        if i >= len(offs):
+            return
+        off = offs[i]
+        if off == 0:
+            net.put(own, block(p.z, p.x), "x", (name, "x"))
+            placed.wait()
+            net.got(block(p.z, 1 - p.x), (name, "x"))
+        valid = p.valid(off)
+        ref = pair(p.z + off)
+        if off:
+            when(valid, lambda: net.got(ref, (name, "z", off)))
+        if off <= 0:
+            net.put(ref, ref, "up", (name, "z", off - 1), both(valid, p.can_up))
+        if off >= 0:
+            net.put(ref, ref, "down", (name, "z", off + 1), both(valid, p.can_down))
+
+    return step, lambda: None
+
+
+def spread_all(net, name, block, own, halves):
+    p = net.place
+    offs = p.offs
+    x, y, c = p.x, p.y, p.c
+
+    def step(i):
+        if i < len(offs):
+            off = offs[i]
+            zz, valid = p.z + off, p.valid(off)
+            ref = block(zz, x, y, c, None)
+            src = own if off == 0 else ref
+            if off:
+                when(valid, lambda: net.got(ref, (name, "z", off)))
+            if off <= 0:
+                net.put(src, ref, "up", (name, "z", off - 1), both(valid, p.can_up))
+            if off >= 0:
+                net.put(src, ref, "down", (name, "z", off + 1), both(valid, p.can_down))
+            if halves:
+                first, second = block(zz, x, y, c, 0), block(zz, x, y, c, 1)
+                src_a, src_b = (first, second) if off else halves
+                net.put(src_a, first, "x", (name, "x1", off), valid)
+                net.put(src_b, second, "y", (name, "y1", off), valid)
+                net.put(src_b, second, "x", (name, "x3", off), valid)
+                net.put(src_a, first, "y", (name, "y3", off), valid)
+            else:
+                net.put(src, ref, "x", (name, "x1", off), valid)
+                net.put(src, ref, "y", (name, "y1", off), valid)
+            net.put(src, ref, "c", (name, "c0", off), valid)
+        if 0 <= i - 1 < len(offs):
+            off = offs[i - 1]
+            zz, valid = p.z + off, p.valid(off)
+            part = 0 if halves else None
+            ref = block(zz, 1 - x, y, c, part)
+            when(valid, lambda: net.got(ref, (name, "x1", off)))
+            net.put(ref, ref, "y", (name, "y2", off), valid)
+            net.put(ref, ref, "c", (name, "c1", off), valid)
+            part = 1 if halves else None
+            ref = block(zz, x, 1 - y, c, part)
+            when(valid, lambda: net.got(ref, (name, "y1", off)))
+            if halves:
+                net.put(ref, ref, "x", (name, "x2", off), valid)
+            net.put(ref, ref, "c", (name, "c2", off), valid)
+        if 0 <= i - 2 < len(offs):
+            off = offs[i - 2]
+            zz, valid = p.z + off, p.valid(off)
+            part = 0 if halves else None
+            ref = block(zz, 1 - x, 1 - y, c, part)
+            when(valid, lambda: net.got(ref, (name, "y2", off)))
+            net.put(ref, ref, "c", (name, "c3", off), valid)
+            if halves:
+                for key, xx, yy, part in (("x2", 1 - x, 1 - y, 1), ("x3", 1 - x, y, 1), ("y3", x, 1 - y, 0)):
+                    ref = block(zz, xx, yy, c, part)
+                    when(valid, lambda ref=ref, key=key: net.got(ref, (name, key, off)))
+                    net.put(ref, ref, "c", (name, "c" + key, off), valid)
+
+    def finish():
+        for off in offs:
+            zz, valid = p.z + off, p.valid(off)
+
+            def body():
+                net.got(block(zz, x, y, 1 - c, None), (name, "c0", off))
+                part = 0 if halves else None
+                net.got(block(zz, 1 - x, y, 1 - c, part), (name, "c1", off))
+                net.got(block(zz, 1 - x, 1 - y, 1 - c, part), (name, "c3", off))
+                part = 1 if halves else None
+                net.got(block(zz, x, 1 - y, 1 - c, part), (name, "c2", off))
+                if halves:
+                    net.got(block(zz, 1 - x, 1 - y, 1 - c, 1), (name, "cx2", off))
+                    net.got(block(zz, 1 - x, y, 1 - c, 1), (name, "cx3", off))
+                    net.got(block(zz, x, 1 - y, 1 - c, 0), (name, "cy3", off))
+
+            when(valid, body)
+
+    return step, finish
+
+
+def run_flows(place, flows, extra=2):
+    for i in range(len(place.offs) + extra):
+        for step, _ in flows:
+            step(i)
+    for _, finish in flows:
+        finish()
+
+
+def first_kernel(
+    depth, wq, wk, wv, wo, inp, og, qkv, full_o, rows, grads, qkv_own, send, recv, local
+):
+    p = Place(depth)
+    net = Net(p, send, recv, local)
+    w_rows, w_cols = wq.shape
+    o_cols = wo.shape[1]
+
+    def column(f):
+        return full_o.at[:, pl.ds(pl.multiple_of(f * o_cols, LANES), o_cols)]
+
+    def columns(z):
+        return full_o.at[:, pl.ds(pl.multiple_of(z * (2 * o_cols), LANES), 2 * o_cols)]
+
+    def token_block(z, x, y, c, part):
+        return grads.at[((z * 2 + x) * 2 + y) * 2 + c]
+
+    for i, w in enumerate((wq, wk, wv)):
+        qkv_own[:, pl.ds(i * w_cols, w_cols)] = w[...]
+    greet(p, ("x", "y", "c", "z"))
+    mine = rows.at[p.t]
+    copies = [
+        net.local(wo, column(p.f)),
+        net.local(qkv_own, qkv.at[p.f]),
+        net.local(og, token_block(p.z, p.x, p.y, p.c, None)),
+        net.local(inp, mine),
+    ]
+    net.put(inp, mine, "y", ("rows", "y"))
+    net.put(inp, mine, "c", ("rows", "c0"))
+    flows = [
+        spread_xz(net, "o", lambda z, x: column(z * 2 + x), columns, wo, copies[0]),
+        spread_zx(net, "qkv", lambda z, x: qkv.at[z * 2 + x], qkv_own),
+        spread_all(net, "og", token_block, og, None),
+    ]
+    for i in range(len(p.offs) + 2):
+        for step, _ in flows:
+            step(i)
+        if i == 1:
+            other = rows.at[(1 - p.y) * 2 + p.c]
+            net.got(other, ("rows", "y"))
+            net.put(other, other, "c", ("rows", "c1"))
+    for _, finish in flows:
+        finish()
+    net.got(rows.at[p.y * 2 + 1 - p.c], ("rows", "c0"))
+    net.got(rows.at[(1 - p.y) * 2 + 1 - p.c], ("rows", "c1"))
+    for copy in copies[1:]:
+        copy.wait()
+    net.finish()
+
+
+def first_gather(depth, w_query, w_key, w_value, w_output, inputs, out_grad, tp):
+    fsdp = 2 * depth
+    w_rows, w_cols = w_query.shape
+    o_rows, o_cols = w_output.shape
+    rows, width = inputs.shape
+    return pl.pallas_call(
+        functools.partial(first_kernel, depth),
+        out_shape=[
+            jax.ShapeDtypeStruct((fsdp, w_rows, 3 * w_cols), BF16),
+            jax.ShapeDtypeStruct((o_rows, fsdp * o_cols), BF16),
+            jax.ShapeDtypeStruct((tp, rows, width), BF16),
+            jax.ShapeDtypeStruct((fsdp * tp, rows, width), BF16),
+        ],
+        in_specs=[VMEM] * 6,
+        out_specs=[ANY] * 4,
+        scratch_shapes=[pltpu.VMEM((w_rows, 3 * w_cols), BF16)] + sems(),
+        compiler_params=comm_params(1, 16),
+        name="first_gather",
+    )(w_query, w_key, w_value, w_output, inputs, out_grad)
+
+
+def mix_kernel(
+    depth, part, inp, gain, router, mask, rank, resid, gates_out, act_all,
+    acc, rc, ry, own, send, recv, local,
+):
+    p = Place(depth)
+    net = Net(p, send, recv, local)
+    rows, width = inp.shape
+    half = rows // 2
+    copy = net.local(part.at[:, p.c], acc)
+    greet(p, ("x", "y", "c", "z"))
+    net.put(part.at[:, 1 - p.c], rc, "c", ("rc",))
+    copy.wait()
+    net.got(rc, ("rc",))
+    far = 1 - p.y
+    add_rows(acc.at[far], rc.at[far], rows)
+    net.put(acc.at[far], ry, "y", ("ry",))
+    add_rows(acc.at[p.y], rc.at[p.y], rows)
+    net.got(ry, ("ry",))
+
+    def norm(i, carry):
+        at = pl.ds(pl.multiple_of(i * 16, 16), 16)
+        branch = acc[p.y, at, :].astype(F32) + ry[at, :].astype(F32)
+        values = inp[at, :].astype(F32) + branch
+        resid[at, :] = values
+        inverse = lax.rsqrt(jnp.mean(values * values, axis=-1, keepdims=True) + EPSILON)
+        own[at, pl.ds(0, width)] = (values * inverse * gain[...]).astype(BF16)
+        return carry
+
+    lax.fori_loop(0, rows // 16, norm, 0)
+    logits = jnp.dot(own[:, pl.ds(0, width)], router[...], preferred_element_type=F32)
+    chosen = mask[...] > 0.0
+    peak = jnp.max(jnp.where(chosen, logits, -1e30), axis=1, keepdims=True)
+    expo = jnp.where(chosen, jnp.exp(jnp.minimum(logits - peak, 0.0)), 0.0)
+    experts = router.shape[1] // 4
+    lane = lax.broadcasted_iota(jnp.int32, expo.shape, 1)
+    total = jnp.sum(jnp.where(lane < experts, expo, 0.0), axis=1, keepdims=True)
+    gates = expo / total
+    gates_out[...] = gates
+    high = gates.astype(BF16).astype(F32)
+    tail = jnp.where(lane < experts, high, jnp.where(lane < 2 * experts, gates - high, rank[...]))
+    own[:, pl.ds(width, LANES)] = tail.astype(BF16)
+
+    def block(z, x, y, c, part_of):
+        ref = act_all.at[((z * 2 + x) * 2 + y) * 2 + c]
+        return ref if part_of is None else ref.at[pl.ds(part_of * half, half)]
+
+    keep = net.local(own, block(p.z, p.x, p.y, p.c, None))
+    halves = (own.at[pl.ds(0, half)], own.at[pl.ds(half, half)])
+    run_flows(p, [spread_all(net, "act", block, own, halves)])
+    keep.wait()
+    net.finish()
+
+
+def mix_gather(depth, part, inputs, gain, router, mask, rank):
+    tp, rows, width = part.shape
+    wide = width + LANES
+    return pl.pallas_call(
+        functools.partial(mix_kernel, depth),
+        out_shape=[
+            jax.ShapeDtypeStruct((rows, width), F32),
+            jax.ShapeDtypeStruct((rows, LANES), F32),
+            jax.ShapeDtypeStruct((2 * depth * tp, rows, wide), BF16),
+        ],
+        in_specs=[ANY, VMEM, VMEM, VMEM, VMEM, VMEM],
+        out_specs=[VMEM, VMEM, ANY],
+        scratch_shapes=[
+            pltpu.VMEM((2, rows, width), BF16),
+            pltpu.VMEM((2, rows, width), BF16),
+            pltpu.VMEM((rows, width), BF16),
+            pltpu.VMEM((rows, wide), BF16),
+        ]
+        + sems(),
+        compiler_params=comm_params(2, 24),
+        name="mix_gather",
+    )(part.reshape(tp // 2, 2, rows, width), inputs, gain[None, :], router, mask, rank)
+
+
+def expert_kernel(
+    capacity, experts, blocks, act, grad, w_gate, w_up, w_down,
+    out, back, x_out, g_out, hid_out, gate_out, up_out, tails, o_keep, r_keep,
+):
+    local_experts, width, hidden = w_gate.shape
+    rows = act.shape[1]
+    slots = local_experts * capacity
+    first = lax.axis_index("fsdp") * local_experts
+    tp_lane = lax.axis_index("tp") * experts + first
+    pick_row = lax.broadcasted_iota(jnp.int32, (8, LANES), 0)
+    pick_lane = lax.broadcasted_iota(jnp.int32, (8, LANES), 1)
+    pick = (
+        (pick_lane == 2 * experts + first + pick_row) & (pick_row < local_experts)
+    ).astype(BF16)
+    places = lax.broadcasted_iota(jnp.int32, (capacity, rows), 0).astype(F32)
+
+    def one_hot(b):
+        tail = act[b, :, pl.ds(width, LANES)]
+        ranks = lax.dot_general(
+            pick, tail, (((1,), (1,)), ((), ())), preferred_element_type=F32
+        )
+        return jnp.concatenate(
+            [
+                (jnp.broadcast_to(ranks[e : e + 1, :], (capacity, rows)) == places).astype(BF16)
+                for e in range(local_experts)
+            ],
+            axis=0,
+        )
+
+    def gather(b, carry):
+        hot = one_hot(b)
+        picked = jnp.dot(hot, act[b], preferred_element_type=F32)
+        pulled = jnp.dot(hot, grad[b], preferred_element_type=F32).astype(BF16)
+        at = pl.ds(pl.multiple_of(b * capacity, capacity), capacity)
+        for e in range(local_experts):
+            part = picked[e * capacity : (e + 1) * capacity]
+            x_out[e, at, :] = part[:, :width].astype(BF16)
+            tails[e, at, :] = part[:, width:]
+            g_out[e, at, :] = pulled[e * capacity : (e + 1) * capacity]
+        return carry
+
+    lax.fori_loop(0, blocks, gather, 0)
+    last = (((1,), (1,)), ((), ()))
+    for e in range(local_experts):
+        lane = lax.broadcasted_iota(jnp.int32, tails.shape[1:], 1)
+        mine = (lane == first + e) | (lane == experts + first + e)
+        gates = jnp.sum(jnp.where(mine, tails[e], 0.0), axis=1, keepdims=True)
+        x_rows, g_rows = x_out[e], g_out[e]
+        pre = jnp.dot(x_rows, w_gate[e], preferred_element_type=F32)
+        up = jnp.dot(x_rows, w_up[e], preferred_element_type=F32)
+        raw = lax.dot_general(g_rows, w_down[e], last, preferred_element_type=F32)
+        sig = jax.nn.sigmoid(pre)
+        silu = pre * sig
+        hid = silu * up
+        gate_grad = jnp.sum(hid * raw, axis=1, keepdims=True)
+        scaled = raw * gates
+        hid_low = (hid * gates).astype(BF16)
+        gate_low = (scaled * up * sig * (1.0 + pre * (1.0 - sig))).astype(BF16)
+        up_low = (scaled * silu).astype(BF16)
+        hid_out[e] = hid_low
+        gate_out[e] = gate_low
+        up_out[e] = up_low
+        o_rows = jnp.dot(hid_low, w_down[e], preferred_element_type=F32).astype(BF16)
+        r_rows = (
+            lax.dot_general(gate_low, w_gate[e], last, preferred_element_type=F32)
+            + lax.dot_general(up_low, w_up[e], last, preferred_element_type=F32)
+        ).astype(BF16)
+        r_tail = jnp.where(lane == tp_lane + e, gate_grad, 0.0).astype(BF16)
+        for b in range(blocks):
+            at = slice(b * capacity, (b + 1) * capacity)
+            o_keep[b, e * capacity : (e + 1) * capacity, :] = o_rows[at]
+            r_keep[b, e * capacity : (e + 1) * capacity, pl.ds(0, width)] = r_rows[at]
+            r_keep[b, e * capacity : (e + 1) * capacity, pl.ds(width, LANES)] = r_tail[at]
+
+    def combine(b, carry):
+        hot = one_hot(b)
+        firsts = (((0,), (0,)), ((), ()))
+        out[b] = lax.dot_general(hot, o_keep[b], firsts, preferred_element_type=F32).astype(BF16)
+        back[b] = lax.dot_general(hot, r_keep[b], firsts, preferred_element_type=F32).astype(BF16)
+        return carry
+
+    lax.fori_loop(0, blocks, combine, 0)
+
+
+def run_experts(act_all, grad_all, w_gate, w_up, w_down, capacity, experts, blocks):
+    count, rows, wide = act_all.shape
+    width = wide - LANES
+    local_experts, _, hidden = w_gate.shape
+    steps = count // blocks
+    slots = blocks * capacity
+
+    def whole(array):
+        return pl.BlockSpec(array.shape, lambda i: (0, 0, 0), pipeline_mode=pl.Buffered(1))
+
+    def token_spec(columns):
+        return pl.BlockSpec((blocks, rows, columns), lambda i: (i, 0, 0))
+
+    def slot_spec(columns):
+        return pl.BlockSpec((local_experts, slots, columns), lambda i: (0, i, 0))
+
+    total = count * capacity
+    shape = jax.ShapeDtypeStruct
+    return pl.pallas_call(
+        functools.partial(expert_kernel, capacity, experts, blocks),
+        grid=(steps,),
+        out_shape=[
+            shape((count, rows, width), BF16),
+            shape((count, rows, wide), BF16),
+            shape((local_experts, total, width), BF16),
+            shape((local_experts, total, width), BF16),
+            shape((local_experts, total, hidden), BF16),
+            shape((local_experts, total, hidden), BF16),
+            shape((local_experts, total, hidden), BF16),
+        ],
+        in_specs=[token_spec(wide), token_spec(width), whole(w_gate), whole(w_up), whole(w_down)],
+        out_specs=[
+            token_spec(width),
+            token_spec(wide),
+            slot_spec(width),
+            slot_spec(width),
+            slot_spec(hidden),
+            slot_spec(hidden),
+            slot_spec(hidden),
+        ],
+        scratch_shapes=[
+            pltpu.VMEM((local_experts, slots, LANES), F32),
+            pltpu.VMEM((blocks, local_experts * capacity, width), BF16),
+            pltpu.VMEM((blocks, local_experts * capacity, wide), BF16),
+        ],
+        compiler_params=pltpu.CompilerParams(vmem_limit_bytes=60 * MIB),
+        name="experts",
+    )(act_all, grad_all, w_gate, w_up, w_down)
+
+
+def chain_z(net, name, off, acc, up, down, rows):
+    p = net.place
+    zz, valid = p.z + off, p.valid(off)
+
+    def take(buffer, key):
+        net.got(buffer.at[zz], key)
+        add_rows(acc(zz), buffer.at[zz], rows)
+
+    if off >= 0:
+        when(both(valid, p.can_down), lambda: take(up, (name, "up", off)))
+    if off <= 0:
+        when(both(valid, p.can_up), lambda: take(down, (name, "down", off)))
+    if off > 0:
+        net.put(acc(zz), up.at[zz], "up", (name, "up", off - 1), valid)
+    if off < 0:
+        net.put(acc(zz), down.at[zz], "down", (name, "down", off + 1), valid)
+
+
+def back_kernel(depth, part, total, acc, rc, ya, xa, xb, yb, up, down, send, recv, local):
+    p = Place(depth)
+    net = Net(p, send, recv, local)
+    x, y, c = p.x, p.y, p.c
+    rows, width = total.shape
+    half = rows // 2
+    a, b = pl.ds(0, half), pl.ds(half, half)
+    offs = p.offs[::-1]
+    copies = {}
+    for off in offs:
+        zz, valid = p.z + off, p.valid(off)
+        copy = pltpu.make_async_copy(part.at[zz, :, :, c], acc.at[zz], net.local_sems.at[len(copies)])
+        when(valid, copy.start)
+        copies[off] = copy
+    greet(p, ("x", "y", "c", "z"))
+    for off in offs:
+        zz = p.z + off
+        net.put(part.at[zz, :, :, 1 - c], rc.at[zz], "c", ("c", off), p.valid(off))
+
+    def step(i):
+        if i < len(offs):
+            off = offs[i]
+            zz, valid = p.z + off, p.valid(off)
+
+            def body():
+                copies[off].wait()
+                net.got(rc.at[zz], ("c", off))
+                for xx in range(2):
+                    for yy in range(2):
+                        add_rows(acc.at[zz, xx, yy], rc.at[zz, xx, yy], rows)
+
+            when(valid, body)
+            net.put(acc.at[zz, :, 1 - y, a], ya.at[zz], "y", ("ya", off), valid)
+            net.put(acc.at[zz, 1 - x, :, b], xb.at[zz], "x", ("xb", off), valid)
+        if 0 <= i - 1 < len(offs):
+            off = offs[i - 1]
+            zz, valid = p.z + off, p.valid(off)
+
+            def body():
+                net.got(ya.at[zz], ("ya", off))
+                for xx in range(2):
+                    add_rows(acc.at[zz, xx, y, a], ya.at[zz, xx], half)
+
+            when(valid, body)
+            net.put(acc.at[zz, 1 - x, y, a], xa.at[zz], "x", ("xa", off), valid)
+
+            def body():
+                net.got(xb.at[zz], ("xb", off))
+                for yy in range(2):
+                    add_rows(acc.at[zz, x, yy, b], xb.at[zz, yy], half)
+
+            when(valid, body)
+            net.put(acc.at[zz, x, 1 - y, b], yb.at[zz], "y", ("yb", off), valid)
+        if 0 <= i - 2 < len(offs):
+            off = offs[i - 2]
+            zz, valid = p.z + off, p.valid(off)
+
+            def body():
+                net.got(xa.at[zz], ("xa", off))
+                add_rows(acc.at[zz, x, y, a], xa.at[zz], half)
+                net.got(yb.at[zz], ("yb", off))
+                add_rows(acc.at[zz, x, y, b], yb.at[zz], half)
+
+            when(valid, body)
+            chain_z(net, "z", off, lambda zz: acc.at[zz, x, y], up, down, rows)
+
+    for i in range(len(offs) + 2):
+        step(i)
+
+    def last(i, carry):
+        at = pl.ds(pl.multiple_of(i * 16, 16), 16)
+        total[at, :] = acc[p.z, x, y, at, :].astype(F32)
+        return carry
+
+    lax.fori_loop(0, rows // 16, last, 0)
+    net.finish()
+
+
+def reduce_back(depth, part):
+    count, rows, wide = part.shape
+    half = rows // 2
+    return pl.pallas_call(
+        functools.partial(back_kernel, depth),
+        out_shape=jax.ShapeDtypeStruct((rows, wide), F32),
+        in_specs=[ANY],
+        out_specs=VMEM,
+        scratch_shapes=[
+            pltpu.VMEM((depth, 2, 2, rows, wide), BF16),
+            pltpu.VMEM((depth, 2, 2, rows, wide), BF16),
+            pltpu.VMEM((depth, 2, half, wide), BF16),
+            pltpu.VMEM((depth, half, wide), BF16),
+            pltpu.VMEM((depth, 2, half, wide), BF16),
+            pltpu.VMEM((depth, half, wide), BF16),
+            pltpu.VMEM((depth, rows, wide), BF16),
+            pltpu.VMEM((depth, rows, wide), BF16),
+        ]
+        + sems(),
+        compiler_params=comm_params(3, 48),
+        name="reduce_back",
+    )(part.reshape(depth, 2, 2, 2, rows, wide))
+
+
+def rows_kernel(depth, mine, whole, send, recv, local):
+    p = Place(depth)
+    net = Net(p, send, recv, local)
+    keep = net.local(mine, whole.at[p.t])
+    greet(p, ("y", "c"))
+    net.put(mine, whole.at[p.t], "y", ("y",))
+    net.put(mine, whole.at[p.t], "c", ("c0",))
+    other = whole.at[(1 - p.y) * 2 + p.c]
+    net.got(other, ("y",))
+    net.put(other, other, "c", ("c1",))
+    net.got(whole.at[p.y * 2 + 1 - p.c], ("c0",))
+    net.got(whole.at[(1 - p.y) * 2 + 1 - p.c], ("c1",))
+    keep.wait()
+    net.finish()
+
+
+def gather_rows(depth, mine, tp):
+    rows, width = mine.shape
+    return pl.pallas_call(
+        functools.partial(rows_kernel, depth),
+        out_shape=jax.ShapeDtypeStruct((tp, rows, width), mine.dtype),
+        in_specs=[ANY],
+        out_specs=ANY,
+        scratch_shapes=sems(),
+        compiler_params=comm_params(4),
+        name="gather_rows",
+    )(mine)
+
+
+def last_kernel(
+    depth, out_part, tail, qkv_part, o_part, row_part,
+    out_sum, q_sum, k_sum, v_sum, o_sum, row_sum,
+    acc, rc, ry, rx, up, down, q_acc, q_rx, q_up, q_down, o_acc, o_up, o_down, o_rx,
+    t_acc, t_rc, t_ry, send, recv, local,
+):
+    p = Place(depth)
+    net = Net(p, send, recv, local)
+    x, y, c = p.x, p.y, p.c
+    rows, width = row_sum.shape
+    w_rows, w_cols = q_sum.shape
+    o_cols = o_sum.shape[1]
+    offs = p.offs[::-1]
+    main, side = pl.ds(0, width), pl.ds(width, LANES)
+    copies, waits = {}, []
+    used = 0
+
+    def load(off, src, dst):
+        nonlocal used
+        copy = pltpu.make_async_copy(src, dst, net.local_sems.at[used])
+        used += 1
+        when(p.valid(off), copy.start)
+        copies.setdefault(off, []).append(copy)
+
+    def pair(ref, z):
+        return ref.at[:, pl.ds(pl.multiple_of(z * (2 * o_cols), LANES), 2 * o_cols)]
+
+    o_load = pltpu.make_async_copy(o_part, o_acc, net.local_sems.at[LOCALS - 1])
+    o_load.start()
+    t_load = pltpu.make_async_copy(row_part.at[:, c], t_acc, net.local_sems.at[LOCALS - 2])
+    t_load.start()
+    for off in offs:
+        zz = p.z + off
+        load(off, out_part.at[zz, :, :, c], acc.at[zz, :, :, :, main])
+        load(off, tail.at[zz, :, :, c], acc.at[zz, :, :, :, side])
+        load(off, qkv_part.at[zz, x], q_acc.at[zz])
+    greet(p, ("x", "y", "c", "z"))
+    net.put(row_part.at[:, 1 - c], t_rc, "c", ("tc",))
+    for off in offs:
+        zz, valid = p.z + off, p.valid(off)
+        net.put(qkv_part.at[zz, 1 - x], q_rx.at[zz], "x", ("qx", off), valid)
+        net.put(out_part.at[zz, :, :, 1 - c], rc.at[zz, :, :, :, main], "c", ("c", off), valid)
+        net.put(tail.at[zz, :, :, 1 - c], rc.at[zz, :, :, :, side], "c", ("ct", off), valid)
+    o_load.wait()
+    t_load.wait()
+    net.got(t_rc, ("tc",))
+    add_rows(t_acc.at[1 - y], t_rc.at[1 - y], rows)
+    net.put(t_acc.at[1 - y], t_ry, "y", ("ty",))
+
+    def step(i):
+        if i < len(offs):
+            off = offs[i]
+            zz, valid = p.z + off, p.valid(off)
+
+            def take(buffer, key):
+                net.got(buffer.at[zz], key)
+                add_rows(pair(o_acc, zz), buffer.at[zz], o_acc.shape[0])
+
+            if off >= 0:
+                when(both(valid, p.can_down), lambda: take(o_up, ("oup", off)))
+            if off <= 0:
+                when(both(valid, p.can_up), lambda: take(o_down, ("odown", off)))
+            if off > 0:
+                net.put(pair(o_acc, zz), o_up.at[zz], "up", ("oup", off - 1), valid)
+            if off < 0:
+                net.put(pair(o_acc, zz), o_down.at[zz], "down", ("odown", off + 1), valid)
+
+            def body():
+                for copy in copies[off]:
+                    copy.wait()
+                net.got(rc.at[zz, :, :, :, main], ("c", off))
+                net.got(rc.at[zz, :, :, :, side], ("ct", off))
+                for xx in range(2):
+                    for yy in range(2):
+                        add_rows(acc.at[zz, xx, yy], rc.at[zz, xx, yy], rows)
+
+            when(valid, body)
+            net.put(acc.at[zz, :, 1 - y], ry.at[zz], "y", ("y", off), valid)
+
+            def body():
+                net.got(q_rx.at[zz], ("qx", off))
+                add_rows(q_acc.at[zz], q_rx.at[zz], w_rows)
+
+            when(valid, body)
+            chain_z(net, "q", off, lambda zz: q_acc.at[zz], q_up, q_down, w_rows)
+        if 0 <= i - 1 < len(offs):
+            off = offs[i - 1]
+            zz, valid = p.z + off, p.valid(off)
+
+            def body():
+                net.got(ry.at[zz], ("y", off))
+                for xx in range(2):
+                    add_rows(acc.at[zz, xx, y], ry.at[zz, xx], rows)
+
+            when(valid, body)
+            net.put(acc.at[zz, 1 - x, y], rx.at[zz], "x", ("x", off), valid)
+        if 0 <= i - 2 < len(offs):
+            off = offs[i - 2]
+            zz, valid = p.z + off, p.valid(off)
+
+            def body():
+                net.got(rx.at[zz], ("x", off))
+                add_rows(acc.at[zz, x, y], rx.at[zz], rows)
+
+            when(valid, body)
+            chain_z(net, "z", off, lambda zz: acc.at[zz, x, y], up, down, rows)
+        if i == len(offs) - 1:
+            net.put(
+                o_acc.at[:, pl.ds(pl.multiple_of((p.z * 2 + 1 - x) * o_cols, LANES), o_cols)],
+                o_rx, "x", ("ox",),
+            )
+
+    for i in range(len(offs) + 2):
+        step(i)
+    at_o = pl.ds(pl.multiple_of((p.z * 2 + x) * o_cols, LANES), o_cols)
+    net.got(o_rx, ("ox",))
+
+    def o_last(i, carry):
+        at = pl.ds(pl.multiple_of(i * 16, 16), 16)
+        o_sum[at, :] = o_acc[at, at_o].astype(F32) + o_rx[at, :].astype(F32)
+        return carry
+
+    lax.fori_loop(0, o_sum.shape[0] // 16, o_last, 0)
+
+    def q_last(i, carry):
+        at = pl.ds(pl.multiple_of(i * 16, 16), 16)
+        for j, ref in enumerate((q_sum, k_sum, v_sum)):
+            ref[at, :] = q_acc[p.z, at, pl.ds(j * w_cols, w_cols)].astype(F32)
+        return carry
+
+    lax.fori_loop(0, w_rows // 16, q_last, 0)
+    net.got(t_ry, ("ty",))
+
+    def rows_last(i, carry):
+        at = pl.ds(pl.multiple_of(i * 16, 16), 16)
+        out_sum[at, :] = acc[p.z, x, y, at, :].astype(F32)
+        row_sum[at, :] = (
+            t_acc[y, at, :].astype(F32) + t_rc[y, at, :].astype(F32) + t_ry[at, :].astype(F32)
+        )
+        return carry
+
+    lax.fori_loop(0, rows // 16, rows_last, 0)
+    net.finish()
+
+
+def last_reduce(depth, out_part, tail, qkv_part, o_part, row_part, w_rows, o_cols):
+    count, rows, width = out_part.shape
+    wide = width + LANES
+    w_cols = qkv_part.shape[1] // 3
+    o_rows = o_part.shape[0]
+    shape = jax.ShapeDtypeStruct
+    return pl.pallas_call(
+        functools.partial(last_kernel, depth),
+        out_shape=[shape((rows, wide), F32)]
+        + [shape((w_rows, w_cols), F32)] * 3
+        + [shape((o_rows, o_cols), F32), shape((rows, width), F32)],
+        in_specs=[ANY] * 5,
+        out_specs=[VMEM] * 6,
+        scratch_shapes=[
+            pltpu.VMEM((depth, 2, 2, rows, wide), BF16),
+            pltpu.VMEM((depth, 2, 2, rows, wide), BF16),
+            pltpu.VMEM((depth, 2, rows, wide), BF16),
+            pltpu.VMEM((depth, rows, wide), BF16),
+            pltpu.VMEM((depth, rows, wide), BF16),
+            pltpu.VMEM((depth, rows, wide), BF16),
+            pltpu.VMEM((depth, w_rows, 3 * w_cols), BF16),
+            pltpu.VMEM((depth, w_rows, 3 * w_cols), BF16),
+            pltpu.VMEM((depth, w_rows, 3 * w_cols), BF16),
+            pltpu.VMEM((depth, w_rows, 3 * w_cols), BF16),
+            pltpu.VMEM((o_rows, depth * 2 * o_cols), BF16),
+            pltpu.VMEM((depth, o_rows, 2 * o_cols), BF16),
+            pltpu.VMEM((depth, o_rows, 2 * o_cols), BF16),
+            pltpu.VMEM((o_rows, o_cols), BF16),
+            pltpu.VMEM((2, rows, width), BF16),
+            pltpu.VMEM((2, rows, width), BF16),
+            pltpu.VMEM((rows, width), BF16),
+        ]
+        + sems(),
+        compiler_params=comm_params(5, 62),
+        name="last_reduce",
+    )(
+        out_part.reshape(depth, 2, 2, 2, rows, width),
+        tail.reshape(depth, 2, 2, 2, rows, LANES),
+        qkv_part.reshape(depth, 2, w_rows, 3 * w_cols),
+        o_part,
+        row_part.reshape(2, 2, rows, width),
+    )
 
 
 def norm_rows(values, gain):
@@ -36,6 +933,136 @@
 def contract_first(left, right):
     return lax.dot_general(
         left, right, (((0,), (0,)), ((), ())), preferred_element_type=jnp.float32
+    )
+
+
+def dense_layer(
+    inputs, out_grad, segments, routes, attn_gain, w_query, w_key, w_value, w_output,
+    moe_gain, router, w_gate, w_up, w_down,
+):
+    tp, fsdp = lax.axis_size("tp"), lax.axis_size("fsdp")
+    depth = fsdp // 2
+    rows, width = inputs.shape
+    local_experts = w_gate.shape[0]
+    experts = local_experts * fsdp
+    top_k = routes.shape[1]
+    capacity = 3 * rows * top_k // (2 * experts)
+    w_rows, w_cols = w_query.shape
+    heads = w_cols // HEAD
+    seq = tp * rows
+
+    named = jnp.any(
+        routes[:, :, None] == jnp.arange(experts, dtype=jnp.int32)[None, None, :], axis=1
+    )
+    hits = named.astype(F32)
+    before = (jnp.arange(rows)[:, None] > jnp.arange(rows)[None, :]).astype(F32)
+    ranks = jnp.where(named, jnp.dot(before, hits, preferred_element_type=F32), -1.0)
+    fill = jnp.zeros((rows, LANES - 3 * experts), F32)
+    blank = jnp.zeros((rows, experts), F32)
+    mask = jnp.concatenate([hits, hits, blank, fill], axis=1)
+    rank = jnp.concatenate([blank, blank, ranks, fill], axis=1)
+    router_pad = jnp.concatenate(
+        [router, router, jnp.zeros((width, LANES - 2 * experts), BF16)], axis=1
+    )
+
+    qkv_full, full_output, whole, grad_all = first_gather(
+        depth, w_query, w_key, w_value, w_output, inputs, out_grad, tp
+    )
+    whole_float = whole.reshape(seq, width).astype(F32)
+    normed_one, inverse_one = norm_rows(whole_float, attn_gain)
+    act_one = normed_one.astype(BF16)
+    qkv_full = qkv_full.reshape(width, 3 * w_cols)
+    qkv = jnp.dot(act_one, qkv_full, preferred_element_type=F32).astype(BF16)
+    query, key_rows, value_rows = [
+        qkv[:, i * w_cols : (i + 1) * w_cols].reshape(seq, heads, HEAD) for i in range(3)
+    ]
+    score_scale = 1.0 / math.sqrt(HEAD)
+    scores = jnp.einsum("qhd,khd->hqk", query, key_rows, preferred_element_type=F32) * score_scale
+    scores = jnp.where((segments[:, None] == segments[None, :])[None], scores, -1e30)
+    probs = jax.nn.softmax(scores, axis=-1)
+    attended = (
+        jnp.einsum("hqk,khd->qhd", probs.astype(BF16), value_rows, preferred_element_type=F32)
+        .reshape(seq, -1)
+        .astype(BF16)
+    )
+    partial = jnp.dot(attended, full_output, preferred_element_type=F32).astype(BF16)
+    resid, gates_wide, act_all = mix_gather(
+        depth, partial.reshape(tp, rows, width), inputs, moe_gain, router_pad, mask, rank
+    )
+    out_part, back_part, x_rows, g_rows, hid_low, gate_low, up_low = run_experts(
+        act_all, grad_all, w_gate, w_up, w_down, capacity, experts, min(4, fsdp * tp)
+    )
+    back = reduce_back(depth, back_part)
+
+    def slots(left, right):
+        return jnp.einsum("esd,esf->edf", left, right, preferred_element_type=F32)
+
+    w_gate_grad = slots(x_rows, gate_low)
+    w_up_grad = slots(x_rows, up_low)
+    w_down_grad = slots(hid_low, g_rows)
+
+    gates = gates_wide[:, :experts]
+    act_two = (
+        resid
+        * (inverse_two := lax.rsqrt(jnp.mean(resid * resid, axis=-1, keepdims=True) + EPSILON))
+        * moe_gain
+    ).astype(BF16)
+    gate_grad = jnp.sum(back[:, width : width + tp * experts].reshape(rows, tp, experts), axis=1)
+    logit_grad = gates * (gate_grad - jnp.sum(gates * gate_grad, axis=1, keepdims=True))
+    act_two_grad = back[:, :width] + lax.dot_general(
+        logit_grad, router.astype(F32), (((1,), (1,)), ((), ())), precision=HIGHEST
+    )
+    router_part = lax.dot_general(
+        act_two.astype(F32), logit_grad, (((0,), (0,)), ((), ())), precision=HIGHEST
+    )
+    resid_part, gain_two_part = norm_back(resid, inverse_two, moe_gain, act_two_grad)
+    resid_grad = out_grad.astype(F32) + resid_part
+    branch_grad = gather_rows(depth, resid_grad.astype(BF16), tp).reshape(seq, width)
+
+    attended_grad = (
+        contract_last(branch_grad, full_output).astype(BF16).reshape(seq, heads, HEAD)
+    )
+    o_part = contract_first(attended, branch_grad).astype(BF16)
+    prob_grad = jnp.einsum("qhd,khd->hqk", attended_grad, value_rows, preferred_element_type=F32)
+    inner = jnp.sum(probs * prob_grad, axis=-1, keepdims=True)
+    score_grad = (probs * (prob_grad - inner) * score_scale).astype(BF16)
+    query_grad = jnp.einsum("hqk,khd->qhd", score_grad, key_rows, preferred_element_type=F32)
+    key_grad = jnp.einsum("hqk,qhd->khd", score_grad, query, preferred_element_type=F32)
+    value_grad = jnp.einsum(
+        "hqk,qhd->khd", probs.astype(BF16), attended_grad, preferred_element_type=F32
+    )
+    low = jnp.concatenate(
+        [g.reshape(seq, -1).astype(BF16) for g in (query_grad, key_grad, value_grad)], axis=1
+    )
+    qkv_part = contract_first(act_one, low).astype(BF16)
+    act_one_grad = contract_last(low, qkv_full)
+    whole_part, gain_one_part = norm_back(whole_float, inverse_one, attn_gain, act_one_grad)
+
+    count = fsdp * tp
+    small = jnp.concatenate([router_part, gain_one_part[:, None], gain_two_part[:, None]], axis=1)
+    small = small.astype(BF16).reshape(count, width // count, experts + 2)
+    tail = jnp.pad(
+        small, ((0, 0), (0, rows - width // count), (0, LANES - experts - 2))
+    )
+    out_sum, q_sum, k_sum, v_sum, o_sum, row_sum = last_reduce(
+        depth, out_part, tail, qkv_part, o_part, whole_part.astype(BF16), w_rows, w_output.shape[1]
+    )
+    output = (resid + out_sum[:, :width]).astype(BF16)
+    input_grad = resid_grad + row_sum
+    side = out_sum[: width // count, width:]
+    return (
+        output,
+        input_grad,
+        side[:, experts],
+        q_sum,
+        k_sum,
+        v_sum,
+        o_sum,
+        side[:, experts + 1],
+        side[:, :experts],
+        w_gate_grad,
+        w_up_grad,
+        w_down_grad,
     )
 
 
@@ -332,9 +1359,20 @@
     )
 
 
+def layer(*args):
+    tokens = args[0].shape[0] * lax.axis_size("fsdp") * lax.axis_size("tp")
+    held = 6 * tokens * (args[0].shape[1] + LANES) * 2
+    even = lax.axis_size("tp") == 4 and lax.axis_size("fsdp") % 2 == 0
+    experts = args[11].shape[0] * lax.axis_size("fsdp")
+    narrow = lax.axis_size("tp") * experts <= LANES and args[1].shape[1] // (lax.axis_size("tp") * lax.axis_size("fsdp")) <= args[0].shape[0]
+    if held <= HBM_BUDGET and even and narrow:
+        return dense_layer(*args)
+    return per_device(*args)
+
+
 def solution(mesh):
     return jax.shard_map(
-        per_device,
+        layer,
         mesh=mesh,
         in_specs=(
             P(("fsdp", "tp"), None),

time: 1780 us -> 807 us (0.45)
  waiting for transfers between devices: 1350 us -> 0 us
  Pallas kernels: 0 us -> 645 us
  matrix products: 203 us -> 105 us
  other arithmetic: 65.8 us -> 14 us
  local copies, waits for them, and re-layouts: 75.9 us -> 27.8 us
  blocking collectives: 28.7 us -> 0 us
  starting transfers between devices: 25 us -> 0 us
    pallas_call x0 -> x6, Pallas kernels: none -> 645 us  [the longest x1 162 us: first_gather(): pl.pallas_call(functools.partial(first_kernel, depth), out_shape=[jax.Sha...]
    reduce_scatter x11 -> x0, waiting for transfers between devices: 638 us -> none  [the longest x1 127 us: per_device(): lax.psum_scatter(down_term.astype(jnp.bfloat16), 'tp', scatter_dimension=...]
    all_to_all x4 -> x0, waiting for transfers between devices: 399 us -> none  [the longest x2 179 us: send_rows(): lax.all_to_all(buffer, 'fsdp', split_axis=1, concat_axis=1, tiled=True)]
    all_gather x9 -> x0, waiting for transfers between devices: 307 us -> none  [the longest x1 47.9 us: per_device(): lax.all_gather(w_query, 'fsdp', axis=0, tiled=True)]
    dot_general x24 -> x13, matrix products: 180 us -> 81.8 us  [the longest x3 50.2 us: slots(): return jnp.einsum('esd,esf->edf', left, right, preferred_element_type=F32)]
    gather x4 -> x0, local copies, waits for them, and re-layouts: 47.3 us -> none  [the longest x1 15.5 us: per_device(): padded_grad[sources].reshape(1, fsdp_count, local_experts * capacity, width)]
    unnamed x2 -> x0, blocking collectives: 28.7 us -> none
    convert_element_type x13 -> x5, other arithmetic: 34.1 us -> 7.11 us  [the longest x1 2.81 us: dense_layer(): whole_part.astype(BF16)]
  transfers between devices with their start and end apart: 24 -> 0, of which waited for: 22 -> 0; matrix products, arithmetic and copies ran while one was open for 15% -> 0% of each run, Pallas kernels for 0% -> 0%
where the time goes in v1:
time: 807 us; the launch traced here: 793 us
  Pallas kernels  645 us (80%)
  matrix products  105 us (13%)
  local copies, waits for them, and re-layouts  27.8 us (3%)
  other arithmetic  14 us (2%)
    pallas_call x1, Pallas kernels, first_gather(): pl.pallas_call(functools.partial(first_kernel, depth), out_shape=[jax.Sha...  162 us
    pallas_call x1, Pallas kernels, last_reduce(): pl.pallas_call(functools.partial(last_kernel, depth), out_shape=[shape((r...  158 us
    pallas_call x1, Pallas kernels, run_experts(): pl.pallas_call(functools.partial(expert_kernel, capacity, experts, blocks...  109 us
    pallas_call x1, Pallas kernels, mix_gather(): pl.pallas_call(functools.partial(mix_kernel, depth), out_shape=[jax.Shape...  103 us
    pallas_call x1, Pallas kernels, reduce_back(): pl.pallas_call(functools.partial(back_kernel, depth), out_shape=jax.Shape...  93.3 us
    dot_general x3, matrix products, slots(): return jnp.einsum('esd,esf->edf', left, right, preferred_element_type=F32)  50.2 us
    unnamed x82, local copies, waits for them, and re-layouts  22 us
    pallas_call x1, Pallas kernels, gather_rows(): pl.pallas_call(functools.partial(rows_kernel, depth), out_shape=jax.Shape...  20.1 us

profile of v1, /device:TPU:2, one launch (start us, length us, event | category | flops | bytes accessed | tf_op | source)
XLA Modules:
  0.0 792.9 jit_solution(14959715252146810249)
XLA Ops:
  0.7 1.0 copy-done.5
  1.7 1.0 copy-done.7
  2.7 0.9 copy-done.9
  3.7 0.9 copy-done.10
  4.6 0.9 copy-done.11
  5.6 0.9 copy-done.12
  6.5 161.7 %first_gather.1 = (bf16[8,256,1536]{2,1,0:T(8,128)(2,1)S(1)}, bf16[512,2048]{1,0:T(8,128)(2,1)S(1)}, bf16[4,128,2048]{2,1,0:T(8,128)(2,1)S(1)}, bf16[32,128,2048]{2,1,0:T(8,128)(2,1)S(1)}) custom-call(bf16[256,512]{1,0:T(8,128)(2,1)S(1)} %copy-done.9, bf16[256,512]{1,0:T(8,128)(2,1)S(1)} %copy-done.10, bf16[256,512]{1,0:T(8,128)(2,1)S(1)} %copy-done.11, ...), custom_call_target="tpu_custom_call" | custom-call | tf_op jit(solution)/shard_map/first_gather/pallas_call | solution.py:347
  168.3 1.3 copy-done.15
  169.6 0.5 fusion.2
  170.1 0.9 fusion.64
  171.0 0.5 fusion.4
  171.6 3.4 convolution_convert_fusion.3
  175.0 1.0 copy-done.3
  176.0 1.9 copy-done.14
  177.9 0.2 fusion.66
  178.1 0.2 copy.157
  178.3 0.2 copy.158
  178.6 0.2 broadcast_compare_fusion
  178.8 3.7 fusion.67
  182.5 2.9 convolution_convert_fusion.7
  185.4 2.6 convolution_convert_fusion.2
  188.1 0.1 copy.128
  188.2 0.1 convolution_select_fusion
  188.3 0.1 copy.126
  188.5 0.1 maximum_maximum_fusion.1
  188.6 0.3 copy.124
  189.0 0.3 maximum_maximum_fusion.router
  189.4 1.6 copy-done.4
  191.0 103.3 %mix_gather.1 = (f32[128,2048]{1,0:T(8,128)S(1)}, f32[128,128]{1,0:T(8,128)S(1)}, bf16[32,128,2176]{2,1,0:T(8,128)(2,1)S(1)}) custom-call(bf16[2,2,128,2048]{3,2,1,0:T(8,128)(2,1)S(1)} %bitcast.84, bf16[128,2048]{1,0:T(8,128)(2,1)S(1)} %copy-done.6, f32[1,2048]{1,0:T(1,128)S(1)} %bitcast.85, bf16[2048,128]{1,0:T(8,128)(2,1)S(1)} %maximum_maximum_fusion.router, ...), custom_call_target="tpu_custom_call" | custom-call | tf_op jit(solution)/shard_map/mix_gather/pallas_call | solution.py:419
  294.3 6.0 copy-done.2
  300.4 108.5 %experts.1 = (bf16[32,128,2048]{2,1,0:T(8,128)(2,1)}, bf16[32,128,2176]{2,1,0:T(8,128)(2,1)}, bf16[4,1536,2048]{2,1,0:T(8,128)(2,1)}, bf16[4,1536,2048]{2,1,0:T(...) custom-call(bf16[32,128,2176]{2,1,0:T(8,128)(2,1)} %copy-done.2, ...), custom_call_target="tpu_custom_call" | custom-call | tf_op jit(solution)/shard_map/experts/pallas_call | solution.py:542
  408.9 18.0 %fusion.70 = f32[4,256,2048]{2,1,0:T(8,128)} fusion(bf16[4,1536,256]{2,1,0:T(8,128)(2,1)} %get-tuple-element.50, bf16[4,1536,2048]{2,1,0:T(8,128)(2,1)} %get-tuple-element.51), kind=kOutput, calls=%fused_computation.106 | convolution fusion | flops 6442450944 | bytes 36700160 | tf_op jit(solution)/shard_map/esd,esf->edf/dot_general | solution.py:998
  426.8 16.1 %fusion.69 = f32[4,2048,256]{2,1,0:T(8,128)} fusion(bf16[4,1536,2048]{2,1,0:T(8,128)(2,1)} %get-tuple-element.47, bf16[4,1536,256]{2,1,0:T(8,128)(2,1)} %get-tuple-element.49), kind=kOutput, calls=%fused_computation.105 | convolution fusion | flops 6442450944 | bytes 36700160 | tf_op jit(solution)/shard_map/esd,esf->edf/dot_general | solution.py:998
  442.9 16.1 %fusion.68 = f32[4,2048,256]{2,1,0:T(8,128)} fusion(bf16[4,1536,2048]{2,1,0:T(8,128)(2,1)} %get-tuple-element.47, bf16[4,1536,256]{2,1,0:T(8,128)(2,1)} %get-tuple-element.48), kind=kOutput, calls=%fused_computation.104 | convolution fusion | flops 6442450944 | bytes 36700160 | tf_op jit(solution)/shard_map/esd,esf->edf/dot_general | solution.py:998
  459.0 93.3 %reduce_back.1 = f32[128,2176]{1,0:T(8,128)S(1)} custom-call(bf16[4,2,2,2,128,2176]{5,4,3,2,1,0:T(8,128)(2,1)} %bitcast.88), custom_call_target="tpu_custom_call" | custom-call | tf_op jit(solution)/shard_map/reduce_back/pallas_call | solution.py:673
  552.5 0.1 multiply_reduce_fusion.4
  552.7 0.2 multiply_reduce_fusion.3
  552.8 1.0 multiply_reduce_fusion.2
  553.8 1.5 fusion.65
  555.4 20.1 %gather_rows.1 = bf16[4,128,2048]{2,1,0:T(8,128)(2,1)} custom-call(bf16[128,2048]{1,0:T(8,128)(2,1)} %get-tuple-element.118.mine), custom_call_target="tpu_custom_call" | custom-call | tf_op jit(solution)/shard_map/gather_rows/pallas_call | solution.py:712
  575.5 4.4 convolution_convert_fusion.1.o_part
  579.8 1.3 convolution_convert_fusion.5
  581.2 2.7 fusion.47
  583.8 7.8 fusion.32
  591.6 7.6 fusion.35
  599.2 3.2 convolution_convert_fusion.6
  602.4 7.2 fusion.12
  609.7 2.8 fusion.11
  612.5 6.4 convolution_convert_fusion
  618.8 0.5 convolution_convert_fusion.4
  619.3 0.3 copy.156
  619.6 1.0 concatenate.31
  620.6 1.0 concatenate.32
  621.6 1.7 fusion.42
  623.3 158.1 %last_reduce.1 = (f32[128,2176]{1,0:T(8,128)}, f32[256,512]{1,0:T(8,128)}, f32[256,512]{1,0:T(8,128)}, f32[256,512]{1,0:T(8,128)}, f32[512,256]{1,0:T(8,128)}, /*index=5*/f32[128,2048]{1,0:T(8,128)}) custom-call(bf16[4,2,2,2,128,2048]{5,4,3,2,1,0:T(8,128)(2,1)} %bitcast.89, bf16[4,2,2,2,128,128]{5,4,3,2,1,0:T(8,128)(2,1)} %bitcast.92, ...), custom_call_target="tpu_custom_call" | custom-call | tf_op jit(solution)/shard_map/last_reduce/pallas_call | solution.py:874
  781.5 2.8 add.51
  784.3 2.2 add_convert_fusion
  786.5 0.8 slice.43
  787.3 0.7 copy.146
  788.0 1.6 slice_reduce_fusion
  789.5 0.8 copy.173
  790.3 0.8 copy.174
  791.1 0.8 copy.175
  791.9 0.8 copy.176
  (79 shorter events, 0.6 us)
Async XLA Ops:
  0.6 1.0 copy-start.5
  1.7 1.0 copy-start.7
  2.7 0.9 copy-start.9
  3.7 0.9 copy-start.10
  4.6 0.9 copy-start.11
  5.6 0.9 copy-start.12
  6.5 164.5 %copy-start.28 = (f32[2048]{0:T(1024)S(1)}, f32[2048]{0:T(1024)}, u32[]{:S(2)}) copy-start(f32[2048]{0:T(1024)} %param.18) | copy-start | bytes 24580
  168.3 1.3 copy-start.15
  169.6 5.4 copy-start
  169.6 6.4 copy-start.3
  169.6 8.3 %copy-start.14 = (bf16[8,256,1536]{2,1,0:T(8,128)(2,1)}, bf16[8,256,1536]{2,1,0:T(8,128)(2,1)S(1)}, u32[]{:S(2)}) copy-start(bf16[8,256,1536]{2,1,0:T(8,128)(2,1)S(1)} %get-tuple-element.33) | copy-start | bytes 18874372
  170.1 1.5 copy-start.29
  177.9 0.7 copy-start.31
  178.3 4.2 copy-start.19
  178.5 4.0 copy-start.21
  182.5 2.9 copy-start.36
  182.5 3.0 copy-start.16
  185.4 2.7 copy-start.34
  185.4 2.7 copy-start.33
  185.4 3.2 copy-start.27
  185.4 3.9 copy-start.6
  185.4 3.9 copy-start.13
  189.4 1.6 copy-start.4
  294.3 6.0 copy-start.2
  552.3 1.5 copy-start.8
  553.8 21.6 %copy-start.35 = (bf16[4,128,512]{2,1,0:T(8,128)(2,1)S(1)}, bf16[4,128,512]{2,1,0:T(8,128)(2,1)}, u32[]{:S(2)}) copy-start(bf16[4,128,512]{2,1,0:T(8,128)(2,1)} %copy-done.34) | copy-start | bytes 1572868
  575.5 4.4 copy-start.17
  575.5 4.4 copy-start.18
  581.1 2.7 copy-start.22
  581.1 2.7 copy-start.37
  583.8 7.8 copy-start.20
  599.2 3.2 copy-start.1
  599.2 3.2 copy-start.32
  602.4 7.2 copy-start.30
  781.5 8.1 %copy-start.26 = (f32[256,512]{1,0:T(8,128)S(1)}, f32[256,512]{1,0:T(8,128)}, u32[]{:S(2)}) copy-start(f32[256,512]{1,0:T(8,128)} %get-tuple-element.152) | copy-start | bytes 1572868
  781.5 8.8 %copy-start.25 = (f32[256,512]{1,0:T(8,128)S(1)}, f32[256,512]{1,0:T(8,128)}, u32[]{:S(2)}) copy-start(f32[256,512]{1,0:T(8,128)} %get-tuple-element.153) | copy-start | bytes 1572868
  781.5 9.6 %copy-start.24 = (f32[256,512]{1,0:T(8,128)S(1)}, f32[256,512]{1,0:T(8,128)}, u32[]{:S(2)}) copy-start(f32[256,512]{1,0:T(8,128)} %get-tuple-element.154) | copy-start | bytes 1572868
  781.5 10.4 %copy-start.23 = (f32[512,256]{1,0:T(8,128)S(1)}, f32[512,256]{1,0:T(8,128)}, u32[]{:S(2)}) copy-start(f32[512,256]{1,0:T(8,128)} %get-tuple-element.155) | copy-start | bytes 1572868

commit v2 on v0

--- a/solution.py
+++ b/solution.py
@@ -1,15 +1,1228 @@
+import functools
 import math
 
 import jax
 import jax.numpy as jnp
 from jax import lax
+from jax.experimental import pallas as pl
+from jax.experimental.pallas import tpu as pltpu
 from jax.sharding import PartitionSpec as P
 
 HEAD = 128
-
-
+LANES = 128
 EPSILON = 1e-05
 HIGHEST = lax.Precision.HIGHEST
+MESH = pl.DeviceIdType.MESH
+ANY = pl.BlockSpec(memory_space=pl.ANY)
+VMEM = pl.BlockSpec(memory_space=pltpu.VMEM)
+MIB = 1 << 20
+HBM_BUDGET = 300 * MIB
+BF16 = jnp.bfloat16
+F32 = jnp.float32
+CONTRACT_FIRST = (((0,), (0,)), ((), ()))
+CONTRACT_LAST = (((1,), (1,)), ((), ()))
+
+
+class Place:
+    def __init__(self, depth):
+        self.depth = depth
+        f, t = lax.axis_index("fsdp"), lax.axis_index("tp")
+        self.f, self.t = f, t
+        self.z, self.x = lax.div(f, 2), lax.rem(f, 2)
+        self.y, self.c = lax.div(t, 2), lax.rem(t, 2)
+        self.to = {
+            "x": (self.z * 2 + 1 - self.x, t),
+            "y": (f, (1 - self.y) * 2 + self.c),
+            "c": (f, self.y * 2 + 1 - self.c),
+            "up": (f + 2, t),
+            "down": (f - 2, t),
+        }
+        self.can_up = self.z < depth - 1
+        self.can_down = self.z > 0
+        offs = [0]
+        for step in range(1, depth):
+            offs += [-step, step]
+        self.offs = offs
+        tables = [sorted(range(depth), key=lambda zz: (abs(zz - z), zz)) for z in range(depth)]
+        self.near = [
+            sum(jnp.where(self.z == z, tables[z][i], 0) for z in range(depth)) for i in range(depth)
+        ]
+        self.far = self.near[::-1]
+        self.tables = tables
+
+    def nearest(self, i):
+        pairs = [(z, k) for z in range(self.depth) for k in range(self.depth)]
+        return sum(
+            jnp.where((self.z == z) & (i == k), self.tables[z][k], 0) for z, k in pairs
+        )
+
+    def valid(self, off):
+        if off == 0:
+            return None
+        return self.z + off >= 0 if off < 0 else self.z + off < self.depth
+
+
+def when(cond, body):
+    if cond is None:
+        body()
+    else:
+        pl.when(cond)(body)
+
+
+def both(first, second):
+    if first is None:
+        return second
+    if second is None:
+        return first
+    return jnp.logical_and(first, second)
+
+
+class Net:
+    def __init__(self, place, send_sems, recv_sems, local_sems):
+        self.place = place
+        self.send_sems, self.recv_sems, self.local_sems = send_sems, recv_sems, local_sems
+        self.keys, self.used, self.sent, self.locals_used = {}, 0, [], 0
+
+    def slot(self, key):
+        if len(key) == 4 and key[1] == "at":
+            base = self.keys.setdefault(key[0], self.used)
+            if base == self.used:
+                self.used += key[2]
+            return base + key[3]
+        base = self.keys.setdefault(key, self.used)
+        if base == self.used:
+            self.used += 1
+        return base
+
+    def put(self, src, dst, to, key, cond=None, guard=None):
+        copy = pltpu.make_async_remote_copy(
+            src_ref=src,
+            dst_ref=dst,
+            send_sem=self.send_sems.at[len(self.sent)],
+            recv_sem=self.recv_sems.at[self.slot(key)],
+            device_id=self.place.to[to],
+            device_id_type=MESH,
+        )
+        self.sent.append((both(cond, guard), copy))
+        when(cond, copy.start)
+
+    def got(self, dst, key):
+        pltpu.make_async_remote_copy(
+            src_ref=dst,
+            dst_ref=dst,
+            send_sem=self.send_sems.at[0],
+            recv_sem=self.recv_sems.at[self.slot(key)],
+            device_id=self.place.to["c"],
+            device_id_type=MESH,
+        ).wait_recv()
+
+    def local(self, src, dst):
+        copy = pltpu.make_async_copy(src, dst, self.local_sems.at[self.locals_used])
+        self.locals_used += 1
+        copy.start()
+        return copy
+
+    def finish(self):
+        for cond, copy in self.sent:
+            when(cond, copy.wait_send)
+
+
+def greet(place, links):
+    barrier = pltpu.get_barrier_semaphore()
+    count = 0
+    for link in links:
+        if link == "z":
+            for name, cond in (("up", place.can_up), ("down", place.can_down)):
+                target = place.to[name]
+                pl.when(cond)(
+                    lambda target=target: pl.semaphore_signal(
+                        barrier, inc=1, device_id=target, device_id_type=MESH
+                    )
+                )
+                count = count + cond.astype(jnp.int32)
+        else:
+            pl.semaphore_signal(barrier, inc=1, device_id=place.to[link], device_id_type=MESH)
+            count = count + 1
+    pl.semaphore_wait(barrier, count)
+
+
+SENDS, RECVS, LOCALS = 160, 160, 24
+
+
+def sems():
+    return [
+        pltpu.SemaphoreType.DMA((SENDS,)),
+        pltpu.SemaphoreType.DMA((RECVS,)),
+        pltpu.SemaphoreType.DMA((LOCALS,)),
+    ]
+
+
+def add_rows(dst, src, rows, step=16):
+    def body(i, carry):
+        at = pl.ds(pl.multiple_of(i * step, step), step)
+        dst[at, :] = (dst[at, :].astype(F32) + src[at, :].astype(F32)).astype(dst.dtype)
+        return carry
+
+    lax.fori_loop(0, rows // step, body, 0)
+
+
+def comm_params(ident, mib=None):
+    limit = None if mib is None else mib * MIB
+    return pltpu.CompilerParams(collective_id=ident, has_side_effects=True, vmem_limit_bytes=limit)
+
+
+def spread_zx(net, name, block, own):
+    p = net.place
+    offs = p.offs
+
+    def step(i):
+        if i >= len(offs):
+            return
+        off = offs[i]
+        zz = p.z + off
+        valid = p.valid(off)
+        ref = block(zz, p.x)
+
+        def body():
+            if off:
+                net.got(ref, (name, "z", off))
+
+        when(valid, body)
+        src = ref if off else own
+        if off <= 0:
+            net.put(src, ref, "up", (name, "z", off - 1), both(valid, p.can_up))
+        if off >= 0:
+            net.put(src, ref, "down", (name, "z", off + 1), both(valid, p.can_down))
+        net.put(src, ref, "x", (name, "x", off), valid)
+
+    def finish():
+        for off in offs:
+            ref = block(p.z + off, 1 - p.x)
+            when(p.valid(off), lambda: net.got(ref, (name, "x", off)))
+
+    return step, finish
+
+
+def spread_xz(net, name, block, pair, own, placed):
+    p = net.place
+    offs = p.offs
+
+    def step(i):
+        if i >= len(offs):
+            return
+        off = offs[i]
+        if off == 0:
+            net.put(own, block(p.z, p.x), "x", (name, "x"))
+            placed.wait()
+            net.got(block(p.z, 1 - p.x), (name, "x"))
+        valid = p.valid(off)
+        ref = pair(p.z + off)
+        if off:
+            when(valid, lambda: net.got(ref, (name, "z", off)))
+        if off <= 0:
+            net.put(ref, ref, "up", (name, "z", off - 1), both(valid, p.can_up))
+        if off >= 0:
+            net.put(ref, ref, "down", (name, "z", off + 1), both(valid, p.can_down))
+
+    return step, lambda: None
+
+
+def first_kernel(
+    depth, wq, wk, wv, wo, inp, qkv, full_o, rows, send, recv, local
+):
+    p = Place(depth)
+    net = Net(p, send, recv, local)
+    w_rows, w_cols = wq.shape
+    o_cols = wo.shape[1]
+
+    def column(f):
+        return full_o.at[:, pl.ds(pl.multiple_of(f * o_cols, LANES), o_cols)]
+
+    def columns(z):
+        return full_o.at[:, pl.ds(pl.multiple_of(z * (2 * o_cols), LANES), 2 * o_cols)]
+
+    greet(p, ("x", "y", "c", "z"))
+    mine = rows.at[p.t]
+    copies = [net.local(wo, column(p.f)), net.local(inp, mine)] + [
+        net.local(w, qkv.at[p.f, :, pl.ds(i * w_cols, w_cols)])
+        for i, w in enumerate((wq, wk, wv))
+    ]
+    net.put(inp, mine, "y", ("rows", "y"))
+    net.put(inp, mine, "c", ("rows", "c0"))
+    def slab(i):
+        at = pl.ds(i * w_cols, w_cols)
+        return lambda z, x: qkv.at[z * 2 + x, :, at]
+
+    flows = [
+        spread_zx(net, f"w{i}", slab(i), w) for i, w in enumerate((wq, wk, wv))
+    ] + [spread_xz(net, "o", lambda z, x: column(z * 2 + x), columns, wo, copies[0])]
+    for i in range(len(p.offs) + 2):
+        for step, _ in flows:
+            step(i)
+        if i == 1:
+            other = rows.at[(1 - p.y) * 2 + p.c]
+            net.got(other, ("rows", "y"))
+            net.put(other, other, "c", ("rows", "c1"))
+    for _, finish in flows:
+        finish()
+    net.got(rows.at[p.y * 2 + 1 - p.c], ("rows", "c0"))
+    net.got(rows.at[(1 - p.y) * 2 + 1 - p.c], ("rows", "c1"))
+    for copy in copies[1:]:
+        copy.wait()
+    net.finish()
+
+
+def first_gather(depth, w_query, w_key, w_value, w_output, inputs, tp):
+    fsdp = 2 * depth
+    w_rows, w_cols = w_query.shape
+    o_rows, o_cols = w_output.shape
+    rows, width = inputs.shape
+    return pl.pallas_call(
+        functools.partial(first_kernel, depth),
+        out_shape=[
+            jax.ShapeDtypeStruct((fsdp, w_rows, 3 * w_cols), BF16),
+            jax.ShapeDtypeStruct((o_rows, fsdp * o_cols), BF16),
+            jax.ShapeDtypeStruct((tp, rows, width), BF16),
+        ],
+        in_specs=[VMEM] * 5,
+        out_specs=[ANY] * 3,
+        scratch_shapes=sems(),
+        compiler_params=comm_params(1, 60),
+        name="first_gather",
+    )(w_query, w_key, w_value, w_output, inputs)
+
+
+SITES = {
+    "x1": ("x", 0, 0, 0),
+    "y1": ("y", 0, 0, 1),
+    "x3": ("x", 0, 0, 1),
+    "y3": ("y", 0, 0, 0),
+    "y2": ("y", 1, 0, 0),
+    "x2": ("x", 0, 1, 1),
+    "c0": ("c", 0, 0, None),
+    "cx": ("c", 1, 0, None),
+    "cy": ("c", 0, 1, None),
+    "cxy": ("c", 1, 1, None),
+}
+NAMES = list(SITES)
+
+
+class Plane:
+    def __init__(self, place, everyone, own, sends, recvs):
+        self.place, self.everyone, self.own = place, everyone, own
+        self.sends, self.recvs = sends, recvs
+        self.half = own.shape[0] // 2
+
+    def ref(self, zz, dx, dy, dc, part):
+        p = self.place
+        x, y, c = p.x + dx - 2 * p.x * dx, p.y + dy - 2 * p.y * dy, p.c + dc - 2 * p.c * dc
+        ref = self.everyone.at[((zz * 2 + x) * 2 + y) * 2 + c]
+        return ref if part is None else ref.at[pl.ds(part * self.half, self.half)]
+
+    def copy(self, site, zz, src=None):
+        link, dx, dy, part = SITES[site]
+        dst = self.ref(zz, dx, dy, 0, part)
+        at = NAMES.index(site) * self.place.depth + zz
+        return pltpu.make_async_remote_copy(
+            src_ref=dst if src is None else src,
+            dst_ref=dst,
+            send_sem=self.sends.at[at],
+            recv_sem=self.recvs.at[at],
+            device_id=self.place.to[link],
+            device_id_type=MESH,
+        )
+
+    def take(self, site, zz):
+        link, dx, dy, part = SITES[site]
+        dx, dy = dx ^ (link == "x"), dy ^ (link == "y")
+        ref = self.ref(zz, dx, dy, int(link == "c"), part)
+        at = NAMES.index(site) * self.place.depth + zz
+        pltpu.make_async_remote_copy(
+            src_ref=ref,
+            dst_ref=ref,
+            send_sem=self.sends.at[at],
+            recv_sem=self.recvs.at[at],
+            device_id=self.place.to[link],
+            device_id_type=MESH,
+        ).wait_recv()
+
+    def z_copy(self, zz):
+        p = self.place
+        base = len(NAMES) * p.depth
+        return pltpu.make_async_remote_copy(
+            src_ref=self.own,
+            dst_ref=self.ref(p.z, 0, 0, 0, None),
+            send_sem=self.sends.at[base + zz],
+            recv_sem=self.recvs.at[base + p.z],
+            device_id=(zz * 2 + p.x, p.t),
+            device_id_type=MESH,
+        )
+
+    def send_z(self):
+        for zz in self.place.near[1:]:
+            self.z_copy(zz).start()
+
+    def first(self, zz, mine=False):
+        p = self.place
+        whole, part_a, part_b = None, None, None
+        if mine:
+            whole = self.own
+            part_a, part_b = whole.at[pl.ds(0, self.half)], whole.at[pl.ds(self.half, self.half)]
+        else:
+            ref = self.ref(zz, 0, 0, 0, None)
+            at = len(NAMES) * p.depth + zz
+            pltpu.make_async_remote_copy(
+                src_ref=ref,
+                dst_ref=ref,
+                send_sem=self.sends.at[at],
+                recv_sem=self.recvs.at[at],
+                device_id=(zz * 2 + p.x, p.t),
+                device_id_type=MESH,
+            ).wait_recv()
+        self.copy("x1", zz, part_a).start()
+        self.copy("y1", zz, part_b).start()
+        self.copy("x3", zz, part_b).start()
+        self.copy("y3", zz, part_a).start()
+        self.copy("c0", zz, whole).start()
+
+    def second(self, zz):
+        self.take("x1", zz)
+        self.copy("y2", zz).start()
+        self.take("y1", zz)
+        self.copy("x2", zz).start()
+
+    def third(self, zz):
+        self.take("x3", zz)
+        self.copy("cx", zz).start()
+        self.take("y3", zz)
+        self.copy("cy", zz).start()
+        self.take("x2", zz)
+        self.take("y2", zz)
+        self.copy("cxy", zz).start()
+
+    def arrived(self, zz):
+        for site in ("c0", "cx", "cy", "cxy"):
+            self.take(site, zz)
+
+    def finish(self):
+        for zz in range(self.place.depth):
+            for site in NAMES:
+                self.copy(site, zz).wait_send()
+            pl.when(self.place.z != zz)(self.z_copy(zz).wait_send)
+
+
+def plane_sems(depth):
+    return [pltpu.SemaphoreType.DMA(((len(NAMES) + 1) * depth,))] * 2
+
+
+def moe_kernel(
+    depth, capacity, experts, blocks,
+    part, inp, og, gain, router, mask, rank, gate_hbm, up_hbm, down_hbm,
+    resid, gates_out, act_all, grad_all, out_hbm, back_hbm, x_hbm, g_hbm, hid_hbm, gl_hbm, ul_hbm,
+    acc, rc, ry, own, w_gate, w_up, w_down, act_in, grad_in, x_rows, g_rows, tails, hid, gl, ul,
+    o_keep, r_keep, out, back,
+    act_send, act_recv, og_send, og_recv, send, recv, local, load_sems, save_sems,
+):
+    p = Place(depth)
+    net = Net(p, send, recv, local)
+    rows, width = inp.shape
+    local_experts = w_gate.shape[0]
+    weights = [
+        net.local(src, dst)
+        for src, dst in ((gate_hbm, w_gate), (up_hbm, w_up), (down_hbm, w_down))
+    ]
+    part_in = net.local(part.at[:, p.c], acc)
+    acts = Plane(p, act_all, own, act_send, act_recv)
+    grads = Plane(p, grad_all, og, og_send, og_recv)
+    barrier = pltpu.get_barrier_semaphore()
+    peers = [p.to["x"], p.to["y"], p.to["c"]] + [(zz * 2 + p.x, p.t) for zz in p.near[1:]]
+    for peer in peers:
+        pl.semaphore_signal(barrier, inc=1, device_id=peer, device_id_type=MESH)
+    pl.semaphore_wait(barrier, len(peers))
+
+    net.put(part.at[:, 1 - p.c], rc, "c", ("rc",))
+    og_kept = net.local(og, grads.ref(p.z, 0, 0, 0, None))
+    grads.send_z()
+    part_in.wait()
+    net.got(rc, ("rc",))
+    far = 1 - p.y
+    add_rows(acc.at[far], rc.at[far], rows)
+    net.put(acc.at[far], ry, "y", ("ry",))
+    grads.first(p.z, True)
+    add_rows(acc.at[p.y], rc.at[p.y], rows)
+    net.got(ry, ("ry",))
+
+    def norm(i, carry):
+        at = pl.ds(pl.multiple_of(i * 16, 16), 16)
+        branch = acc[p.y, at, :].astype(F32) + ry[at, :].astype(F32)
+        values = inp[at, :].astype(F32) + branch
+        resid[at, :] = values
+        inverse = lax.rsqrt(jnp.mean(values * values, axis=-1, keepdims=True) + EPSILON)
+        own[at, pl.ds(0, width)] = (values * inverse * gain[...]).astype(BF16)
+        return carry
+
+    lax.fori_loop(0, rows // 16, norm, 0)
+    logits = jnp.dot(own[:, pl.ds(0, width)], router[...], preferred_element_type=F32)
+    chosen = mask[...] > 0.0
+    peak = jnp.max(jnp.where(chosen, logits, -1e30), axis=1, keepdims=True)
+    expo = jnp.where(chosen, jnp.exp(jnp.minimum(logits - peak, 0.0)), 0.0)
+    lane = lax.broadcasted_iota(jnp.int32, expo.shape, 1)
+    total = jnp.sum(jnp.where(lane < experts, expo, 0.0), axis=1, keepdims=True)
+    gates = expo / total
+    gates_out[...] = gates
+    high = gates.astype(BF16).astype(F32)
+    tail = jnp.where(lane < experts, high, jnp.where(lane < 2 * experts, gates - high, rank[...]))
+    own[:, pl.ds(width, LANES)] = tail.astype(BF16)
+    acts.send_z()
+    acts.first(p.z, True)
+    act_kept = net.local(own, acts.ref(p.z, 0, 0, 0, None))
+    grads.second(p.z)
+    acts.second(p.z)
+    grads.first(p.near[1])
+    grads.third(p.z)
+    acts.third(p.z)
+    acts.first(p.near[1])
+    grads.arrived(p.z)
+    acts.arrived(p.z)
+    og_kept.wait()
+    act_kept.wait()
+    for copy in weights:
+        copy.wait()
+
+    first_expert = p.f * local_experts
+    tp_lane = p.t * experts + first_expert
+    pick_row = lax.broadcasted_iota(jnp.int32, (8, LANES), 0)
+    pick_lane = lax.broadcasted_iota(jnp.int32, (8, LANES), 1)
+    pick = (
+        (pick_lane == 2 * experts + first_expert + pick_row) & (pick_row < local_experts)
+    ).astype(BF16)
+    places = lax.broadcasted_iota(jnp.int32, (capacity, rows), 0).astype(F32)
+    slots = blocks * capacity
+
+    def loads(zz, j):
+        at = pl.ds((zz * 2 + j) * blocks, blocks)
+        return [
+            pltpu.make_async_copy(act_all.at[at], act_in.at[j], load_sems.at[j, 0]),
+            pltpu.make_async_copy(grad_all.at[at], grad_in.at[j], load_sems.at[j, 1]),
+        ]
+
+    def save(zz, j, k):
+        if k < 5:
+            where = pl.ds(pl.multiple_of((zz * 2 + j) * slots, 16), slots)
+            src = (x_rows, g_rows, hid, gl, ul)[k]
+            dst = (x_hbm, g_hbm, hid_hbm, gl_hbm, ul_hbm)[k].at[:, where]
+        else:
+            src = (out, back)[k - 5]
+            dst = (out_hbm, back_hbm)[k - 5].at[pl.ds((zz * 2 + j) * blocks, blocks)]
+        return pltpu.make_async_copy(src, dst, save_sems.at[k])
+
+    def one_hot(j, b):
+        tail = act_in[j, b, :, pl.ds(width, LANES)]
+        ranks = lax.dot_general(pick, tail, CONTRACT_LAST, preferred_element_type=F32)
+        return jnp.concatenate(
+            [
+                (jnp.broadcast_to(ranks[e : e + 1, :], (capacity, rows)) == places).astype(BF16)
+                for e in range(local_experts)
+            ],
+            axis=0,
+        )
+
+    def work(zz, j, started, serve):
+        for copy in loads(zz, j):
+            copy.wait()
+
+        def settle(ks):
+            def body():
+                for k in ks:
+                    save(zz, j, k).wait()
+
+            when(started, body)
+
+        settle((0, 1))
+
+        def gather(b, carry):
+            hot = one_hot(j, b)
+            picked = jnp.dot(hot, act_in[j, b], preferred_element_type=F32)
+            pulled = jnp.dot(hot, grad_in[j, b], preferred_element_type=F32).astype(BF16)
+            at = pl.ds(pl.multiple_of(b * capacity, 16), capacity)
+            for e in range(local_experts):
+                piece = picked[e * capacity : (e + 1) * capacity]
+                x_rows[e, at, :] = piece[:, :width].astype(BF16)
+                tails[e, at, :] = piece[:, width:]
+                g_rows[e, at, :] = pulled[e * capacity : (e + 1) * capacity]
+            return carry
+
+        lax.fori_loop(0, blocks, gather, 0)
+        for k in (0, 1):
+            save(zz, j, k).start()
+        serve(0)
+        settle((2, 3, 4))
+        for e in range(local_experts):
+            tail_lane = lax.broadcasted_iota(jnp.int32, (slots, LANES), 1)
+            mine = (tail_lane == first_expert + e) | (tail_lane == experts + first_expert + e)
+            gates_of = jnp.sum(jnp.where(mine, tails[e], 0.0), axis=1, keepdims=True)
+            pre = jnp.dot(x_rows[e], w_gate[e], preferred_element_type=F32)
+            up = jnp.dot(x_rows[e], w_up[e], preferred_element_type=F32)
+            raw = lax.dot_general(g_rows[e], w_down[e], CONTRACT_LAST, preferred_element_type=F32)
+            sig = jax.nn.sigmoid(pre)
+            silu = pre * sig
+            hidden = silu * up
+            gate_grad = jnp.sum(hidden * raw, axis=1, keepdims=True)
+            scaled = raw * gates_of
+            hid_low = (hidden * gates_of).astype(BF16)
+            gate_low = (scaled * up * sig * (1.0 + pre * (1.0 - sig))).astype(BF16)
+            up_low = (scaled * silu).astype(BF16)
+            hid[e] = hid_low
+            gl[e] = gate_low
+            ul[e] = up_low
+            o_rows = jnp.dot(hid_low, w_down[e], preferred_element_type=F32).astype(BF16)
+            r_rows = (
+                lax.dot_general(gate_low, w_gate[e], CONTRACT_LAST, preferred_element_type=F32)
+                + lax.dot_general(up_low, w_up[e], CONTRACT_LAST, preferred_element_type=F32)
+            ).astype(BF16)
+            r_tail = jnp.where(tail_lane == tp_lane + e, gate_grad, 0.0).astype(BF16)
+            for b in range(blocks):
+                at = slice(b * capacity, (b + 1) * capacity)
+                to = slice(e * capacity, (e + 1) * capacity)
+                o_keep[b, to, :] = o_rows[at]
+                r_keep[b, to, pl.ds(0, width)] = r_rows[at]
+                r_keep[b, to, pl.ds(width, LANES)] = r_tail[at]
+            serve(1 + e)
+        for k in (2, 3, 4):
+            save(zz, j, k).start()
+        settle((5, 6))
+
+        def combine(b, carry):
+            hot = one_hot(j, b)
+            out[b] = lax.dot_general(
+                hot, o_keep[b], CONTRACT_FIRST, preferred_element_type=F32
+            ).astype(BF16)
+            back[b] = lax.dot_general(
+                hot, r_keep[b], CONTRACT_FIRST, preferred_element_type=F32
+            ).astype(BF16)
+            return carry
+
+        lax.fori_loop(0, blocks, combine, 0)
+        for k in (5, 6):
+            save(zz, j, k).start()
+
+    for copy in loads(p.z, 0):
+        copy.start()
+
+    def group(g, carry):
+        zz, later, last = p.nearest(g), p.nearest(g + 1), p.nearest(g + 2)
+        more, still = g + 1 < depth, g + 2 < depth
+        for copy in loads(zz, 1):
+            copy.start()
+
+        def serve_one(k):
+            if k == 0:
+                pl.when(more)(lambda: grads.second(later))
+            if k == 1:
+                pl.when(more)(lambda: acts.second(later))
+            if k == 2:
+                pl.when(still)(lambda: grads.first(last))
+            if k == 4:
+                pl.when(more)(lambda: grads.third(later))
+
+        work(zz, 0, g > 0, serve_one)
+
+        def serve_two(k):
+            if k == 0:
+                pl.when(more)(lambda: acts.third(later))
+            if k == 1:
+                pl.when(still)(lambda: acts.first(last))
+            if k == 4:
+
+                def ready():
+                    grads.arrived(later)
+                    acts.arrived(later)
+                    for copy in loads(later, 0):
+                        copy.start()
+
+                pl.when(more)(ready)
+
+        work(zz, 1, None, serve_two)
+        return carry
+
+    lax.fori_loop(0, depth, group, 0)
+    for k in range(7):
+        save(0, 1, k).wait()
+    acts.finish()
+    grads.finish()
+    net.finish()
+
+
+def run_moe(
+    depth, capacity, experts, part, inputs, out_grad, gain, router, mask, rank, w_gate, w_up, w_down
+):
+    tp, rows, width = part.shape
+    wide = width + LANES
+    count = 2 * depth * tp
+    local_experts, _, hidden = w_gate.shape
+    blocks = tp
+    slots = blocks * capacity
+    total = count * capacity
+    shape = jax.ShapeDtypeStruct
+    kept = [shape((local_experts, total, width), BF16)] * 2
+    kept += [shape((local_experts, total, hidden), BF16)] * 3
+    return pl.pallas_call(
+        functools.partial(moe_kernel, depth, capacity, experts, blocks),
+        out_shape=[
+            shape((rows, width), F32),
+            shape((rows, LANES), F32),
+            shape((count, rows, wide), BF16),
+            shape((count, rows, width), BF16),
+            shape((count, rows, width), BF16),
+            shape((count, rows, wide), BF16),
+        ]
+        + kept,
+        in_specs=[ANY] + [VMEM] * 6 + [ANY] * 3,
+        out_specs=[VMEM] * 2 + [ANY] * 9,
+        scratch_shapes=[
+            pltpu.VMEM((2, rows, width), BF16),
+            pltpu.VMEM((2, rows, width), BF16),
+            pltpu.VMEM((rows, width), BF16),
+            pltpu.VMEM((rows, wide), BF16),
+            pltpu.VMEM(w_gate.shape, BF16),
+            pltpu.VMEM(w_up.shape, BF16),
+            pltpu.VMEM(w_down.shape, BF16),
+            pltpu.VMEM((2, blocks, rows, wide), BF16),
+            pltpu.VMEM((2, blocks, rows, width), BF16),
+            pltpu.VMEM((local_experts, slots, width), BF16),
+            pltpu.VMEM((local_experts, slots, width), BF16),
+            pltpu.VMEM((local_experts, slots, LANES), F32),
+            pltpu.VMEM((local_experts, slots, hidden), BF16),
+            pltpu.VMEM((local_experts, slots, hidden), BF16),
+            pltpu.VMEM((local_experts, slots, hidden), BF16),
+            pltpu.VMEM((blocks, local_experts * capacity, width), BF16),
+            pltpu.VMEM((blocks, local_experts * capacity, wide), BF16),
+            pltpu.VMEM((blocks, rows, width), BF16),
+            pltpu.VMEM((blocks, rows, wide), BF16),
+        ]
+        + plane_sems(depth) * 2
+        + sems()
+        + [pltpu.SemaphoreType.DMA((2, 2)), pltpu.SemaphoreType.DMA((7,))],
+        compiler_params=comm_params(2, 60),
+        name="moe",
+    )(
+        part.reshape(tp // 2, 2, rows, width), inputs, out_grad, gain[None, :], router, mask, rank,
+        w_gate, w_up, w_down,
+    )
+
+
+def chain_z(net, name, zz, acc, inbox, rows):
+    p = net.place
+    extra = p.depth
+
+    def take(slot):
+        net.got(inbox.at[slot], (name, "at", extra + 1, slot))
+        add_rows(acc, inbox.at[slot], rows)
+
+    pl.when((zz >= p.z) & p.can_down)(lambda: take(jnp.where(zz == p.z, extra, zz)))
+    pl.when((zz <= p.z) & p.can_up)(lambda: take(zz))
+    slot = jnp.where(zz == p.z + 1, extra, zz)
+    net.put(acc, inbox.at[slot], "up", (name, "at", extra + 1, slot), zz > p.z)
+    net.put(acc, inbox.at[zz], "down", (name, "at", extra + 1, zz), zz < p.z)
+
+
+def reduce_xy(net, name, fill, acc, ya, xa, xb, yb, inbox):
+    p = net.place
+    x, y, depth = p.x, p.y, p.depth
+    rows = acc.shape[3]
+    half = rows // 2
+    a, b = pl.ds(0, half), pl.ds(half, half)
+
+    def key(what, zz):
+        return (name + what, "at", depth, zz)
+
+    def step(i):
+        if i < depth:
+            zz = p.far[i]
+            fill(i, zz)
+            net.put(acc.at[zz, :, 1 - y, a], ya.at[zz], "y", key("ya", zz))
+            net.put(acc.at[zz, 1 - x, :, b], xb.at[zz], "x", key("xb", zz))
+        if 0 <= i - 1 < depth:
+            zz = p.far[i - 1]
+            net.got(ya.at[zz], key("ya", zz))
+            add_rows(acc.at[zz, 1 - x, y, a], ya.at[zz, 1 - x], half)
+            net.put(acc.at[zz, 1 - x, y, a], xa.at[zz], "x", key("xa", zz))
+            net.got(xb.at[zz], key("xb", zz))
+            add_rows(acc.at[zz, x, 1 - y, b], xb.at[zz, 1 - y], half)
+            net.put(acc.at[zz, x, 1 - y, b], yb.at[zz], "y", key("yb", zz))
+            add_rows(acc.at[zz, x, y, a], ya.at[zz, x], half)
+            add_rows(acc.at[zz, x, y, b], xb.at[zz, y], half)
+        if 0 <= i - 2 < depth:
+            zz = p.far[i - 2]
+            net.got(xa.at[zz], key("xa", zz))
+            add_rows(acc.at[zz, x, y, a], xa.at[zz], half)
+            net.got(yb.at[zz], key("yb", zz))
+            add_rows(acc.at[zz, x, y, b], yb.at[zz], half)
+            chain_z(net, name + "z", zz, acc.at[zz, x, y], inbox, rows)
+
+    return step
+
+
+def reduce_scratch(depth, rows, wide):
+    half = rows // 2
+    return [
+        pltpu.VMEM((depth, 2, 2, rows, wide), BF16),
+        pltpu.VMEM((depth, 2, half, wide), BF16),
+        pltpu.VMEM((depth, half, wide), BF16),
+        pltpu.VMEM((depth, 2, half, wide), BF16),
+        pltpu.VMEM((depth, half, wide), BF16),
+        pltpu.VMEM((depth + 1, rows, wide), BF16),
+    ]
+
+
+def widen(dst, src, rows):
+    def body(i, carry):
+        at = pl.ds(pl.multiple_of(i * 16, 16), 16)
+        dst[at, :] = src[at, :].astype(F32)
+        return carry
+
+    lax.fori_loop(0, rows // 16, body, 0)
+
+
+def back_kernel(
+    depth, part, out_part, x_rows, g_rows, hid, gate_low, up_low,
+    total, out_other, w_gate_grad, w_up_grad, w_down_grad,
+    acc, ya, xa, xb, yb, inbox, rc, big, left, right, found, found_down,
+    send, recv, local, load_sems, save_sems,
+):
+    p = Place(depth)
+    net = Net(p, send, recv, local)
+    c = p.c
+    rows, width = total.shape
+    local_experts = x_rows.shape[0]
+
+    def loads(u):
+        e, slot = u // 2, u % 2
+        if u % 2 == 0:
+            pairs = ((x_rows, big.at[slot]), (gate_low, left.at[slot]), (up_low, right.at[slot]))
+        else:
+            pairs = ((g_rows, big.at[slot]), (hid, left.at[slot]))
+        return [
+            pltpu.make_async_copy(src.at[e], dst, load_sems.at[slot, j])
+            for j, (src, dst) in enumerate(pairs)
+        ]
+
+    def saves(u):
+        e = u // 2
+        if u % 2 == 0:
+            targets = (w_gate_grad, w_up_grad)
+            return [
+                pltpu.make_async_copy(found.at[j], ref.at[e], save_sems.at[j])
+                for j, ref in enumerate(targets)
+            ]
+        return [pltpu.make_async_copy(found_down, w_down_grad.at[e], save_sems.at[2])]
+
+    units = 2 * local_experts
+
+    def unit(u):
+        slot = u % 2
+        for copy in loads(u):
+            copy.wait()
+        if u >= 2:
+            for copy in saves(u - 2):
+                copy.wait()
+        if u % 2 == 0:
+            wide = 256
+
+            def body(i, carry):
+                at = pl.ds(pl.multiple_of(i * wide, wide), wide)
+                tile = big[slot, :, at]
+                for j, ref in enumerate((left, right)):
+                    found[j, at, :] = lax.dot_general(
+                        tile, ref[slot], CONTRACT_FIRST, preferred_element_type=F32
+                    )
+                return carry
+
+            lax.fori_loop(0, width // wide, body, 0)
+        else:
+            wide = 512
+
+            def body(i, carry):
+                at = pl.ds(pl.multiple_of(i * wide, wide), wide)
+                found_down[:, at] = lax.dot_general(
+                    left[slot], big[slot, :, at], CONTRACT_FIRST, preferred_element_type=F32
+                )
+                return carry
+
+            lax.fori_loop(0, width // wide, body, 0)
+        for copy in saves(u):
+            copy.start()
+        if u + 2 < units:
+            for copy in loads(u + 2):
+                copy.start()
+
+    fills = []
+    for i in range(depth):
+        zz = p.far[i]
+        fills.append(net.local(part.at[zz, :, :, c], acc.at[zz]))
+    for u in range(2):
+        for copy in loads(u):
+            copy.start()
+    greet(p, ("x", "y", "c", "z"))
+    for i in range(depth):
+        zz = p.far[i]
+        net.put(part.at[zz, :, :, 1 - c], rc.at[zz], "c", ("c", "at", depth, zz))
+    for zz in range(depth):
+        net.put(out_part.at[zz, :, :, 1 - c], out_other.at[zz], "c", ("oc", "at", depth, zz))
+
+    def fill(i, zz):
+        fills[i].wait()
+        net.got(rc.at[zz], ("c", "at", depth, zz))
+        for xx in range(2):
+            for yy in range(2):
+                add_rows(acc.at[zz, xx, yy], rc.at[zz, xx, yy], rows)
+
+    step = reduce_xy(net, "b", fill, acc, ya, xa, xb, yb, inbox)
+    u = 0
+    for i in range(depth + 2):
+        step(i)
+        for _ in range(2 if i < depth - 1 else 1):
+            if u < units:
+                unit(u)
+                u += 1
+    while u < units:
+        unit(u)
+        u += 1
+    for k in (units - 2, units - 1):
+        for copy in saves(k):
+            copy.wait()
+
+    def last(i, carry):
+        at = pl.ds(pl.multiple_of(i * 16, 16), 16)
+        total[at, :] = acc[p.z, p.x, p.y, at, :].astype(F32)
+        return carry
+
+    lax.fori_loop(0, rows // 16, last, 0)
+    for zz in range(depth):
+        net.got(out_other.at[zz], ("oc", "at", depth, zz))
+    net.finish()
+
+
+def reduce_back(depth, part, out_part, x_rows, g_rows, hid, gate_low, up_low):
+    count, rows, wide = part.shape
+    width = out_part.shape[2]
+    local_experts, slots, hidden = hid.shape
+    shape = jax.ShapeDtypeStruct
+    return pl.pallas_call(
+        functools.partial(back_kernel, depth),
+        out_shape=[
+            shape((rows, wide), F32),
+            shape((depth, 2, 2, rows, width), BF16),
+            shape((local_experts, width, hidden), F32),
+            shape((local_experts, width, hidden), F32),
+            shape((local_experts, hidden, width), F32),
+        ],
+        in_specs=[ANY] * 7,
+        out_specs=[VMEM] + [ANY] * 4,
+        scratch_shapes=reduce_scratch(depth, rows, wide)
+        + [
+            pltpu.VMEM((depth, 2, 2, rows, wide), BF16),
+            pltpu.VMEM((2, slots, width), BF16),
+            pltpu.VMEM((2, slots, hidden), BF16),
+            pltpu.VMEM((2, slots, hidden), BF16),
+            pltpu.VMEM((2, width, hidden), F32),
+            pltpu.VMEM((hidden, width), F32),
+        ]
+        + sems()
+        + [pltpu.SemaphoreType.DMA((2, 3)), pltpu.SemaphoreType.DMA((3,))],
+        compiler_params=comm_params(3, 60),
+        name="reduce_back",
+    )(
+        part.reshape(depth, 2, 2, 2, rows, wide),
+        out_part.reshape(depth, 2, 2, 2, rows, width),
+        x_rows, g_rows, hid, gate_low, up_low,
+    )
+
+
+def attend_back_kernel(
+    depth, mine, act_hbm, wqkv_hbm, wo_hbm, qkv_hbm, att_hbm, seg_col, seg_row, out_part, out_other,
+    qkv_part, act_grad, o_sum, out_sum,
+    acc, ya, xa, xb, yb, inbox, other, bg, act, wqkv, wo, qkv, att, ag, low, o_acc, o_inbox, o_rx,
+    send, recv, local, other_sems,
+):
+    p = Place(depth)
+    net = Net(p, send, recv, local)
+    x, y, c = p.x, p.y, p.c
+    rows, width = out_sum.shape
+    seq = act.shape[0]
+    cols = wo.shape[0]
+    heads = cols // HEAD
+    o_cols = o_sum.shape[1]
+
+    def block(t):
+        return bg.at[pl.ds(pl.multiple_of(t * rows, rows), rows)]
+
+    own = net.local(mine, block(p.t))
+    load_wo = net.local(wo_hbm, wo)
+    load_att = net.local(att_hbm, att)
+    load_qkv = net.local(qkv_hbm, qkv)
+    load_act = net.local(act_hbm, act)
+    load_w = net.local(wqkv_hbm, wqkv)
+    greet(p, ("x", "y", "c", "z"))
+    own.wait()
+    net.put(block(p.t), block(p.t), "y", ("bg", "y"))
+    net.put(block(p.t), block(p.t), "c", ("bg", "c0"))
+
+    def load_other(i):
+        zz = p.far[i]
+        return [
+            pltpu.make_async_copy(out_part.at[zz, :, :, c], acc.at[zz], other_sems.at[0, i % 2]),
+            pltpu.make_async_copy(out_other.at[zz], other.at[i % 2], other_sems.at[1, i % 2]),
+        ]
+
+    for i in range(2):
+        for copy in load_other(i):
+            copy.start()
+
+    def fill(i, zz):
+        for copy in load_other(i):
+            copy.wait()
+        for xx in range(2):
+            for yy in range(2):
+                add_rows(acc.at[zz, xx, yy], other.at[i % 2, xx, yy], rows)
+        if i + 2 < depth:
+            for copy in load_other(i + 2):
+                copy.start()
+
+    out_step = reduce_xy(net, "out", fill, acc, ya, xa, xb, yb, inbox)
+
+    def o_pair(z):
+        return o_acc.at[:, pl.ds(pl.multiple_of(z * (2 * o_cols), LANES), 2 * o_cols)]
+
+    def o_step(i):
+        if i < depth:
+            chain_z(net, "oz", p.far[i], o_pair(p.far[i]), o_inbox, cols)
+        if i == depth - 1:
+            theirs = pl.ds(pl.multiple_of((p.z * 2 + 1 - x) * o_cols, LANES), o_cols)
+            net.put(o_acc.at[:, theirs], o_rx, "x", ("ox",))
+
+    out_step(0)
+    far = block((1 - y) * 2 + c)
+    net.got(far, ("bg", "y"))
+    net.put(far, far, "c", ("bg", "c1"))
+    net.got(block(y * 2 + 1 - c), ("bg", "c0"))
+    net.got(block((1 - y) * 2 + 1 - c), ("bg", "c1"))
+    load_wo.wait()
+    ag[...] = lax.dot_general(
+        bg[...], wo[...], CONTRACT_LAST, preferred_element_type=F32
+    ).astype(BF16)
+    out_step(1)
+    load_att.wait()
+    wide = 512
+
+    def o_body(i, carry):
+        at = pl.ds(pl.multiple_of(i * wide, wide), wide)
+        o_acc[:, at] = lax.dot_general(
+            att[...], bg[:, at], CONTRACT_FIRST, preferred_element_type=F32
+        ).astype(BF16)
+        return carry
+
+    lax.fori_loop(0, width // wide, o_body, 0)
+    load_qkv.wait()
+    scale = 1.0 / math.sqrt(HEAD)
+    same = seg_col[...] == seg_row[...]
+    for h in range(heads):
+        o_step(h)
+        out_step(2 + h)
+        at = slice(h * HEAD, (h + 1) * HEAD)
+        query = qkv[:, h * HEAD : (h + 1) * HEAD]
+        keys = qkv[:, cols + h * HEAD : cols + (h + 1) * HEAD]
+        values = qkv[:, 2 * cols + h * HEAD : 2 * cols + (h + 1) * HEAD]
+        grad = ag[:, at]
+        scores = lax.dot_general(query, keys, CONTRACT_LAST, preferred_element_type=F32) * scale
+        scores = jnp.where(same, scores, -1e30)
+        expo = jnp.exp(scores - jnp.max(scores, axis=-1, keepdims=True))
+        probs = expo / jnp.sum(expo, axis=-1, keepdims=True)
+        prob_grad = lax.dot_general(grad, values, CONTRACT_LAST, preferred_element_type=F32)
+        inner = jnp.sum(probs * prob_grad, axis=-1, keepdims=True)
+        score_grad = (probs * (prob_grad - inner) * scale).astype(BF16)
+        low[:, at] = jnp.dot(score_grad, keys, preferred_element_type=F32).astype(BF16)
+        low[:, cols + h * HEAD : cols + (h + 1) * HEAD] = lax.dot_general(
+            score_grad, query, CONTRACT_FIRST, preferred_element_type=F32
+        ).astype(BF16)
+        low[:, 2 * cols + h * HEAD : 2 * cols + (h + 1) * HEAD] = lax.dot_general(
+            probs.astype(BF16), grad, CONTRACT_FIRST, preferred_element_type=F32
+        ).astype(BF16)
+    for i in range(heads, max(depth, heads)):
+        o_step(i)
+        out_step(2 + i)
+    load_act.wait()
+    load_w.wait()
+    w_rows = wqkv.shape[1]
+
+    def w_body(f, carry):
+        at = pl.ds(pl.multiple_of(f * w_rows, w_rows), w_rows)
+        qkv_part[f] = lax.dot_general(
+            act[:, at], low[...], CONTRACT_FIRST, preferred_element_type=F32
+        ).astype(BF16)
+        act_grad[:, at] = lax.dot_general(
+            low[...], wqkv[f], CONTRACT_LAST, preferred_element_type=F32
+        )
+        return carry
+
+    lax.fori_loop(0, wqkv.shape[0], w_body, 0)
+    widen(out_sum, acc.at[p.z, x, y], rows)
+    net.got(o_rx, ("ox",))
+    at_o = pl.ds(pl.multiple_of((p.z * 2 + x) * o_cols, LANES), o_cols)
+
+    def o_last(i, carry):
+        at = pl.ds(pl.multiple_of(i * 16, 16), 16)
+        o_sum[at, :] = o_acc[at, at_o].astype(F32) + o_rx[at, :].astype(F32)
+        return carry
+
+    lax.fori_loop(0, cols // 16, o_last, 0)
+    net.finish()
+
+
+def attend_back(depth, mine, act, wqkv, wo, qkv, att, segments, out_part, out_other, o_cols):
+    rows, width = mine.shape
+    seq, cols = att.shape
+    fsdp, w_rows, w_wide = wqkv.shape
+    shape = jax.ShapeDtypeStruct
+    return pl.pallas_call(
+        functools.partial(attend_back_kernel, depth),
+        out_shape=[
+            shape((fsdp, w_rows, w_wide), BF16),
+            shape((seq, width), F32),
+            shape((cols, o_cols), F32),
+            shape((rows, width), F32),
+        ],
+        in_specs=[ANY] * 6 + [VMEM] * 2 + [ANY] * 2,
+        out_specs=[VMEM] * 4,
+        scratch_shapes=reduce_scratch(depth, rows, width)
+        + [
+            pltpu.VMEM((2, 2, 2, rows, width), BF16),
+            pltpu.VMEM((seq, width), BF16),
+            pltpu.VMEM((seq, width), BF16),
+            pltpu.VMEM((fsdp, w_rows, w_wide), BF16),
+            pltpu.VMEM((cols, width), BF16),
+            pltpu.VMEM((seq, w_wide), BF16),
+            pltpu.VMEM((seq, cols), BF16),
+            pltpu.VMEM((seq, cols), BF16),
+            pltpu.VMEM((seq, w_wide), BF16),
+            pltpu.VMEM((cols, width), BF16),
+            pltpu.VMEM((depth + 1, cols, 2 * o_cols), BF16),
+            pltpu.VMEM((cols, o_cols), BF16),
+        ]
+        + sems()
+        + [pltpu.SemaphoreType.DMA((2, 2))],
+        compiler_params=comm_params(4, 63),
+        name="attend_back",
+    )(
+        mine, act, wqkv, wo, qkv, att, segments[:, None], segments[None, :],
+        out_part.reshape(depth, 2, 2, 2, rows, width), out_other,
+    )
+
+
+def last_kernel(
+    depth, tail, qkv_part, row_part, q_sum, k_sum, v_sum, row_sum, tail_sum,
+    q_acc, q_rx, q_inbox, t_acc, t_rc, t_ry, s_acc, s_rc, s_ry, s_rx, s_inbox, send, recv, local,
+):
+    p = Place(depth)
+    net = Net(p, send, recv, local)
+    x, y, c = p.x, p.y, p.c
+    rows, width = row_sum.shape
+    w_rows, w_cols = q_sum.shape
+    small = s_acc.shape[3]
+    loads = [net.local(qkv_part.at[p.far[i], x], q_acc.at[p.far[i]]) for i in range(depth)]
+    t_load = net.local(row_part.at[:, c], t_acc)
+    s_load = net.local(tail.at[:, :, :, c], s_acc)
+    greet(p, ("x", "y", "c", "z"))
+    for i in range(depth):
+        zz = p.far[i]
+        net.put(qkv_part.at[zz, 1 - x], q_rx.at[zz], "x", ("qx", "at", depth, zz))
+    net.put(tail.at[:, :, :, 1 - c], s_rc, "c", ("sc",))
+    net.put(row_part.at[:, 1 - c], t_rc, "c", ("tc",))
+    t_load.wait()
+    net.got(t_rc, ("tc",))
+    add_rows(t_acc.at[1 - y], t_rc.at[1 - y], rows)
+    net.put(t_acc.at[1 - y], t_ry, "y", ("ty",))
+    s_load.wait()
+    net.got(s_rc, ("sc",))
+    for zz in range(depth):
+        for xx in range(2):
+            add_rows(s_acc.at[zz, xx, 1 - y], s_rc.at[zz, xx, 1 - y], small)
+    net.put(s_acc.at[:, :, 1 - y], s_ry, "y", ("sy",))
+    for zz in range(depth):
+        for xx in range(2):
+            add_rows(s_acc.at[zz, xx, y], s_rc.at[zz, xx, y], small)
+    for i in range(depth):
+        zz = p.far[i]
+        loads[i].wait()
+        net.got(q_rx.at[zz], ("qx", "at", depth, zz))
+        add_rows(q_acc.at[zz], q_rx.at[zz], w_rows)
+        chain_z(net, "qz", zz, q_acc.at[zz], q_inbox, w_rows)
+        if i == 0:
+            net.got(s_ry, ("sy",))
+            for z in range(depth):
+                for xx in range(2):
+                    add_rows(s_acc.at[z, xx, y], s_ry.at[z, xx], small)
+            net.put(s_acc.at[:, 1 - x, y], s_rx, "x", ("sx",))
+    net.got(s_rx, ("sx",))
+    for z in range(depth):
+        add_rows(s_acc.at[z, x, y], s_rx.at[z], small)
+    for i in range(depth):
+        chain_z(net, "sz", p.far[i], s_acc.at[p.far[i], x, y], s_inbox, small)
+
+    def q_last(i, carry):
+        at = pl.ds(pl.multiple_of(i * 16, 16), 16)
+        for j, ref in enumerate((q_sum, k_sum, v_sum)):
+            ref[at, :] = q_acc[p.z, at, pl.ds(j * w_cols, w_cols)].astype(F32)
+        return carry
+
+    lax.fori_loop(0, w_rows // 16, q_last, 0)
+    net.got(t_ry, ("ty",))
+
+    def rows_last(i, carry):
+        at = pl.ds(pl.multiple_of(i * 16, 16), 16)
+        row_sum[at, :] = (
+            t_acc[y, at, :].astype(F32) + t_rc[y, at, :].astype(F32) + t_ry[at, :].astype(F32)
+        )
+        return carry
+
+    lax.fori_loop(0, rows // 16, rows_last, 0)
+    widen(tail_sum, s_acc.at[p.z, x, y], small)
+    net.finish()
+
+
+def last_reduce(depth, tail, qkv_part, row_part):
+    count, small, lanes = tail.shape
+    fsdp, w_rows, w_wide = qkv_part.shape
+    tp, rows, width = row_part.shape
+    w_cols = w_wide // 3
+    shape = jax.ShapeDtypeStruct
+    return pl.pallas_call(
+        functools.partial(last_kernel, depth),
+        out_shape=[shape((w_rows, w_cols), F32)] * 3
+        + [shape((rows, width), F32), shape((small, lanes), F32)],
+        in_specs=[ANY] * 3,
+        out_specs=[VMEM] * 5,
+        scratch_shapes=[
+            pltpu.VMEM((depth, w_rows, w_wide), BF16),
+            pltpu.VMEM((depth, w_rows, w_wide), BF16),
+            pltpu.VMEM((depth + 1, w_rows, w_wide), BF16),
+            pltpu.VMEM((2, rows, width), BF16),
+            pltpu.VMEM((2, rows, width), BF16),
+            pltpu.VMEM((rows, width), BF16),
+            pltpu.VMEM((depth, 2, 2, small, lanes), BF16),
+            pltpu.VMEM((depth, 2, 2, small, lanes), BF16),
+            pltpu.VMEM((depth, 2, small, lanes), BF16),
+            pltpu.VMEM((depth, small, lanes), BF16),
+            pltpu.VMEM((depth + 1, small, lanes), BF16),
+        ]
+        + sems(),
+        compiler_params=comm_params(5, 40),
+        name="last_reduce",
+    )(
+        tail.reshape(depth, 2, 2, 2, small, lanes),
+        qkv_part.reshape(depth, 2, w_rows, w_wide),
+        row_part.reshape(2, 2, rows, width),
+    )
 
 
 def norm_rows(values, gain):
@@ -36,6 +1249,111 @@
 def contract_first(left, right):
     return lax.dot_general(
         left, right, (((0,), (0,)), ((), ())), preferred_element_type=jnp.float32
+    )
+
+
+def dense_layer(
+    inputs, out_grad, segments, routes, attn_gain, w_query, w_key, w_value, w_output,
+    moe_gain, router, w_gate, w_up, w_down,
+):
+    tp, fsdp = lax.axis_size("tp"), lax.axis_size("fsdp")
+    depth = fsdp // 2
+    rows, width = inputs.shape
+    local_experts = w_gate.shape[0]
+    experts = local_experts * fsdp
+    top_k = routes.shape[1]
+    capacity = 3 * rows * top_k // (2 * experts)
+    w_rows, w_cols = w_query.shape
+    heads = w_cols // HEAD
+    seq = tp * rows
+
+    named = jnp.any(
+        routes[:, :, None] == jnp.arange(experts, dtype=jnp.int32)[None, None, :], axis=1
+    )
+    hits = named.astype(F32)
+    before = (jnp.arange(rows)[:, None] > jnp.arange(rows)[None, :]).astype(F32)
+    ranks = jnp.where(named, jnp.dot(before, hits, preferred_element_type=F32), -1.0)
+    fill = jnp.zeros((rows, LANES - 3 * experts), F32)
+    blank = jnp.zeros((rows, experts), F32)
+    mask = jnp.concatenate([hits, hits, blank, fill], axis=1)
+    rank = jnp.concatenate([blank, blank, ranks, fill], axis=1)
+    router_pad = jnp.concatenate(
+        [router, router, jnp.zeros((width, LANES - 2 * experts), BF16)], axis=1
+    )
+
+    qkv_full, full_output, whole = first_gather(
+        depth, w_query, w_key, w_value, w_output, inputs, tp
+    )
+    whole_float = whole.reshape(seq, width).astype(F32)
+    normed_one, inverse_one = norm_rows(whole_float, attn_gain)
+    act_one = normed_one.astype(BF16)
+    qkv = jnp.dot(act_one, qkv_full.reshape(width, 3 * w_cols), preferred_element_type=F32).astype(BF16)
+    query, key_rows, value_rows = [
+        qkv[:, i * w_cols : (i + 1) * w_cols].reshape(seq, heads, HEAD) for i in range(3)
+    ]
+    score_scale = 1.0 / math.sqrt(HEAD)
+    scores = jnp.einsum("qhd,khd->hqk", query, key_rows, preferred_element_type=F32) * score_scale
+    scores = jnp.where((segments[:, None] == segments[None, :])[None], scores, -1e30)
+    probs = jax.nn.softmax(scores, axis=-1)
+    attended = (
+        jnp.einsum("hqk,khd->qhd", probs.astype(BF16), value_rows, preferred_element_type=F32)
+        .reshape(seq, -1)
+        .astype(BF16)
+    )
+    partial = jnp.dot(attended, full_output, preferred_element_type=F32).astype(BF16)
+    resid, gates_wide, _, _, out_part, back_part, x_rows, g_rows, hid_low, gate_low, up_low = run_moe(
+        depth, capacity, experts, partial.reshape(tp, rows, width), inputs, out_grad, moe_gain,
+        router_pad, mask, rank, w_gate, w_up, w_down,
+    )
+    back, out_other, w_gate_grad, w_up_grad, w_down_grad = reduce_back(
+        depth, back_part, out_part, x_rows, g_rows, hid_low, gate_low, up_low
+    )
+    gates = gates_wide[:, :experts]
+    act_two = (
+        resid
+        * (inverse_two := lax.rsqrt(jnp.mean(resid * resid, axis=-1, keepdims=True) + EPSILON))
+        * moe_gain
+    ).astype(BF16)
+    gate_grad = jnp.sum(back[:, width : width + tp * experts].reshape(rows, tp, experts), axis=1)
+    logit_grad = gates * (gate_grad - jnp.sum(gates * gate_grad, axis=1, keepdims=True))
+    act_two_grad = back[:, :width] + lax.dot_general(
+        logit_grad, router.astype(F32), (((1,), (1,)), ((), ())), precision=HIGHEST
+    )
+    router_part = lax.dot_general(
+        act_two.astype(F32), logit_grad, (((0,), (0,)), ((), ())), precision=HIGHEST
+    )
+    resid_part, gain_two_part = norm_back(resid, inverse_two, moe_gain, act_two_grad)
+    resid_grad = out_grad.astype(F32) + resid_part
+    qkv_part, act_one_grad, o_sum, out_sum = attend_back(
+        depth, resid_grad.astype(BF16), act_one, qkv_full, full_output, qkv, attended, segments,
+        out_part, out_other, w_output.shape[1],
+    )
+    whole_part, gain_one_part = norm_back(whole_float, inverse_one, attn_gain, act_one_grad)
+
+    count = fsdp * tp
+    piece = width // count
+    small = jnp.concatenate([router_part, gain_one_part[:, None], gain_two_part[:, None]], axis=1)
+    small = small.astype(BF16).reshape(count, piece, experts + 2)
+    tail = jnp.pad(small, ((0, 0), (0, -piece % 16), (0, LANES - experts - 2)))
+    q_sum, k_sum, v_sum, row_sum, side = last_reduce(
+        depth, tail, qkv_part, whole_part.astype(BF16).reshape(tp, rows, width)
+    )
+    output = (resid + out_sum).astype(BF16)
+    input_grad = resid_grad + row_sum
+    side = side[:piece]
+    return (
+        output,
+        input_grad,
+        side[:, experts],
+        q_sum,
+        k_sum,
+        v_sum,
+        o_sum,
+        side[:, experts + 1],
+        side[:, :experts],
+        w_gate_grad,
+        w_up_grad,
+        w_down_grad,
     )
 
 
@@ -332,9 +1650,20 @@
     )
 
 
+def layer(*args):
+    tokens = args[0].shape[0] * lax.axis_size("fsdp") * lax.axis_size("tp")
+    held = 6 * tokens * (args[0].shape[1] + LANES) * 2
+    even = lax.axis_size("tp") == 4 and lax.axis_size("fsdp") % 2 == 0
+    experts = args[11].shape[0] * lax.axis_size("fsdp")
+    narrow = lax.axis_size("tp") * experts <= LANES and args[1].shape[1] // (lax.axis_size("tp") * lax.axis_size("fsdp")) <= args[0].shape[0]
+    if held <= HBM_BUDGET and even and narrow:
+        return dense_layer(*args)
+    return per_device(*args)
+
+
 def solution(mesh):
     return jax.shard_map(
-        per_device,
+        layer,
         mesh=mesh,
         in_specs=(
             P(("fsdp", "tp"), None),

time: 1780 us -> 708 us (0.40)
  waiting for transfers between devices: 1350 us -> 0 us
  Pallas kernels: 0 us -> 626 us
  matrix products: 203 us -> 12.4 us
  local copies, waits for them, and re-layouts: 75.9 us -> 33.9 us
  other arithmetic: 65.8 us -> 25.8 us
  blocking collectives: 28.7 us -> 0 us
  starting transfers between devices: 25 us -> 0 us
    reduce_scatter x11 -> x0, waiting for transfers between devices: 638 us -> none  [the longest x1 127 us: per_device(): lax.psum_scatter(down_term.astype(jnp.bfloat16), 'tp', scatter_dimension=...]
    pallas_call x0 -> x5, Pallas kernels: none -> 626 us  [the longest x1 203 us: run_moe(): pl.pallas_call(functools.partial(moe_kernel, depth, capacity, experts, bl...]
    all_to_all x4 -> x0, waiting for transfers between devices: 399 us -> none  [the longest x2 179 us: send_rows(): lax.all_to_all(buffer, 'fsdp', split_axis=1, concat_axis=1, tiled=True)]
    all_gather x9 -> x0, waiting for transfers between devices: 307 us -> none  [the longest x1 47.9 us: per_device(): lax.all_gather(w_query, 'fsdp', axis=0, tiled=True)]
    dot_general x32 -> x7, matrix products: 203 us -> 12.4 us  [the longest x1 3.42 us: dense_layer(): jnp.dot(act_one, qkv_full.reshape(width, 3 * w_cols), preferred_element_t...]
    gather x4 -> x0, local copies, waits for them, and re-layouts: 47.3 us -> none  [the longest x1 15.5 us: per_device(): padded_grad[sources].reshape(1, fsdp_count, local_experts * capacity, width)]
    unnamed x2 -> x0, blocking collectives: 28.7 us -> none
    convert_element_type x13 -> x6, other arithmetic: 34.1 us -> 10.2 us  [the longest x2 4.19 us: dense_layer(): act_one = normed_one.astype(BF16)]
  transfers between devices with their start and end apart: 24 -> 0, of which waited for: 22 -> 0; matrix products, arithmetic and copies ran while one was open for 15% -> 0% of each run, Pallas kernels for 0% -> 0%
where the time goes in v2:
time: 708 us; the launch traced here: 700 us
  Pallas kernels  626 us (88%)
  local copies, waits for them, and re-layouts  33.9 us (5%)
  other arithmetic  25.8 us (4%)
  matrix products  12.4 us (2%)
    pallas_call x1, Pallas kernels, run_moe(): pl.pallas_call(functools.partial(moe_kernel, depth, capacity, experts, bl...  203 us
    pallas_call x1, Pallas kernels, attend_back(): pl.pallas_call(functools.partial(attend_back_kernel, depth), out_shape=[s...  130 us
    pallas_call x1, Pallas kernels, reduce_back(): pl.pallas_call(functools.partial(back_kernel, depth), out_shape=[shape((r...  104 us
    pallas_call x1, Pallas kernels, first_gather(): pl.pallas_call(functools.partial(first_kernel, depth), out_shape=[jax.Sha...  98.8 us
    pallas_call x1, Pallas kernels, last_reduce(): pl.pallas_call(functools.partial(last_kernel, depth), out_shape=[shape((w...  90.1 us
    unnamed x56, local copies, waits for them, and re-layouts  25.6 us

profile of v2, /device:TPU:2, one launch (start us, length us, event | category | flops | bytes accessed | tf_op | source)
XLA Modules:
  0.0 699.6 jit_solution(18382738432462756801)
XLA Ops:
  0.6 98.8 %first_gather.1 = (bf16[8,256,1536]{2,1,0:T(8,128)(2,1)}, bf16[512,2048]{1,0:T(8,128)(2,1)}, bf16[4,128,2048]{2,1,0:T(8,128)(2,1)}) custom-call(bf16[256,512]{1,0:T(8,128)(2,1)} %wq.1, bf16[256,512]{1,0:T(8,128)(2,1)} %wk.1, bf16[256,512]{1,0:T(8,128)(2,1)} %wv.1, bf16[512,256]{1,0:T(8,128)(2,1)} %wo.1, bf16[128,2048]{1,0:T(8,128)(2,1)} %inp.3), custom_call_target="tpu_custom_call" | custom-call | tf_op jit(solution)/shard_map/first_gather/pallas_call | solution.py:280
  99.5 2.2 fusion.1
  101.7 2.3 fusion.3
  104.0 3.4 convolution_convert_fusion.1.qkv_hbm
  107.5 0.0 copy-start.7
  107.5 0.0 copy-start.17
  107.5 0.2 slice_bitcast_fusion.1
  107.7 0.7 fusion.23
  108.4 0.2 copy-done.7
  108.6 0.2 broadcast_compare_fusion
  108.8 4.0 fusion.35
  112.8 0.2 copy.108
  113.1 2.8 fusion.17
  115.9 0.0 copy-start.12
  115.9 0.0 copy-start.14
  115.9 0.0 copy-done.10
  115.9 2.6 convolution_convert_fusion
  118.5 0.1 copy.96
  118.7 0.1 convolution_select_fusion
  118.8 0.1 copy.94
  118.9 0.1 pad.10.clone
  119.0 0.8 maximum_maximum_fusion.1
  119.8 0.3 copy.92
  120.0 0.1 pad.16.clone
  120.1 1.1 maximum_maximum_fusion.router
  121.2 203.3 %moe.1 = (f32[128,2048]{1,0:T(8,128)}, f32[128,128]{1,0:T(8,128)}, bf16[32,128,2176]{2,1,0:T(8,128)(2,1)}, bf16[32,128,2048]{2,1,0:T(8,128)(2,1)}, bf16[32,128,2...) custom-call(bf16[2,2,128,2048]{3,2,1,0:T(8,128)(2,1)} %bitcast.71, ...), custom_call_target="tpu_custom_call" | custom-call | tf_op jit(solution)/shard_map/moe/pallas_call | solution.py:669
  324.6 104.2 %reduce_back.1 = (f32[128,2176]{1,0:T(8,128)}, bf16[4,2,2,128,2048]{4,3,2,1,0:T(8,128)(2,1)}, f32[4,2048,256]{2,1,0:T(8,128)}, f32[4,2048,256]{2,1,0:T(8,128)}, f32[4,256,2048]{2,1,0:T(8,128)}) custom-call(bf16[4,2,2,2,128,2176]{5,4,3,2,1,0:T(8,128)(2,1)} %bitcast.65, bf16[4,2,2,2,128,2048]{5,4,3,2,1,0:T(8,128)(2,1)} %bitcast.63, ...), custom_call_target="tpu_custom_call" | custom-call | tf_op jit(solution)/shard_map/reduce_back/pallas_call | solution.py:911
  428.8 0.8 slice.32
  429.7 0.1 copy.98
  429.8 0.1 copy.100
  429.9 0.1 multiply_reduce_fusion.3
  430.0 0.2 multiply_reduce_fusion.2
  430.2 0.0 copy-start.16
  430.2 2.3 multiply_reduce_fusion
  432.5 2.6 fusion.34
  435.1 2.0 copy.109.att_hbm
  437.1 1.9 fusion.5.act_hbm
  439.0 0.9 copy.101.seg_col
  439.9 129.6 %attend_back.1 = (bf16[8,256,1536]{2,1,0:T(8,128)(2,1)}, f32[512,2048]{1,0:T(8,128)}, f32[512,256]{1,0:T(8,128)}, f32[128,2048]{1,0:T(8,128)}) custom-call(bf16[128,2048]{1,0:T(8,128)(2,1)} %get-tuple-element.130.mine, bf16[512,2048]{1,0:T(8,128)(2,1)} %fusion.5.act_hbm, bf16[8,256,1536]{2,1,0:T(8,128)(2,1)} %get-tuple-element.39.wqkv_hbm, ...), custom_call_target="tpu_custom_call" | custom-call | tf_op jit(solution)/shard_map/attend_back/pallas_call | solution.py:1087
  569.4 4.2 fusion.11
  573.7 0.4 copy-done.6
  574.1 1.0 fusion.10
  575.1 0.2 copy-done.5
  575.3 0.5 convolution_convert_fusion.2
  575.8 0.3 copy.110
  576.1 1.0 concatenate.27
  577.1 1.8 concatenate.28
  578.9 1.6 fusion.22
  580.5 2.8 copy-done
  583.3 90.1 %last_reduce.1 = (f32[256,512]{1,0:T(8,128)S(1)}, f32[256,512]{1,0:T(8,128)S(1)}, f32[256,512]{1,0:T(8,128)S(1)}, f32[128,2048]{1,0:T(8,128)S(1)}, f32[64,128]{1,0:T(8,128)S(1)}) custom-call(bf16[4,2,2,2,64,128]{5,4,3,2,1,0:T(8,128)(2,1)S(1)} %bitcast.61, bf16[4,2,256,1536]{3,2,1,0:T(8,128)(2,1)S(1)} %bitcast.60, bf16[2,2,128,2048]{3,2,1,0:T(8,128)(2,1)S(1)} %bitcast.59), custom_call_target="tpu_custom_call" | custom-call | tf_op jit(solution)/shard_map/last_reduce/pallas_call | solution.py:1199
  673.4 0.0 copy-start.1
  673.5 1.1 add.51
  674.6 0.0 copy-done.1
  674.6 0.7 copy.105
  675.3 0.7 slice_reduce_fusion
  676.0 2.5 add_convert_fusion
  678.4 2.0 copy.129
  680.4 0.8 copy.130
  681.2 0.8 copy.131
  682.0 0.8 copy.132
  682.8 7.8 %copy.133 = f32[4,2048,256]{2,1,0:T(8,128)} copy(f32[4,2048,256]{2,1,0:T(8,128)} %get-tuple-element.167) | data formatting | bytes 16777216
  690.6 4.3 copy.134
  694.8 1.0 slice-done.1
  695.8 3.4 copy.135
  (45 shorter events, 0.2 us)
Async XLA Ops:
  99.4 4.6 copy-start.8
  107.5 1.1 copy-start.7
  107.5 1.1 copy-start.17
  113.1 2.9 copy-start.10
  115.9 2.7 copy-start.12
  115.9 2.6 copy-start.18
  115.9 3.9 copy-start.14
  324.6 105.3 %copy-start.11 = (f32[128,128]{1,0:T(8,128)S(1)}, f32[128,128]{1,0:T(8,128)}, u32[]{:S(2)}) copy-start(f32[128,128]{1,0:T(8,128)} %get-tuple-element.50) | copy-start | bytes 196612
  324.6 105.4 %copy-start.4 = (f32[128,2048]{1,0:T(8,128)S(1)}, f32[128,2048]{1,0:T(8,128)}, u32[]{:S(2)}) copy-start(f32[128,2048]{1,0:T(8,128)} %get-tuple-element.41) | copy-start | bytes 3145732
  324.6 105.6 %copy-start.15 = (f32[2048]{0:T(1024)S(1)}, f32[2048]{0:T(1024)}, u32[]{:S(2)}) copy-start(f32[2048]{0:T(1024)} %param.23) | copy-start | bytes 24580
  430.2 6.9 copy-start.2
  430.2 6.9 copy-start.16
  569.4 4.3 copy-start.3
  569.4 4.7 copy-start.6
  574.1 1.2 copy-start.5
  580.5 2.8 copy-start
  583.3 90.1 %copy-start.9 = (f32[128,2048]{1,0:T(8,128)S(1)}, f32[128,2048]{1,0:T(8,128)}, u32[]{:S(2)}) copy-start(f32[128,2048]{1,0:T(8,128)} %get-tuple-element.131) | copy-start | bytes 3145732
  673.4 1.1 copy-start.1
  673.5 8.6 %copy-start.13 = (f32[512,256]{1,0:T(8,128)S(1)}, f32[512,256]{1,0:T(8,128)}, u32[]{:S(2)}) copy-start(f32[512,256]{1,0:T(8,128)} %get-tuple-element.164) | copy-start | bytes 1572868
  678.4 12.2 %slice-start.2 = ((s8[8388608]{0:T(1024)(128)(4,1)}), s8[4194304]{0:T(1024)(128)(4,1)S(1)}, s32[]{:S(2)}) async-start(s8[8388608]{0:T(1024)(128)(4,1)} %bitcast.68), calls=%async_computation.2 | async-start | bytes 8388608
  682.8 7.8 %slice-start.3 = ((s8[8388608]{0:T(1024)(128)(4,1)}), s8[4194304]{0:T(1024)(128)(4,1)S(1)}, s32[]{:S(2)}) async-start(s8[8388608]{0:T(1024)(128)(4,1)} %bitcast.68), calls=%async_computation.3 | async-start | bytes 8388608
  682.8 12.0 %slice-start = ((s8[8388608]{0:T(1024)(128)(4,1)}), s8[4194304]{0:T(1024)(128)(4,1)S(1)}, s32[]{:S(2)}) async-start(s8[8388608]{0:T(1024)(128)(4,1)} %bitcast.66), calls=%async_computation | async-start | bytes 8388608
  690.6 5.2 slice-start.1

commit v3 on v2

--- a/solution.py
+++ b/solution.py
@@ -207,12 +207,12 @@
     p = net.place
     offs = p.offs
 
+    def begin():
+        net.put(own, block(p.z, p.x), "x", (name, "x"))
+
     def step(i):
-        if i >= len(offs):
-            return
         off = offs[i]
         if off == 0:
-            net.put(own, block(p.z, p.x), "x", (name, "x"))
             placed.wait()
             net.got(block(p.z, 1 - p.x), (name, "x"))
         valid = p.valid(off)
@@ -224,72 +224,7 @@
         if off >= 0:
             net.put(ref, ref, "down", (name, "z", off + 1), both(valid, p.can_down))
 
-    return step, lambda: None
-
-
-def first_kernel(
-    depth, wq, wk, wv, wo, inp, qkv, full_o, rows, send, recv, local
-):
-    p = Place(depth)
-    net = Net(p, send, recv, local)
-    w_rows, w_cols = wq.shape
-    o_cols = wo.shape[1]
-
-    def column(f):
-        return full_o.at[:, pl.ds(pl.multiple_of(f * o_cols, LANES), o_cols)]
-
-    def columns(z):
-        return full_o.at[:, pl.ds(pl.multiple_of(z * (2 * o_cols), LANES), 2 * o_cols)]
-
-    greet(p, ("x", "y", "c", "z"))
-    mine = rows.at[p.t]
-    copies = [net.local(wo, column(p.f)), net.local(inp, mine)] + [
-        net.local(w, qkv.at[p.f, :, pl.ds(i * w_cols, w_cols)])
-        for i, w in enumerate((wq, wk, wv))
-    ]
-    net.put(inp, mine, "y", ("rows", "y"))
-    net.put(inp, mine, "c", ("rows", "c0"))
-    def slab(i):
-        at = pl.ds(i * w_cols, w_cols)
-        return lambda z, x: qkv.at[z * 2 + x, :, at]
-
-    flows = [
-        spread_zx(net, f"w{i}", slab(i), w) for i, w in enumerate((wq, wk, wv))
-    ] + [spread_xz(net, "o", lambda z, x: column(z * 2 + x), columns, wo, copies[0])]
-    for i in range(len(p.offs) + 2):
-        for step, _ in flows:
-            step(i)
-        if i == 1:
-            other = rows.at[(1 - p.y) * 2 + p.c]
-            net.got(other, ("rows", "y"))
-            net.put(other, other, "c", ("rows", "c1"))
-    for _, finish in flows:
-        finish()
-    net.got(rows.at[p.y * 2 + 1 - p.c], ("rows", "c0"))
-    net.got(rows.at[(1 - p.y) * 2 + 1 - p.c], ("rows", "c1"))
-    for copy in copies[1:]:
-        copy.wait()
-    net.finish()
-
-
-def first_gather(depth, w_query, w_key, w_value, w_output, inputs, tp):
-    fsdp = 2 * depth
-    w_rows, w_cols = w_query.shape
-    o_rows, o_cols = w_output.shape
-    rows, width = inputs.shape
-    return pl.pallas_call(
-        functools.partial(first_kernel, depth),
-        out_shape=[
-            jax.ShapeDtypeStruct((fsdp, w_rows, 3 * w_cols), BF16),
-            jax.ShapeDtypeStruct((o_rows, fsdp * o_cols), BF16),
-            jax.ShapeDtypeStruct((tp, rows, width), BF16),
-        ],
-        in_specs=[VMEM] * 5,
-        out_specs=[ANY] * 3,
-        scratch_shapes=sems(),
-        compiler_params=comm_params(1, 60),
-        name="first_gather",
-    )(w_query, w_key, w_value, w_output, inputs)
+    return begin, step
 
 
 SITES = {
@@ -346,39 +281,56 @@
             device_id_type=MESH,
         ).wait_recv()
 
-    def z_copy(self, zz):
+    def z_copy(self, zz, up):
+        p = self.place
+        ref = self.ref(zz, 0, 0, 0, None)
+        base = len(NAMES) * p.depth
+        return pltpu.make_async_remote_copy(
+            src_ref=ref,
+            dst_ref=ref,
+            send_sem=self.sends.at[base + (0 if up else p.depth) + zz],
+            recv_sem=self.recvs.at[base + zz],
+            device_id=p.to["up" if up else "down"],
+            device_id_type=MESH,
+        )
+
+    def each_z(self, zz, act):
+        p = self.place
+        pl.when((zz <= p.z) & p.can_up)(lambda: act(True))
+        pl.when((zz >= p.z) & p.can_down)(lambda: act(False))
+
+    def own_along_z(self):
         p = self.place
         base = len(NAMES) * p.depth
-        return pltpu.make_async_remote_copy(
-            src_ref=self.own,
-            dst_ref=self.ref(p.z, 0, 0, 0, None),
-            send_sem=self.sends.at[base + zz],
-            recv_sem=self.recvs.at[base + p.z],
-            device_id=(zz * 2 + p.x, p.t),
-            device_id_type=MESH,
-        )
-
-    def send_z(self):
-        for zz in self.place.near[1:]:
-            self.z_copy(zz).start()
+
+        def start(up):
+            pltpu.make_async_remote_copy(
+                src_ref=self.own,
+                dst_ref=self.ref(p.z, 0, 0, 0, None),
+                send_sem=self.sends.at[base + (0 if up else p.depth) + p.z],
+                recv_sem=self.recvs.at[base + p.z],
+                device_id=p.to["up" if up else "down"],
+                device_id_type=MESH,
+            ).start()
+
+        self.each_z(p.z, start)
+
+    def take_z(self, zz):
+        self.z_copy(zz, True).wait_recv()
+
+    def along_z(self, zz, near_too=True):
+        p = self.place
+        if near_too:
+            self.take_z(zz)
+        else:
+            pl.when((zz != p.z + 1) & (zz != p.z - 1))(lambda: self.take_z(zz))
+        self.each_z(zz, lambda up: self.z_copy(zz, up).start())
 
     def first(self, zz, mine=False):
-        p = self.place
         whole, part_a, part_b = None, None, None
         if mine:
             whole = self.own
             part_a, part_b = whole.at[pl.ds(0, self.half)], whole.at[pl.ds(self.half, self.half)]
-        else:
-            ref = self.ref(zz, 0, 0, 0, None)
-            at = len(NAMES) * p.depth + zz
-            pltpu.make_async_remote_copy(
-                src_ref=ref,
-                dst_ref=ref,
-                send_sem=self.sends.at[at],
-                recv_sem=self.recvs.at[at],
-                device_id=(zz * 2 + p.x, p.t),
-                device_id_type=MESH,
-            ).wait_recv()
         self.copy("x1", zz, part_a).start()
         self.copy("y1", zz, part_b).start()
         self.copy("x3", zz, part_b).start()
@@ -404,20 +356,198 @@
         for site in ("c0", "cx", "cy", "cxy"):
             self.take(site, zz)
 
-    def finish(self):
-        for zz in range(self.place.depth):
+    def finish(self, zs, z_zs):
+        for zz in zs:
             for site in NAMES:
                 self.copy(site, zz).wait_send()
-            pl.when(self.place.z != zz)(self.z_copy(zz).wait_send)
+        for zz in z_zs:
+            self.each_z(zz, lambda up, zz=zz: self.z_copy(zz, up).wait_send())
 
 
 def plane_sems(depth):
-    return [pltpu.SemaphoreType.DMA(((len(NAMES) + 1) * depth,))] * 2
+    return [pltpu.SemaphoreType.DMA(((len(NAMES) + 2) * depth,))] * 2
+
+
+def same_document(seg_row):
+    row = seg_row[...]
+    column = jnp.transpose(jnp.broadcast_to(row, (LANES, row.shape[1])))[:, 0:1]
+    return column == row
+
+
+def first_kernel(
+    depth, wq, wk, wv, wo, inp, og, gain, seg_row,
+    qkv_hbm, o_hbm, rows_hbm, act_hbm, proj_hbm, att_hbm, part_hbm, grad_all,
+    weights, full_o, rows, act, proj, att, part, og_send, og_recv, send, recv, local,
+):
+    p = Place(depth)
+    net = Net(p, send, recv, local)
+    grads = Plane(p, grad_all, og, og_send, og_recv)
+    w_rows, w_cols = wq.shape
+    o_cols = wo.shape[1]
+    count, width = inp.shape
+    fsdp, heads = 2 * depth, w_cols // HEAD
+
+    def column(f):
+        return full_o.at[:, pl.ds(pl.multiple_of(f * o_cols, LANES), o_cols)]
+
+    def columns(z):
+        return full_o.at[:, pl.ds(pl.multiple_of(z * (2 * o_cols), LANES), 2 * o_cols)]
+
+    def slab(i):
+        return lambda z, x: weights.at[i, z * 2 + x]
+
+    greet(p, ("x", "y", "c", "z"))
+    mine = rows.at[p.t]
+    net.put(inp, mine, "y", ("rows", "y"))
+    net.put(inp, mine, "c", ("rows", "c0"))
+    placed = net.local(wo, column(p.f))
+    owns = [net.local(inp, mine)]
+    owns += [net.local(w, weights.at[i, p.f]) for i, w in enumerate((wq, wk, wv))]
+    kept = net.local(og, grads.ref(p.z, 0, 0, 0, None))
+    flows = [spread_zx(net, f"w{i}", slab(i), w) for i, w in enumerate((wq, wk, wv))]
+    o_begin, o_step = spread_xz(net, "o", lambda z, x: column(z * 2 + x), columns, wo, placed)
+    steps = len(p.offs)
+
+    def norm():
+        other = rows.at[(1 - p.y) * 2 + p.c]
+        net.got(other, ("rows", "y"))
+        net.put(other, other, "c", ("rows", "c1"))
+        net.got(rows.at[p.y * 2 + 1 - p.c], ("rows", "c0"))
+        net.got(rows.at[(1 - p.y) * 2 + 1 - p.c], ("rows", "c1"))
+        owns[0].wait()
+        for t in range(rows.shape[0]):
+
+            def body(i, carry):
+                at = pl.ds(pl.multiple_of(i * 16, 16), 16)
+                values = rows[t, at, :].astype(F32)
+                inverse = lax.rsqrt(jnp.mean(values * values, axis=-1, keepdims=True) + EPSILON)
+                to = pl.ds(pl.multiple_of(t * count + i * 16, 16), 16)
+                act[to, :] = (values * inverse * gain[...]).astype(BF16)
+                return carry
+
+            lax.fori_loop(0, count // 16, body, 0)
+
+    saves = []
+
+    def rows_in():
+        norm()
+        saves.append(net.local(rows, rows_hbm))
+        saves.append(net.local(act, act_hbm))
+
+    def project_with(i):
+        owns[1 + i].wait()
+        flows[i][1]()
+        saves.append(net.local(weights.at[i], qkv_hbm.at[i]))
+        wide = 256
+
+        def project(k, carry):
+            at = pl.ds(pl.multiple_of(k * wide, wide), wide)
+            to = pl.ds(pl.multiple_of(i * w_cols + k * wide, wide), wide)
+            matrix = weights[i, :, :, at].reshape(width, wide)
+            proj[:, to] = jnp.dot(act[...], matrix, preferred_element_type=F32).astype(BF16)
+            return carry
+
+        lax.fori_loop(0, w_cols // wide, project, 0)
+
+    scale = 1.0 / math.sqrt(HEAD)
+
+    def head(h):
+        if h == 0:
+            saves.append(net.local(proj, proj_hbm))
+        same = same_document(seg_row)
+        query, keys, values = [
+            proj[:, i * w_cols + h * HEAD : i * w_cols + (h + 1) * HEAD] for i in range(3)
+        ]
+        scores = lax.dot_general(query, keys, CONTRACT_LAST, preferred_element_type=F32) * scale
+        scores = jnp.where(same, scores, -1e30)
+        expo = jnp.exp(scores - jnp.max(scores, axis=-1, keepdims=True))
+        probs = (expo / jnp.sum(expo, axis=-1, keepdims=True)).astype(BF16)
+        att[:, h * HEAD : (h + 1) * HEAD] = jnp.dot(
+            probs, values, preferred_element_type=F32
+        ).astype(BF16)
+
+    def out_rows(k, carry):
+        at = pl.ds(pl.multiple_of(k * 256, 256), 256)
+        part[:, at] = jnp.dot(att[...], full_o[:, at], preferred_element_type=F32).astype(BF16)
+        return carry
+
+    def branch():
+        saves.append(net.local(full_o, o_hbm))
+        saves.append(net.local(att, att_hbm))
+        lax.fori_loop(0, width // 256, out_rows, 0)
+        saves.append(net.local(part, part_hbm))
+
+    (q_step, _), (k_step, _), (v_step, _) = flows
+
+    def g_first():
+        grads.first(p.z, True)
+
+    if depth == 4 and heads == 4:
+        perform(
+            (v_step, 0), (o_begin,), (k_step, 0), (q_step, 0), (o_step, 0), (q_step, 1),
+            (q_step, 2), (v_step, 1), (v_step, 2), (q_step, 3), (k_step, 1), (k_step, 2),
+            (v_step, 3), (k_step, 3), (q_step, 4), (o_step, 1), (v_step, 4), (q_step, 5),
+            (k_step, 4), (o_step, 2), (q_step, 6), (rows_in,), (k_step, 5), (v_step, 5),
+            (v_step, 6), (project_with, 0), (k_step, 6), (g_first,), (o_step, 3), (o_step, 4),
+            (project_with, 1), (grads.own_along_z,), (project_with, 2), (head, 0), (grads.second, p.z),
+            (head, 1), (head, 2), (grads.third, p.z), (o_step, 5), (head, 3), (o_step, 6), (branch,),
+            (grads.arrived, p.z),
+        )
+    else:
+        perform((o_begin,), (g_first,), *every(steps, q_step, k_step, v_step, o_step), (rows_in,))
+        perform((grads.second, p.z), (grads.third, p.z), *every(3, project_with))
+        perform(*every(heads, head), (branch,), (grads.own_along_z,), (grads.arrived, p.z))
+    pl.when(p.can_down)(lambda: grads.take_z(p.z - 1))
+    pl.when(p.can_up)(lambda: grads.take_z(p.z + 1))
+    kept.wait()
+    for copy in saves:
+        copy.wait()
+    grads.finish([p.z], [p.z])
+    net.finish()
+
+
+def first_gather(depth, w_query, w_key, w_value, w_output, inputs, out_grad, gain, segments, tp):
+    fsdp = 2 * depth
+    w_rows, w_cols = w_query.shape
+    o_rows, o_cols = w_output.shape
+    rows, width = inputs.shape
+    seq = tp * rows
+    shape = jax.ShapeDtypeStruct
+    return pl.pallas_call(
+        functools.partial(first_kernel, depth),
+        out_shape=[
+            shape((3, fsdp, w_rows, w_cols), BF16),
+            shape((o_rows, fsdp * o_cols), BF16),
+            shape((tp, rows, width), BF16),
+            shape((seq, width), BF16),
+            shape((seq, 3 * w_cols), BF16),
+            shape((seq, w_cols), BF16),
+            shape((seq, width), BF16),
+            shape((fsdp * tp, rows, width), BF16),
+        ],
+        in_specs=[VMEM] * 8,
+        out_specs=[ANY] * 8,
+        scratch_shapes=[
+            pltpu.VMEM((3, fsdp, w_rows, w_cols), BF16),
+            pltpu.VMEM((o_rows, fsdp * o_cols), BF16),
+            pltpu.VMEM((tp, rows, width), BF16),
+            pltpu.VMEM((seq, width), BF16),
+            pltpu.VMEM((seq, 3 * w_cols), BF16),
+            pltpu.VMEM((seq, w_cols), BF16),
+            pltpu.VMEM((seq, width), BF16),
+        ]
+        + plane_sems(depth)
+        + sems(),
+        compiler_params=comm_params(1, 60),
+        name="first_gather",
+    )(
+        w_query, w_key, w_value, w_output, inputs, out_grad, gain[None, :], segments[None, :],
+    )
 
 
 def moe_kernel(
     depth, capacity, experts, blocks,
-    part, inp, og, gain, router, mask, rank, gate_hbm, up_hbm, down_hbm,
+    part, inp, og, gain, router, mask, rank, gate_hbm, up_hbm, down_hbm, grad_in_hbm,
     resid, gates_out, act_all, grad_all, out_hbm, back_hbm, x_hbm, g_hbm, hid_hbm, gl_hbm, ul_hbm,
     acc, rc, ry, own, w_gate, w_up, w_down, act_in, grad_in, x_rows, g_rows, tails, hid, gl, ul,
     o_keep, r_keep, out, back,
@@ -434,60 +564,52 @@
     part_in = net.local(part.at[:, p.c], acc)
     acts = Plane(p, act_all, own, act_send, act_recv)
     grads = Plane(p, grad_all, og, og_send, og_recv)
-    barrier = pltpu.get_barrier_semaphore()
-    peers = [p.to["x"], p.to["y"], p.to["c"]] + [(zz * 2 + p.x, p.t) for zz in p.near[1:]]
-    for peer in peers:
-        pl.semaphore_signal(barrier, inc=1, device_id=peer, device_id_type=MESH)
-    pl.semaphore_wait(barrier, len(peers))
+    greet(p, ("x", "y", "c", "z"))
 
     net.put(part.at[:, 1 - p.c], rc, "c", ("rc",))
-    og_kept = net.local(og, grads.ref(p.z, 0, 0, 0, None))
-    grads.send_z()
-    part_in.wait()
-    net.got(rc, ("rc",))
     far = 1 - p.y
-    add_rows(acc.at[far], rc.at[far], rows)
-    net.put(acc.at[far], ry, "y", ("ry",))
-    grads.first(p.z, True)
-    add_rows(acc.at[p.y], rc.at[p.y], rows)
-    net.got(ry, ("ry",))
-
-    def norm(i, carry):
-        at = pl.ds(pl.multiple_of(i * 16, 16), 16)
-        branch = acc[p.y, at, :].astype(F32) + ry[at, :].astype(F32)
-        values = inp[at, :].astype(F32) + branch
-        resid[at, :] = values
-        inverse = lax.rsqrt(jnp.mean(values * values, axis=-1, keepdims=True) + EPSILON)
-        own[at, pl.ds(0, width)] = (values * inverse * gain[...]).astype(BF16)
-        return carry
-
-    lax.fori_loop(0, rows // 16, norm, 0)
-    logits = jnp.dot(own[:, pl.ds(0, width)], router[...], preferred_element_type=F32)
-    chosen = mask[...] > 0.0
-    peak = jnp.max(jnp.where(chosen, logits, -1e30), axis=1, keepdims=True)
-    expo = jnp.where(chosen, jnp.exp(jnp.minimum(logits - peak, 0.0)), 0.0)
-    lane = lax.broadcasted_iota(jnp.int32, expo.shape, 1)
-    total = jnp.sum(jnp.where(lane < experts, expo, 0.0), axis=1, keepdims=True)
-    gates = expo / total
-    gates_out[...] = gates
-    high = gates.astype(BF16).astype(F32)
-    tail = jnp.where(lane < experts, high, jnp.where(lane < 2 * experts, gates - high, rank[...]))
-    own[:, pl.ds(width, LANES)] = tail.astype(BF16)
-    acts.send_z()
-    acts.first(p.z, True)
-    act_kept = net.local(own, acts.ref(p.z, 0, 0, 0, None))
-    grads.second(p.z)
-    acts.second(p.z)
-    grads.first(p.near[1])
-    grads.third(p.z)
-    acts.third(p.z)
-    acts.first(p.near[1])
-    grads.arrived(p.z)
-    acts.arrived(p.z)
-    og_kept.wait()
-    act_kept.wait()
-    for copy in weights:
-        copy.wait()
+
+    def along_y():
+        part_in.wait()
+        net.got(rc, ("rc",))
+        add_rows(acc.at[far], rc.at[far], rows)
+        net.put(acc.at[far], ry, "y", ("ry",))
+        add_rows(acc.at[p.y], rc.at[p.y], rows)
+
+    kept = []
+
+    def norm():
+        net.got(ry, ("ry",))
+
+        def body(i, carry):
+            at = pl.ds(pl.multiple_of(i * 16, 16), 16)
+            branch = acc[p.y, at, :].astype(F32) + ry[at, :].astype(F32)
+            values = inp[at, :].astype(F32) + branch
+            resid[at, :] = values
+            inverse = lax.rsqrt(jnp.mean(values * values, axis=-1, keepdims=True) + EPSILON)
+            own[at, pl.ds(0, width)] = (values * inverse * gain[...]).astype(BF16)
+            return carry
+
+        lax.fori_loop(0, rows // 16, body, 0)
+        twice = jnp.concatenate(
+            [router[...]] * 2 + [jnp.zeros((LANES - 2 * experts, width), BF16)], axis=0
+        )
+        logits = lax.dot_general(
+            own[:, pl.ds(0, width)], twice, CONTRACT_LAST, preferred_element_type=F32
+        )
+        chosen = mask[...] > 0.0
+        peak = jnp.max(jnp.where(chosen, logits, -1e30), axis=1, keepdims=True)
+        expo = jnp.where(chosen, jnp.exp(jnp.minimum(logits - peak, 0.0)), 0.0)
+        lane = lax.broadcasted_iota(jnp.int32, expo.shape, 1)
+        total = jnp.sum(jnp.where(lane < experts, expo, 0.0), axis=1, keepdims=True)
+        gates = expo / total
+        gates_out[...] = gates
+        high = gates.astype(BF16).astype(F32)
+        tail = jnp.where(
+            lane < experts, high, jnp.where(lane < 2 * experts, gates - high, rank[...])
+        )
+        own[:, pl.ds(width, LANES)] = tail.astype(BF16)
+        kept.append(net.local(own, acts.ref(p.z, 0, 0, 0, None)))
 
     first_expert = p.f * local_experts
     tp_lane = p.t * experts + first_expert
@@ -605,56 +727,80 @@
         lax.fori_loop(0, blocks, combine, 0)
         for k in (5, 6):
             save(zz, j, k).start()
-
-    for copy in loads(p.z, 0):
-        copy.start()
+        serve(5)
+
+    def load(i):
+        if i == 0:
+            kept[0].wait()
+            for copy in weights:
+                copy.wait()
+        for copy in loads(p.near[i], 0):
+            copy.start()
+
+    near = p.near
+    g1, g2, g3 = grads.first, grads.second, grads.third
+    a1, a2, a3 = acts.first, acts.second, acts.third
+    if depth == 4:
+        perform(
+            (grads.along_z, near[1], False), (along_y,), (g1, near[1]),
+            (grads.along_z, near[2], False), (norm,), (acts.own_along_z,), (a1, p.z, True),
+            (acts.along_z, near[1]), (a2, p.z), (g2, near[1]), (a1, near[1]),
+            (acts.along_z, near[2]), (a3, p.z), (a1, near[2]), (acts.arrived, p.z), (load, 0),
+        )
+        service = {
+            (0, 0, 0): [(g3, near[1])],
+            (0, 0, 1): [(acts.along_z, near[3])],
+            (0, 0, 3): [(a2, near[1]), (g1, near[2])],
+            (0, 1, 1): [(grads.along_z, near[3], False)],
+            (0, 1, 2): [(a3, near[1]), (a2, near[2])],
+            (0, 1, 4): [(acts.arrived, near[1])],
+            (0, 1, 5): [(g2, near[2]), (grads.arrived, near[1]), (load, 1)],
+            (1, 0, 4): [(a1, near[3])],
+            (1, 0, 5): [(g3, near[2])],
+            (1, 1, 1): [(grads.arrived, near[2])],
+            (1, 1, 2): [(a3, near[2]), (a2, near[3])],
+            (1, 1, 4): [(acts.arrived, near[2]), (load, 2)],
+            (2, 0, 0): [(g1, near[3])],
+            (2, 0, 1): [(a3, near[3])],
+            (2, 0, 5): [(g2, near[3])],
+            (2, 1, 3): [(g3, near[3])],
+            (2, 1, 5): [(acts.arrived, near[3]), (grads.arrived, near[3]), (load, 3)],
+        }
+    else:
+        perform((along_y,), (norm,), (acts.own_along_z,))
+        for i, zz in enumerate(near):
+            if i:
+                perform((acts.along_z, zz), (grads.along_z, zz, False))
+                perform((g1, zz), (g2, zz), (g3, zz), (grads.arrived, zz))
+            perform((a1, zz, i == 0), (a2, zz), (a3, zz), (acts.arrived, zz))
+        load(0)
+        service = {(g, 1, 4): [(load, g + 1)] for g in range(depth - 1)}
 
     def group(g, carry):
-        zz, later, last = p.nearest(g), p.nearest(g + 1), p.nearest(g + 2)
-        more, still = g + 1 < depth, g + 2 < depth
+        zz = p.nearest(g)
         for copy in loads(zz, 1):
             copy.start()
 
-        def serve_one(k):
-            if k == 0:
-                pl.when(more)(lambda: grads.second(later))
-            if k == 1:
-                pl.when(more)(lambda: acts.second(later))
-            if k == 2:
-                pl.when(still)(lambda: grads.first(last))
-            if k == 4:
-                pl.when(more)(lambda: grads.third(later))
-
-        work(zz, 0, g > 0, serve_one)
-
-        def serve_two(k):
-            if k == 0:
-                pl.when(more)(lambda: acts.third(later))
-            if k == 1:
-                pl.when(still)(lambda: acts.first(last))
-            if k == 4:
-
-                def ready():
-                    grads.arrived(later)
-                    acts.arrived(later)
-                    for copy in loads(later, 0):
-                        copy.start()
-
-                pl.when(more)(ready)
-
-        work(zz, 1, None, serve_two)
+        def serve(j, k):
+            for (at, half, place), steps in service.items():
+                if (half, place) == (j, k):
+                    pl.when(g == at)(functools.partial(perform, *steps))
+
+        work(zz, 0, g > 0, functools.partial(serve, 0))
+        work(zz, 1, None, functools.partial(serve, 1))
         return carry
 
     lax.fori_loop(0, depth, group, 0)
     for k in range(7):
         save(0, 1, k).wait()
-    acts.finish()
-    grads.finish()
+    acts.finish(range(depth), range(depth))
+    grads.finish(near[1:], near[1:])
     net.finish()
 
 
 def run_moe(
-    depth, capacity, experts, part, inputs, out_grad, gain, router, mask, rank, w_gate, w_up, w_down
+    depth, capacity, experts, part, inputs, out_grad, gain, router, mask, rank, w_gate, w_up, w_down,
+    grad_all,
 ):
     tp, rows, width = part.shape
     wide = width + LANES
@@ -677,8 +823,9 @@
             shape((count, rows, wide), BF16),
         ]
         + kept,
-        in_specs=[ANY] + [VMEM] * 6 + [ANY] * 3,
+        in_specs=[ANY] + [VMEM] * 6 + [ANY] * 4,
         out_specs=[VMEM] * 2 + [ANY] * 9,
+        input_output_aliases={10: 3},
         scratch_shapes=[
             pltpu.VMEM((2, rows, width), BF16),
             pltpu.VMEM((2, rows, width), BF16),
@@ -707,17 +854,17 @@
         name="moe",
     )(
         part.reshape(tp // 2, 2, rows, width), inputs, out_grad, gain[None, :], router, mask, rank,
-        w_gate, w_up, w_down,
-    )
-
-
-def chain_z(net, name, zz, acc, inbox, rows):
+        w_gate, w_up, w_down, grad_all,
+    )
+
+
+def chain_z(net, name, zz, acc, inbox, rows, add=None):
     p = net.place
     extra = p.depth
 
     def take(slot):
         net.got(inbox.at[slot], (name, "at", extra + 1, slot))
-        add_rows(acc, inbox.at[slot], rows)
+        (add or add_rows)(acc, inbox.at[slot], rows)
 
     pl.when((zz >= p.z) & p.can_down)(lambda: take(jnp.where(zz == p.z, extra, zz)))
     pl.when((zz <= p.z) & p.can_up)(lambda: take(zz))
@@ -726,53 +873,104 @@
     net.put(acc, inbox.at[zz], "down", (name, "at", extra + 1, zz), zz < p.z)
 
 
-def reduce_xy(net, name, fill, acc, ya, xa, xb, yb, inbox):
-    p = net.place
-    x, y, depth = p.x, p.y, p.depth
-    rows = acc.shape[3]
-    half = rows // 2
-    a, b = pl.ds(0, half), pl.ds(half, half)
-
-    def key(what, zz):
-        return (name + what, "at", depth, zz)
-
-    def step(i):
-        if i < depth:
-            zz = p.far[i]
-            fill(i, zz)
-            net.put(acc.at[zz, :, 1 - y, a], ya.at[zz], "y", key("ya", zz))
-            net.put(acc.at[zz, 1 - x, :, b], xb.at[zz], "x", key("xb", zz))
-        if 0 <= i - 1 < depth:
-            zz = p.far[i - 1]
-            net.got(ya.at[zz], key("ya", zz))
-            add_rows(acc.at[zz, 1 - x, y, a], ya.at[zz, 1 - x], half)
-            net.put(acc.at[zz, 1 - x, y, a], xa.at[zz], "x", key("xa", zz))
-            net.got(xb.at[zz], key("xb", zz))
-            add_rows(acc.at[zz, x, 1 - y, b], xb.at[zz, 1 - y], half)
-            net.put(acc.at[zz, x, 1 - y, b], yb.at[zz], "y", key("yb", zz))
-            add_rows(acc.at[zz, x, y, a], ya.at[zz, x], half)
-            add_rows(acc.at[zz, x, y, b], xb.at[zz, y], half)
-        if 0 <= i - 2 < depth:
-            zz = p.far[i - 2]
-            net.got(xa.at[zz], key("xa", zz))
-            add_rows(acc.at[zz, x, y, a], xa.at[zz], half)
-            net.got(yb.at[zz], key("yb", zz))
-            add_rows(acc.at[zz, x, y, b], yb.at[zz], half)
-            chain_z(net, name + "z", zz, acc.at[zz, x, y], inbox, rows)
-
-    return step
-
-
-def reduce_scratch(depth, rows, wide):
-    half = rows // 2
+class Reduce:
+    def __init__(self, net, name, fill, acc, ya, xa, xb, yb, inbox, z_inbox, xc, yc):
+        self.net, self.name, self.fill, self.acc = net, name, fill, acc
+        self.ya, self.xa, self.xb, self.yb = ya, xa, xb, yb
+        self.inbox, self.z_inbox, self.xc, self.yc = inbox, z_inbox, xc, yc
+        self.rows_a, self.rows_b, self.rows_c = ya.shape[2], xb.shape[2], yc.shape[0]
+        self.rows_ab = self.rows_a + self.rows_b
+        self.a, self.b = pl.ds(0, self.rows_a), pl.ds(self.rows_a, self.rows_b)
+        self.ab, self.c = pl.ds(0, self.rows_ab), pl.ds(self.rows_ab, self.rows_c)
+
+    def key(self, what, zz):
+        return (self.name + what, "at", self.net.place.depth, zz)
+
+    def one(self, i):
+        p, net, acc = self.net.place, self.net, self.acc
+        zz = p.far[i]
+        self.fill(i, zz)
+        net.put(acc.at[zz, :, 1 - p.y, self.a], self.ya.at[zz], "y", self.key("ya", zz))
+        net.put(acc.at[zz, 1 - p.x, :, self.b], self.xb.at[zz], "x", self.key("xb", zz))
+
+    def two(self, i):
+        p, net, acc = self.net.place, self.net, self.acc
+        x, y, zz = p.x, p.y, p.far[i]
+        net.got(self.xb.at[zz], self.key("xb", zz))
+        add_rows(acc.at[zz, x, 1 - y, self.b], self.xb.at[zz, 1 - y], self.rows_b)
+        net.put(acc.at[zz, x, 1 - y, self.b], self.yb.at[zz], "y", self.key("yb", zz))
+        net.got(self.ya.at[zz], self.key("ya", zz))
+        add_rows(acc.at[zz, 1 - x, y, self.a], self.ya.at[zz, 1 - x], self.rows_a)
+        net.put(acc.at[zz, 1 - x, y, self.a], self.xa.at[zz], "x", self.key("xa", zz))
+        add_rows(acc.at[zz, x, y, self.a], self.ya.at[zz, x], self.rows_a)
+        add_rows(acc.at[zz, x, y, self.b], self.xb.at[zz, y], self.rows_b)
+
+    def three(self, i):
+        p, net, acc = self.net.place, self.net, self.acc
+        x, y, zz = p.x, p.y, p.far[i]
+        net.got(self.xa.at[zz], self.key("xa", zz))
+        add_rows(acc.at[zz, x, y, self.a], self.xa.at[zz], self.rows_a)
+        net.got(self.yb.at[zz], self.key("yb", zz))
+        add_rows(acc.at[zz, x, y, self.b], self.yb.at[zz], self.rows_b)
+        chain_z(net, self.name + "z", zz, acc.at[zz, x, y, self.ab], self.inbox, self.rows_ab)
+
+    def along_z(self, i):
+        p = self.net.place
+        zz = p.far[i]
+
+        def add(dst, src, rows):
+            for xx in range(2):
+                for yy in range(2):
+                    add_rows(dst.at[xx, yy], src.at[xx, yy], rows)
+
+        chain_z(
+            self.net, self.name + "c", zz, self.acc.at[zz, :, :, self.c], self.z_inbox, self.rows_c, add
+        )
+
+    def then_x(self):
+        p, net = self.net.place, self.net
+        net.put(self.acc.at[p.z, 1 - p.x, :, self.c], self.xc, "x", (self.name + "xc",))
+
+    def then_y(self):
+        p, net, x, y = self.net.place, self.net, self.net.place.x, self.net.place.y
+        net.got(self.xc, (self.name + "xc",))
+        add_rows(self.acc.at[p.z, x, 1 - y, self.c], self.xc.at[1 - y], self.rows_c)
+        net.put(self.acc.at[p.z, x, 1 - y, self.c], self.yc, "y", (self.name + "yc",))
+        add_rows(self.acc.at[p.z, x, y, self.c], self.xc.at[y], self.rows_c)
+
+    def end(self):
+        p, net = self.net.place, self.net
+        net.got(self.yc, (self.name + "yc",))
+        add_rows(self.acc.at[p.z, p.x, p.y, self.c], self.yc, self.rows_c)
+
+
+def reduce_scratch(depth, rows, wide, parts):
+    a, b = parts
+    c = rows - a - b
     return [
         pltpu.VMEM((depth, 2, 2, rows, wide), BF16),
-        pltpu.VMEM((depth, 2, half, wide), BF16),
-        pltpu.VMEM((depth, half, wide), BF16),
-        pltpu.VMEM((depth, 2, half, wide), BF16),
-        pltpu.VMEM((depth, half, wide), BF16),
-        pltpu.VMEM((depth + 1, rows, wide), BF16),
+        pltpu.VMEM((depth, 2, a, wide), BF16),
+        pltpu.VMEM((depth, a, wide), BF16),
+        pltpu.VMEM((depth, 2, b, wide), BF16),
+        pltpu.VMEM((depth, b, wide), BF16),
+        pltpu.VMEM((depth + 1, a + b, wide), BF16),
+        pltpu.VMEM((depth + 1, 2, 2, c, wide), BF16),
+        pltpu.VMEM((2, c, wide), BF16),
+        pltpu.VMEM((c, wide), BF16),
     ]
+
+
+def tile_rows(rows, share):
+    return max(16, int(rows * share) // 16 * 16)
+
+
+def perform(*steps):
+    for function, *args in steps:
+        function(*args)
+
+
+def every(depth, *functions):
+    return [(function, i) for function in functions for i in range(depth)]
 
 
 def widen(dst, src, rows):
@@ -787,7 +985,7 @@
 def back_kernel(
     depth, part, out_part, x_rows, g_rows, hid, gate_low, up_low,
     total, out_other, w_gate_grad, w_up_grad, w_down_grad,
-    acc, ya, xa, xb, yb, inbox, rc, big, left, right, found, found_down,
+    acc, ya, xa, xb, yb, inbox, z_inbox, xc, yc, rc, big, left, right, found, found_down,
     send, recv, local, load_sems, save_sems,
 ):
     p = Place(depth)
@@ -835,7 +1033,7 @@
                 for j, ref in enumerate((left, right)):
                     found[j, at, :] = lax.dot_general(
                         tile, ref[slot], CONTRACT_FIRST, preferred_element_type=F32
-                    )
+                    ).astype(BF16)
                 return carry
 
             lax.fori_loop(0, width // wide, body, 0)
@@ -846,7 +1044,7 @@
                 at = pl.ds(pl.multiple_of(i * wide, wide), wide)
                 found_down[:, at] = lax.dot_general(
                     left[slot], big[slot, :, at], CONTRACT_FIRST, preferred_element_type=F32
-                )
+                ).astype(BF16)
                 return carry
 
             lax.fori_loop(0, width // wide, body, 0)
@@ -860,15 +1058,10 @@
     for i in range(depth):
         zz = p.far[i]
         fills.append(net.local(part.at[zz, :, :, c], acc.at[zz]))
-    for u in range(2):
-        for copy in loads(u):
-            copy.start()
     greet(p, ("x", "y", "c", "z"))
     for i in range(depth):
         zz = p.far[i]
         net.put(part.at[zz, :, :, 1 - c], rc.at[zz], "c", ("c", "at", depth, zz))
-    for zz in range(depth):
-        net.put(out_part.at[zz, :, :, 1 - c], out_other.at[zz], "c", ("oc", "at", depth, zz))
 
     def fill(i, zz):
         fills[i].wait()
@@ -877,17 +1070,25 @@
             for yy in range(2):
                 add_rows(acc.at[zz, xx, yy], rc.at[zz, xx, yy], rows)
 
-    step = reduce_xy(net, "b", fill, acc, ya, xa, xb, yb, inbox)
-    u = 0
-    for i in range(depth + 2):
-        step(i)
-        for _ in range(2 if i < depth - 1 else 1):
-            if u < units:
-                unit(u)
-                u += 1
-    while u < units:
-        unit(u)
-        u += 1
+    flow = Reduce(net, "b", fill, acc, ya, xa, xb, yb, inbox, z_inbox, xc, yc)
+    def begin():
+        for v in range(2):
+            for copy in loads(v):
+                copy.start()
+        for zz in range(depth):
+            net.put(out_part.at[zz, :, :, 1 - c], out_other.at[zz], "c", ("oc", "at", depth, zz))
+
+    one, two, three, along_z = flow.one, flow.two, flow.three, flow.along_z
+    if depth == 4 and units == 8:
+        perform(
+            (one, 0), (along_z, 0), (one, 1), (begin,), (one, 2), (unit, 0), (along_z, 1),
+            (along_z, 2), (two, 0), (one, 3), (unit, 1), (unit, 2), (two, 1), (unit, 3), (two, 2),
+            (three, 0), (unit, 4), (along_z, 3), (flow.then_x,), (unit, 5), (three, 1),
+            (three, 2), (two, 3), (unit, 6), (flow.then_y,), (unit, 7), (flow.end,), (three, 3),
+        )
+    else:
+        perform(*every(depth, one), (begin,), *every(depth, two, three, along_z))
+        perform((flow.then_x,), (flow.then_y,), (flow.end,), *every(units, unit))
     for k in (units - 2, units - 1):
         for copy in saves(k):
             copy.wait()
@@ -913,20 +1114,20 @@
         out_shape=[
             shape((rows, wide), F32),
             shape((depth, 2, 2, rows, width), BF16),
-            shape((local_experts, width, hidden), F32),
-            shape((local_experts, width, hidden), F32),
-            shape((local_experts, hidden, width), F32),
+            shape((local_experts, width, hidden), BF16),
+            shape((local_experts, width, hidden), BF16),
+            shape((local_experts, hidden, width), BF16),
         ],
         in_specs=[ANY] * 7,
         out_specs=[VMEM] + [ANY] * 4,
-        scratch_shapes=reduce_scratch(depth, rows, wide)
+        scratch_shapes=reduce_scratch(depth, rows, wide, [tile_rows(rows, 0.375)] * 2)
         + [
             pltpu.VMEM((depth, 2, 2, rows, wide), BF16),
             pltpu.VMEM((2, slots, width), BF16),
             pltpu.VMEM((2, slots, hidden), BF16),
             pltpu.VMEM((2, slots, hidden), BF16),
-            pltpu.VMEM((2, width, hidden), F32),
-            pltpu.VMEM((hidden, width), F32),
+            pltpu.VMEM((2, width, hidden), BF16),
+            pltpu.VMEM((hidden, width), BF16),
         ]
         + sems()
         + [pltpu.SemaphoreType.DMA((2, 3)), pltpu.SemaphoreType.DMA((3,))],
@@ -940,10 +1141,10 @@
 
 
 def attend_back_kernel(
-    depth, mine, act_hbm, wqkv_hbm, wo_hbm, qkv_hbm, att_hbm, seg_col, seg_row, out_part, out_other,
-    qkv_part, act_grad, o_sum, out_sum,
-    acc, ya, xa, xb, yb, inbox, other, bg, act, wqkv, wo, qkv, att, ag, low, o_acc, o_inbox, o_rx,
-    send, recv, local, other_sems,
+    depth, mine, act_hbm, wqkv_hbm, wo_hbm, qkv_hbm, att_hbm, whole_hbm, seg_row, gain, out_part, out_other,
+    qkv_part, whole_part, gain_part, o_sum, o_rest, out_sum,
+    acc, ya, xa, xb, yb, inbox, z_inbox, xc, yc, other, bg, act, wqkv, wo, qkv, att, ag, low, o_acc, o_inbox, o_rx,
+    whole, act_grad, send, recv, local, other_sems,
 ):
     p = Place(depth)
     net = Net(p, send, recv, local)
@@ -952,7 +1153,7 @@
     seq = act.shape[0]
     cols = wo.shape[0]
     heads = cols // HEAD
-    o_cols = o_sum.shape[1]
+    o_rows, o_cols = o_sum.shape
 
     def block(t):
         return bg.at[pl.ds(pl.multiple_of(t * rows, rows), rows)]
@@ -963,6 +1164,7 @@
     load_qkv = net.local(qkv_hbm, qkv)
     load_act = net.local(act_hbm, act)
     load_w = net.local(wqkv_hbm, wqkv)
+    load_whole = net.local(whole_hbm, whole)
     greet(p, ("x", "y", "c", "z"))
     own.wait()
     net.put(block(p.t), block(p.t), "y", ("bg", "y"))
@@ -989,46 +1191,52 @@
             for copy in load_other(i + 2):
                 copy.start()
 
-    out_step = reduce_xy(net, "out", fill, acc, ya, xa, xb, yb, inbox)
+    flow = Reduce(net, "out", fill, acc, ya, xa, xb, yb, inbox, z_inbox, xc, yc)
 
     def o_pair(z):
         return o_acc.at[:, pl.ds(pl.multiple_of(z * (2 * o_cols), LANES), 2 * o_cols)]
 
     def o_step(i):
         if i < depth:
-            chain_z(net, "oz", p.far[i], o_pair(p.far[i]), o_inbox, cols)
-        if i == depth - 1:
-            theirs = pl.ds(pl.multiple_of((p.z * 2 + 1 - x) * o_cols, LANES), o_cols)
-            net.put(o_acc.at[:, theirs], o_rx, "x", ("ox",))
-
-    out_step(0)
-    far = block((1 - y) * 2 + c)
-    net.got(far, ("bg", "y"))
-    net.put(far, far, "c", ("bg", "c1"))
-    net.got(block(y * 2 + 1 - c), ("bg", "c0"))
-    net.got(block((1 - y) * 2 + 1 - c), ("bg", "c1"))
-    load_wo.wait()
-    ag[...] = lax.dot_general(
-        bg[...], wo[...], CONTRACT_LAST, preferred_element_type=F32
-    ).astype(BF16)
-    out_step(1)
-    load_att.wait()
+            chain_z(net, "oz", p.far[i], o_pair(p.far[i]), o_inbox, o_rows)
+
+    def o_along_x():
+        theirs = pl.ds(pl.multiple_of((p.z * 2 + 1 - x) * o_cols, LANES), o_cols)
+        net.put(o_acc.at[:, theirs], o_rx, "x", ("ox",))
+
+    def rows_in():
+        far = block((1 - y) * 2 + c)
+        net.got(far, ("bg", "y"))
+        net.put(far, far, "c", ("bg", "c1"))
+        net.got(block(y * 2 + 1 - c), ("bg", "c0"))
+        net.got(block((1 - y) * 2 + 1 - c), ("bg", "c1"))
+
+    def attended_grad():
+        load_wo.wait()
+        ag[...] = lax.dot_general(
+            bg[...], wo[...], CONTRACT_LAST, preferred_element_type=F32
+        ).astype(BF16)
+
     wide = 512
 
     def o_body(i, carry):
         at = pl.ds(pl.multiple_of(i * wide, wide), wide)
-        o_acc[:, at] = lax.dot_general(
+        found = lax.dot_general(
             att[...], bg[:, at], CONTRACT_FIRST, preferred_element_type=F32
         ).astype(BF16)
+        o_acc[:, at] = found[:o_rows]
+        o_rest[:, at] = found[o_rows:]
         return carry
 
-    lax.fori_loop(0, width // wide, o_body, 0)
-    load_qkv.wait()
+    def o_terms():
+        load_att.wait()
+        load_qkv.wait()
+        lax.fori_loop(0, width // wide, o_body, 0)
+
     scale = 1.0 / math.sqrt(HEAD)
-    same = seg_col[...] == seg_row[...]
-    for h in range(heads):
-        o_step(h)
-        out_step(2 + h)
+    same = same_document(seg_row)
+
+    def head(h):
         at = slice(h * HEAD, (h + 1) * HEAD)
         query = qkv[:, h * HEAD : (h + 1) * HEAD]
         keys = qkv[:, cols + h * HEAD : cols + (h + 1) * HEAD]
@@ -1048,24 +1256,67 @@
         low[:, 2 * cols + h * HEAD : 2 * cols + (h + 1) * HEAD] = lax.dot_general(
             probs.astype(BF16), grad, CONTRACT_FIRST, preferred_element_type=F32
         ).astype(BF16)
-    for i in range(heads, max(depth, heads)):
-        o_step(i)
-        out_step(2 + i)
-    load_act.wait()
-    load_w.wait()
-    w_rows = wqkv.shape[1]
+
+    w_rows, w_cols = wqkv.shape[2:]
 
     def w_body(f, carry):
         at = pl.ds(pl.multiple_of(f * w_rows, w_rows), w_rows)
         qkv_part[f] = lax.dot_general(
             act[:, at], low[...], CONTRACT_FIRST, preferred_element_type=F32
         ).astype(BF16)
-        act_grad[:, at] = lax.dot_general(
-            low[...], wqkv[f], CONTRACT_LAST, preferred_element_type=F32
+        act_grad[:, at] = sum(
+            lax.dot_general(
+                low[:, i * w_cols : (i + 1) * w_cols], wqkv[i, f], CONTRACT_LAST,
+                preferred_element_type=F32,
+            )
+            for i in range(3)
         )
         return carry
 
-    lax.fori_loop(0, wqkv.shape[0], w_body, 0)
+    count = wqkv.shape[1]
+    pieces = 4
+
+    def w_piece(i):
+        if i == 0:
+            load_act.wait()
+            load_w.wait()
+        lax.fori_loop(i * count // pieces, (i + 1) * count // pieces, w_body, 0)
+
+    def norm_piece(i):
+        if i == 0:
+            load_whole.wait()
+            gain_part[...] = jnp.zeros_like(gain_part)
+        span = seq // pieces // 16
+
+        def body(k, total):
+            at = pl.ds(pl.multiple_of((i * span + k) * 16, 16), 16)
+            values, grad = whole[at, :].astype(F32), act_grad[at, :]
+            inverse = lax.rsqrt(jnp.mean(values * values, axis=-1, keepdims=True) + EPSILON)
+            scaled = gain[...] * grad
+            pull = jnp.mean(values * scaled, axis=-1, keepdims=True)
+            whole_part[at, :] = (
+                inverse * scaled - values * (inverse * inverse * inverse) * pull
+            ).astype(BF16)
+            return total + jnp.sum(grad * values * inverse, axis=0, keepdims=True)
+
+        total = lax.fori_loop(0, span, body, jnp.zeros(gain_part.shape, F32))
+        gain_part[...] += total
+
+    one, two, three, along_z = flow.one, flow.two, flow.three, flow.along_z
+    if depth == 4 and heads == 4:
+        perform(
+            (one, 0), (one, 1), (one, 2), (along_z, 0), (along_z, 1), (rows_in,),
+            (attended_grad,), (o_terms,), (o_step, 0), (along_z, 2), (two, 0), (head, 0),
+            (two, 1), (one, 3), (o_step, 1), (o_step, 2), (head, 1), (head, 2), (head, 3),
+            (two, 2), (three, 0), (w_piece, 0), (o_step, 3), (w_piece, 1), (along_z, 3),
+            (flow.then_x,), (o_along_x,), (w_piece, 2), (three, 1), (three, 2), (flow.then_y,),
+            (w_piece, 3), (norm_piece, 0), (norm_piece, 1), (two, 3), (norm_piece, 2), (flow.end,), (norm_piece, 3), (three, 3),
+        )
+    else:
+        perform(*every(depth, one), (rows_in,), (attended_grad,), (o_terms,))
+        perform(*every(heads, head), *every(pieces, w_piece, norm_piece))
+        perform(*every(depth, two, three, along_z, o_step), (o_along_x,))
+        perform((flow.then_x,), (flow.then_y,), (flow.end,))
     widen(out_sum, acc.at[p.z, x, y], rows)
     net.got(o_rx, ("ox",))
     at_o = pl.ds(pl.multiple_of((p.z * 2 + x) * o_cols, LANES), o_cols)
@@ -1075,99 +1326,168 @@
         o_sum[at, :] = o_acc[at, at_o].astype(F32) + o_rx[at, :].astype(F32)
         return carry
 
-    lax.fori_loop(0, cols // 16, o_last, 0)
+    lax.fori_loop(0, o_rows // 16, o_last, 0)
     net.finish()
 
 
-def attend_back(depth, mine, act, wqkv, wo, qkv, att, segments, out_part, out_other, o_cols):
+def attend_back(
+    depth, mine, act, wqkv, wo, qkv, att, whole, segments, gain, out_part, out_other, o_cols
+):
     rows, width = mine.shape
     seq, cols = att.shape
-    fsdp, w_rows, w_wide = wqkv.shape
+    _, fsdp, w_rows, w_cols = wqkv.shape
+    w_wide = 3 * w_cols
     shape = jax.ShapeDtypeStruct
     return pl.pallas_call(
         functools.partial(attend_back_kernel, depth),
         out_shape=[
             shape((fsdp, w_rows, w_wide), BF16),
-            shape((seq, width), F32),
-            shape((cols, o_cols), F32),
+            shape((seq, width), BF16),
+            shape((1, width), F32),
+            shape((cols // 2, o_cols), F32),
+            shape((cols // 2, width), BF16),
             shape((rows, width), F32),
         ],
-        in_specs=[ANY] * 6 + [VMEM] * 2 + [ANY] * 2,
-        out_specs=[VMEM] * 4,
-        scratch_shapes=reduce_scratch(depth, rows, width)
+        in_specs=[ANY] * 7 + [VMEM] * 2 + [ANY] * 2,
+        out_specs=[VMEM] * 6,
+        scratch_shapes=reduce_scratch(
+            depth, rows, width, [tile_rows(rows, 0.375), tile_rows(rows, 0.5)]
+        )
         + [
             pltpu.VMEM((2, 2, 2, rows, width), BF16),
             pltpu.VMEM((seq, width), BF16),
             pltpu.VMEM((seq, width), BF16),
-            pltpu.VMEM((fsdp, w_rows, w_wide), BF16),
+            pltpu.VMEM(wqkv.shape, BF16),
             pltpu.VMEM((cols, width), BF16),
             pltpu.VMEM((seq, w_wide), BF16),
             pltpu.VMEM((seq, cols), BF16),
             pltpu.VMEM((seq, cols), BF16),
             pltpu.VMEM((seq, w_wide), BF16),
-            pltpu.VMEM((cols, width), BF16),
-            pltpu.VMEM((depth + 1, cols, 2 * o_cols), BF16),
-            pltpu.VMEM((cols, o_cols), BF16),
+            pltpu.VMEM((cols // 2, width), BF16),
+            pltpu.VMEM((depth + 1, cols // 2, 2 * o_cols), BF16),
+            pltpu.VMEM((cols // 2, o_cols), BF16),
+            pltpu.VMEM((seq, width), BF16),
+            pltpu.VMEM((seq, width), F32),
         ]
         + sems()
         + [pltpu.SemaphoreType.DMA((2, 2))],
         compiler_params=comm_params(4, 63),
         name="attend_back",
     )(
-        mine, act, wqkv, wo, qkv, att, segments[:, None], segments[None, :],
+        mine, act, wqkv, wo, qkv, att, whole, segments[None, :], gain[None, :],
         out_part.reshape(depth, 2, 2, 2, rows, width), out_other,
     )
 
 
 def last_kernel(
-    depth, tail, qkv_part, row_part, q_sum, k_sum, v_sum, row_sum, tail_sum,
-    q_acc, q_rx, q_inbox, t_acc, t_rc, t_ry, s_acc, s_rc, s_ry, s_rx, s_inbox, send, recv, local,
+    depth, tail, qkv_part, row_part, o_part, q_sum, k_sum, v_sum, row_sum, tail_sum, o_sum,
+    q_acc, q_rx, q_inbox, t_acc, t_rc, t_ry, s_acc, s_rc, s_ry, s_rx, s_inbox,
+    o_acc, o_inbox, o_rx, send, recv, local,
 ):
     p = Place(depth)
     net = Net(p, send, recv, local)
     x, y, c = p.x, p.y, p.c
     rows, width = row_sum.shape
     w_rows, w_cols = q_sum.shape
+    o_rows, o_cols = o_sum.shape
     small = s_acc.shape[3]
-    loads = [net.local(qkv_part.at[p.far[i], x], q_acc.at[p.far[i]]) for i in range(depth)]
+    o_load = net.local(o_part, o_acc)
     t_load = net.local(row_part.at[:, c], t_acc)
     s_load = net.local(tail.at[:, :, :, c], s_acc)
+    loads = [net.local(qkv_part.at[p.far[i], x], q_acc.at[p.far[i]]) for i in range(depth)]
     greet(p, ("x", "y", "c", "z"))
-    for i in range(depth):
+
+    def q_along_x(i):
         zz = p.far[i]
         net.put(qkv_part.at[zz, 1 - x], q_rx.at[zz], "x", ("qx", "at", depth, zz))
-    net.put(tail.at[:, :, :, 1 - c], s_rc, "c", ("sc",))
-    net.put(row_part.at[:, 1 - c], t_rc, "c", ("tc",))
-    t_load.wait()
-    net.got(t_rc, ("tc",))
-    add_rows(t_acc.at[1 - y], t_rc.at[1 - y], rows)
-    net.put(t_acc.at[1 - y], t_ry, "y", ("ty",))
-    s_load.wait()
-    net.got(s_rc, ("sc",))
-    for zz in range(depth):
-        for xx in range(2):
-            add_rows(s_acc.at[zz, xx, 1 - y], s_rc.at[zz, xx, 1 - y], small)
-    net.put(s_acc.at[:, :, 1 - y], s_ry, "y", ("sy",))
-    for zz in range(depth):
-        for xx in range(2):
-            add_rows(s_acc.at[zz, xx, y], s_rc.at[zz, xx, y], small)
-    for i in range(depth):
+
+    def q_along_z(i):
         zz = p.far[i]
         loads[i].wait()
         net.got(q_rx.at[zz], ("qx", "at", depth, zz))
         add_rows(q_acc.at[zz], q_rx.at[zz], w_rows)
         chain_z(net, "qz", zz, q_acc.at[zz], q_inbox, w_rows)
+
+    def o_along_z(i):
         if i == 0:
-            net.got(s_ry, ("sy",))
-            for z in range(depth):
-                for xx in range(2):
-                    add_rows(s_acc.at[z, xx, y], s_ry.at[z, xx], small)
-            net.put(s_acc.at[:, 1 - x, y], s_rx, "x", ("sx",))
-    net.got(s_rx, ("sx",))
-    for z in range(depth):
-        add_rows(s_acc.at[z, x, y], s_rx.at[z], small)
-    for i in range(depth):
+            o_load.wait()
+        zz = p.far[i]
+        pair = o_acc.at[:, pl.ds(pl.multiple_of(zz * (2 * o_cols), LANES), 2 * o_cols)]
+        chain_z(net, "oz", zz, pair, o_inbox, o_rows)
+
+    def o_along_x():
+        theirs = pl.ds(pl.multiple_of((p.z * 2 + 1 - x) * o_cols, LANES), o_cols)
+        net.put(o_acc.at[:, theirs], o_rx, "x", ("ox",))
+
+    def cores():
+        net.put(row_part.at[:, 1 - c], t_rc, "c", ("tc",))
+        net.put(tail.at[:, :, :, 1 - c], s_rc, "c", ("sc",))
+
+    def along_y():
+        t_load.wait()
+        net.got(t_rc, ("tc",))
+        add_rows(t_acc.at[1 - y], t_rc.at[1 - y], rows)
+        net.put(t_acc.at[1 - y], t_ry, "y", ("ty",))
+        s_load.wait()
+        net.got(s_rc, ("sc",))
+        for zz in range(depth):
+            for xx in range(2):
+                add_rows(s_acc.at[zz, xx, 1 - y], s_rc.at[zz, xx, 1 - y], small)
+        net.put(s_acc.at[:, :, 1 - y], s_ry, "y", ("sy",))
+        for zz in range(depth):
+            for xx in range(2):
+                add_rows(s_acc.at[zz, xx, y], s_rc.at[zz, xx, y], small)
+
+    def s_along_x():
+        net.got(s_ry, ("sy",))
+        for z in range(depth):
+            for xx in range(2):
+                add_rows(s_acc.at[z, xx, y], s_ry.at[z, xx], small)
+        net.put(s_acc.at[:, 1 - x, y], s_rx, "x", ("sx",))
+
+    def s_in():
+        net.got(s_rx, ("sx",))
+        for z in range(depth):
+            add_rows(s_acc.at[z, x, y], s_rx.at[z], small)
+
+    def s_along_z(i):
         chain_z(net, "sz", p.far[i], s_acc.at[p.far[i], x, y], s_inbox, small)
+
+    def rows_in():
+        net.got(t_ry, ("ty",))
+
+        def body(i, carry):
+            at = pl.ds(pl.multiple_of(i * 16, 16), 16)
+            row_sum[at, :] = (
+                t_acc[y, at, :].astype(F32) + t_rc[y, at, :].astype(F32) + t_ry[at, :].astype(F32)
+            )
+            return carry
+
+        lax.fori_loop(0, rows // 16, body, 0)
+
+    def o_in():
+        net.got(o_rx, ("ox",))
+        at_o = pl.ds(pl.multiple_of((p.z * 2 + x) * o_cols, LANES), o_cols)
+
+        def body(i, carry):
+            at = pl.ds(pl.multiple_of(i * 16, 16), 16)
+            o_sum[at, :] = o_acc[at, at_o].astype(F32) + o_rx[at, :].astype(F32)
+            return carry
+
+        lax.fori_loop(0, o_rows // 16, body, 0)
+
+    if depth == 4:
+        perform(
+            (q_along_x, 0), (cores,), (o_along_z, 0), (q_along_x, 1), (o_along_z, 1), (along_y,),
+            (o_along_z, 2), (s_along_x,), (q_along_x, 2), (q_along_z, 0), (q_along_x, 3),
+            (o_along_z, 3), (rows_in,), (s_in,), (o_along_x,), (s_along_z, 0), (q_along_z, 1),
+            (q_along_z, 2), (s_along_z, 1), (o_in,), (s_along_z, 2), (q_along_z, 3),
+            (s_along_z, 3),
+        )
+    else:
+        perform(*every(depth, q_along_x), (cores,), (along_y,), (s_along_x,))
+        perform(*every(depth, q_along_z, o_along_z), (s_in,), (o_along_x,))
+        perform(*every(depth, s_along_z), (rows_in,), (o_in,))
 
     def q_last(i, carry):
         at = pl.ds(pl.multiple_of(i * 16, 16), 16)
@@ -1176,32 +1496,23 @@
         return carry
 
     lax.fori_loop(0, w_rows // 16, q_last, 0)
-    net.got(t_ry, ("ty",))
-
-    def rows_last(i, carry):
-        at = pl.ds(pl.multiple_of(i * 16, 16), 16)
-        row_sum[at, :] = (
-            t_acc[y, at, :].astype(F32) + t_rc[y, at, :].astype(F32) + t_ry[at, :].astype(F32)
-        )
-        return carry
-
-    lax.fori_loop(0, rows // 16, rows_last, 0)
     widen(tail_sum, s_acc.at[p.z, x, y], small)
     net.finish()
 
 
-def last_reduce(depth, tail, qkv_part, row_part):
+def last_reduce(depth, tail, qkv_part, row_part, o_part):
     count, small, lanes = tail.shape
     fsdp, w_rows, w_wide = qkv_part.shape
     tp, rows, width = row_part.shape
     w_cols = w_wide // 3
+    o_rows, o_cols = o_part.shape[0], width // fsdp
     shape = jax.ShapeDtypeStruct
     return pl.pallas_call(
         functools.partial(last_kernel, depth),
         out_shape=[shape((w_rows, w_cols), F32)] * 3
-        + [shape((rows, width), F32), shape((small, lanes), F32)],
-        in_specs=[ANY] * 3,
-        out_specs=[VMEM] * 5,
+        + [shape((rows, width), F32), shape((small, lanes), F32), shape((o_rows, o_cols), F32)],
+        in_specs=[ANY] * 4,
+        out_specs=[VMEM] * 6,
         scratch_shapes=[
             pltpu.VMEM((depth, w_rows, w_wide), BF16),
             pltpu.VMEM((depth, w_rows, w_wide), BF16),
@@ -1214,14 +1525,18 @@
             pltpu.VMEM((depth, 2, small, lanes), BF16),
             pltpu.VMEM((depth, small, lanes), BF16),
             pltpu.VMEM((depth + 1, small, lanes), BF16),
+            pltpu.VMEM((o_rows, width), BF16),
+            pltpu.VMEM((depth + 1, o_rows, 2 * o_cols), BF16),
+            pltpu.VMEM((o_rows, o_cols), BF16),
         ]
         + sems(),
-        compiler_params=comm_params(5, 40),
+        compiler_params=comm_params(5, 48),
         name="last_reduce",
     )(
         tail.reshape(depth, 2, 2, 2, small, lanes),
         qkv_part.reshape(depth, 2, w_rows, w_wide),
         row_part.reshape(2, 2, rows, width),
+        o_part,
     )
 
 
@@ -1277,33 +1592,12 @@
     blank = jnp.zeros((rows, experts), F32)
     mask = jnp.concatenate([hits, hits, blank, fill], axis=1)
     rank = jnp.concatenate([blank, blank, ranks, fill], axis=1)
-    router_pad = jnp.concatenate(
-        [router, router, jnp.zeros((width, LANES - 2 * experts), BF16)], axis=1
-    )
-
-    qkv_full, full_output, whole = first_gather(
-        depth, w_query, w_key, w_value, w_output, inputs, tp
-    )
-    whole_float = whole.reshape(seq, width).astype(F32)
-    normed_one, inverse_one = norm_rows(whole_float, attn_gain)
-    act_one = normed_one.astype(BF16)
-    qkv = jnp.dot(act_one, qkv_full.reshape(width, 3 * w_cols), preferred_element_type=F32).astype(BF16)
-    query, key_rows, value_rows = [
-        qkv[:, i * w_cols : (i + 1) * w_cols].reshape(seq, heads, HEAD) for i in range(3)
-    ]
-    score_scale = 1.0 / math.sqrt(HEAD)
-    scores = jnp.einsum("qhd,khd->hqk", query, key_rows, preferred_element_type=F32) * score_scale
-    scores = jnp.where((segments[:, None] == segments[None, :])[None], scores, -1e30)
-    probs = jax.nn.softmax(scores, axis=-1)
-    attended = (
-        jnp.einsum("hqk,khd->qhd", probs.astype(BF16), value_rows, preferred_element_type=F32)
-        .reshape(seq, -1)
-        .astype(BF16)
-    )
-    partial = jnp.dot(attended, full_output, preferred_element_type=F32).astype(BF16)
+    qkv_full, full_output, whole, act_one, qkv, attended, partial, grad_all = first_gather(
+        depth, w_query, w_key, w_value, w_output, inputs, out_grad, attn_gain, segments, tp
+    )
     resid, gates_wide, _, _, out_part, back_part, x_rows, g_rows, hid_low, gate_low, up_low = run_moe(
         depth, capacity, experts, partial.reshape(tp, rows, width), inputs, out_grad, moe_gain,
-        router_pad, mask, rank, w_gate, w_up, w_down,
+        router.T, mask, rank, w_gate, w_up, w_down, grad_all,
     )
     back, out_other, w_gate_grad, w_up_grad, w_down_grad = reduce_back(
         depth, back_part, out_part, x_rows, g_rows, hid_low, gate_low, up_low
@@ -1324,20 +1618,19 @@
     )
     resid_part, gain_two_part = norm_back(resid, inverse_two, moe_gain, act_two_grad)
     resid_grad = out_grad.astype(F32) + resid_part
-    qkv_part, act_one_grad, o_sum, out_sum = attend_back(
-        depth, resid_grad.astype(BF16), act_one, qkv_full, full_output, qkv, attended, segments,
-        out_part, out_other, w_output.shape[1],
-    )
-    whole_part, gain_one_part = norm_back(whole_float, inverse_one, attn_gain, act_one_grad)
-
+    qkv_part, whole_part, gain_one_part, o_first, o_rest, out_sum = attend_back(
+        depth, resid_grad.astype(BF16), act_one, qkv_full, full_output, qkv, attended,
+        whole.reshape(seq, width), segments, attn_gain, out_part, out_other, w_output.shape[1],
+    )
     count = fsdp * tp
     piece = width // count
-    small = jnp.concatenate([router_part, gain_one_part[:, None], gain_two_part[:, None]], axis=1)
+    small = jnp.concatenate([router_part, gain_one_part.reshape(-1, 1), gain_two_part[:, None]], axis=1)
     small = small.astype(BF16).reshape(count, piece, experts + 2)
     tail = jnp.pad(small, ((0, 0), (0, -piece % 16), (0, LANES - experts - 2)))
-    q_sum, k_sum, v_sum, row_sum, side = last_reduce(
-        depth, tail, qkv_part, whole_part.astype(BF16).reshape(tp, rows, width)
-    )
+    q_sum, k_sum, v_sum, row_sum, side, o_second = last_reduce(
+        depth, tail, qkv_part, whole_part.reshape(tp, rows, width), o_rest
+    )
+    o_sum = jnp.concatenate([o_first, o_second], axis=0)
     output = (resid + out_sum).astype(BF16)
     input_grad = resid_grad + row_sum
     side = side[:piece]
@@ -1351,9 +1644,9 @@
         o_sum,
         side[:, experts + 1],
         side[:, :experts],
-        w_gate_grad,
-        w_up_grad,
-        w_down_grad,
+        w_gate_grad.astype(F32),
+        w_up_grad.astype(F32),
+        w_down_grad.astype(F32),
     )
 
 

time: 708 us -> 588 us (0.83)
  Pallas kernels: 626 us -> 542 us
  local copies, waits for them, and re-layouts: 33.9 us -> 8.22 us
  matrix products: 12.4 us -> 2.73 us
    pallas_call x1, Pallas kernels: 130 us -> 87.6 us  [attend_back(): pl.pallas_call(functools.partial(attend_back_kernel, depth), out_shape=[s...]
    pallas_call x1, Pallas kernels: 104 us -> 79.1 us  [reduce_back(): pl.pallas_call(functools.partial(back_kernel, depth), out_shape=[shape((r...]
    unnamed x56 -> x24, local copies, waits for them, and re-layouts: 25.6 us -> 3.11 us
    pallas_call x1, Pallas kernels: 203 us -> 189 us  [run_moe(): pl.pallas_call(functools.partial(moe_kernel, depth, capacity, experts, bl...]
    convert_element_type x3, other arithmetic: 5.18 us -> 15.1 us  [the longest x1 6.47 us: dense_layer(): w_gate_grad.astype(F32)]
    dot_general x4 -> x0, matrix products: 9.52 us -> none  [the longest x1 3.42 us: dense_layer(): jnp.dot(act_one, qkv_full.reshape(width, 3 * w_cols), preferred_element_t...]
    pallas_call x1, Pallas kernels: 90.1 us -> 81.2 us  [last_reduce(): pl.pallas_call(functools.partial(last_kernel, depth), out_shape=[shape((w...]
where the time goes in v3:
time: 588 us; the launch traced here: 579 us
  Pallas kernels  542 us (92%)
  other arithmetic  25.1 us (4%)
  local copies, waits for them, and re-layouts  8.22 us (1%)
    pallas_call x1, Pallas kernels, run_moe(): pl.pallas_call(functools.partial(moe_kernel, depth, capacity, experts, bl...  189 us
    pallas_call x1, Pallas kernels, first_gather(): pl.pallas_call(functools.partial(first_kernel, depth), out_shape=[shape((...  105 us
    pallas_call x1, Pallas kernels, attend_back(): pl.pallas_call(functools.partial(attend_back_kernel, depth), out_shape=[s...  87.6 us
    pallas_call x1, Pallas kernels, last_reduce(): pl.pallas_call(functools.partial(last_kernel, depth), out_shape=[shape((w...  81.2 us
    pallas_call x1, Pallas kernels, reduce_back(): pl.pallas_call(functools.partial(back_kernel, depth), out_shape=[shape((r...  79.1 us

profile of v3, /device:TPU:2, one launch (start us, length us, event | category | flops | bytes accessed | tf_op | source)
XLA Modules:
  0.0 579.3 jit_solution(14020684582456886167)
XLA Ops:
  0.7 0.1 pad.12.clone
  0.7 0.7 fusion.7
  1.4 0.1 copy.60
  1.6 0.1 convolution_select_fusion
  1.7 0.1 copy.58
  1.8 0.8 maximum_maximum_fusion
  2.6 104.9 %first_gather.1 = (bf16[3,8,256,512]{3,2,1,0:T(8,128)(2,1)}, bf16[512,2048]{1,0:T(8,128)(2,1)}, bf16[4,128,2048]{2,1,0:T(8,128)(2,1)}, bf16[512,2048]{1,0:T(8,12...) custom-call(bf16[256,512]{1,0:T(8,128)(2,1)} %wq.1, ...), custom_call_target="tpu_custom_call" | custom-call | tf_op jit(solution)/shard_map/first_gather/pallas_call | solution.py:516
  107.4 189.3 %moe.1 = (f32[128,2048]{1,0:T(8,128)}, f32[128,128]{1,0:T(8,128)}, bf16[32,128,2176]{2,1,0:T(8,128)(2,1)}, bf16[32,128,2048]{2,1,0:T(8,128)(2,1)}, bf16[32,128,2...) custom-call(bf16[2,2,128,2048]{3,2,1,0:T(8,128)(2,1)} %bitcast.24, ...), custom_call_target="tpu_custom_call", output_to_operand_aliasing={{3}: (10, {})} | custom-call | tf_op jit(solution)/shard_map/moe/pallas_call | solution.py:815
  296.7 0.0 copy-start.1
  296.7 0.0 copy-start.6
  296.7 0.0 copy-start.7
  296.8 0.0 copy-start.9
  296.8 79.1 %reduce_back.1 = (f32[128,2176]{1,0:T(8,128)}, bf16[4,2,2,128,2048]{4,3,2,1,0:T(8,128)(2,1)}, bf16[4,2048,256]{2,1,0:T(8,128)(2,1)}, bf16[4,2048,256]{2,1,0:T(8,128)(2,1)}, bf16[4,256,2048]{2,1,0:T(8,128)(2,1)}) custom-call(bf16[4,2,2,2,128,2176]{5,4,3,2,1,0:T(8,128)(2,1)} %bitcast.20, bf16[4,2,2,2,128,2048]{5,4,3,2,1,0:T(8,128)(2,1)} %bitcast.18, ...), custom_call_target="tpu_custom_call" | custom-call | tf_op jit(solution)/shard_map/reduce_back/pallas_call | solution.py:1112
  375.9 0.0 copy-start.2
  375.9 0.0 copy-done.1
  375.9 0.2 multiply_reduce_fusion.2
  376.1 0.9 slice.20
  376.9 0.1 copy.62
  377.0 0.1 copy.64
  377.1 0.0 copy-done.6
  377.1 0.1 multiply_reduce_fusion.3
  377.2 0.0 copy-done.7
  377.2 0.0 copy-done.9
  377.3 2.1 multiply_reduce_fusion
  379.4 0.5 convolution_convert_fusion
  379.9 0.3 copy.70
  380.1 1.8 concatenate.28
  382.0 0.0 copy-done.2
  382.0 1.5 fusion.8
  383.5 87.6 %attend_back.1 = (bf16[8,256,1536]{2,1,0:T(8,128)(2,1)}, bf16[512,2048]{1,0:T(8,128)(2,1)}, f32[1,2048]{1,0:T(1,128)}, f32[256,256]{1,0:T(8,128)}, bf16[256,2048]{1,0:T(8,128)(2,1)}, /*index=5*/f32[128,2048]{1,0:T(8,128)}) custom-call(bf16[128,2048]{1,0:T(8,128)(2,1)} %get-tuple-element.144.mine, bf16[512,2048]{1,0:T(8,128)(2,1)} %get-tuple-element.58.act_hbm, ...), custom_call_target="tpu_custom_call" | custom-call | tf_op jit(solution)/shard_map/attend_back/pallas_call | solution.py:1341
  471.1 0.0 copy-start
  471.1 2.5 add_convert_fusion
  473.6 0.7 convert_reduce_fusion
  474.4 1.0 concatenate.27
  475.4 1.6 fusion.4
  477.0 0.0 copy-done
  477.0 0.0 copy-start.5
  477.0 0.0 copy-start.8
  477.0 81.2 %last_reduce.1 = (f32[256,512]{1,0:T(8,128)S(1)}, f32[256,512]{1,0:T(8,128)S(1)}, f32[256,512]{1,0:T(8,128)S(1)}, f32[128,2048]{1,0:T(8,128)S(1)}, f32[64,128]{1,0:T(8,128)S(1)}, /*index=5*/f32[256,256]{1,0:T(8,128)S(1)}) custom-call(bf16[4,2,2,2,64,128]{5,4,3,2,1,0:T(8,128)(2,1)S(1)} %bitcast.16, bf16[4,2,256,1536]{3,2,1,0:T(8,128)(2,1)} %bitcast.21, ...), custom_call_target="tpu_custom_call" | custom-call | tf_op jit(solution)/shard_map/last_reduce/pallas_call | solution.py:1510
  558.3 0.0 copy-done.5
  558.3 1.1 add.33
  559.4 0.7 slice_reduce_fusion
  560.1 0.7 copy.68
  560.8 0.0 copy-done.8
  560.8 0.8 pad_maximum_fusion
  561.6 0.0 copy-start.4
  561.6 6.5 %convert_element_type.36 = f32[4,2048,256]{2,1,0:T(8,128)} convert(bf16[4,2048,256]{2,1,0:T(8,128)(2,1)} %get-tuple-element.77) | non-fusion elementwise | flops 2097152 | bytes 12582912 | tf_op jit(solution)/shard_map/convert_element_type | solution.py:1647
  568.1 0.0 copy-done.4
  568.1 0.0 copy-start.3
  568.1 4.1 convert_element_type.37
  572.2 0.0 copy-done.3
  572.2 4.4 convert_element_type.38
  576.7 0.8 copy.76
  577.5 0.8 copy.77
  578.3 0.8 copy.78
  (6 shorter events, 0.0 us)
Async XLA Ops:
  296.7 79.2 %copy-start.1 = (f32[128,2048]{1,0:T(8,128)S(1)}, f32[128,2048]{1,0:T(8,128)}, u32[]{:S(2)}) copy-start(f32[128,2048]{1,0:T(8,128)} %get-tuple-element.48) | copy-start | bytes 3145732
  296.7 80.4 %copy-start.6 = (f32[128,128]{1,0:T(8,128)S(1)}, f32[128,128]{1,0:T(8,128)}, u32[]{:S(2)}) copy-start(f32[128,128]{1,0:T(8,128)} %get-tuple-element.57) | copy-start | bytes 196612
  296.7 80.5 %copy-start.7 = (bf16[2048,32]{0,1:T(8,128)(2,1)S(1)}, bf16[2048,32]{0,1:T(8,128)(2,1)}, u32[]{:S(2)}) copy-start(bf16[2048,32]{0,1:T(8,128)(2,1)} %param.24) | copy-start | bytes 393220
  296.8 80.5 %copy-start.9 = (f32[2048]{0:T(1024)S(1)}, f32[2048]{0:T(1024)}, u32[]{:S(2)}) copy-start(f32[2048]{0:T(1024)} %param.23) | copy-start | bytes 24580
  375.9 6.1 %copy-start.2 = (bf16[128,2048]{1,0:T(8,128)(2,1)S(1)}, bf16[128,2048]{1,0:T(8,128)(2,1)}, u32[]{:S(2)}) copy-start(bf16[128,2048]{1,0:T(8,128)(2,1)} %og.3) | copy-start | bytes 1572868
  471.1 5.9 %copy-start = (bf16[256,2048]{1,0:T(8,128)(2,1)S(1)}, bf16[256,2048]{1,0:T(8,128)(2,1)}, u32[]{:S(2)}) copy-start(bf16[256,2048]{1,0:T(8,128)(2,1)} %get-tuple-element.69.o_part) | copy-start | bytes 3145732
  477.0 81.3 %copy-start.5 = (f32[128,2048]{1,0:T(8,128)S(1)}, f32[128,2048]{1,0:T(8,128)}, u32[]{:S(2)}) copy-start(f32[128,2048]{1,0:T(8,128)} %get-tuple-element.145) | copy-start | bytes 3145732
  477.0 83.8 %copy-start.8 = (f32[256,256]{1,0:T(8,128)S(1)}, f32[256,256]{1,0:T(8,128)}, u32[]{:S(2)}) copy-start(f32[256,256]{1,0:T(8,128)} %get-tuple-element.75) | copy-start | bytes 786436
  561.6 6.5 %copy-start.4 = (bf16[4,2048,256]{2,1,0:T(8,128)(2,1)S(1)}, bf16[4,2048,256]{2,1,0:T(8,128)(2,1)}, u32[]{:S(2)}) copy-start(bf16[4,2048,256]{2,1,0:T(8,128)(2,1)} %get-tuple-element.78) | copy-start | bytes 12582916
  568.1 4.1 copy-start.3

commit v4 on v3

--- a/solution.py
+++ b/solution.py
@@ -318,12 +318,8 @@
     def take_z(self, zz):
         self.z_copy(zz, True).wait_recv()
 
-    def along_z(self, zz, near_too=True):
-        p = self.place
-        if near_too:
-            self.take_z(zz)
-        else:
-            pl.when((zz != p.z + 1) & (zz != p.z - 1))(lambda: self.take_z(zz))
+    def along_z(self, zz):
+        self.take_z(zz)
         self.each_z(zz, lambda up: self.z_copy(zz, up).start())
 
     def first(self, zz, mine=False):
@@ -343,18 +339,24 @@
         self.take("y1", zz)
         self.copy("x2", zz).start()
 
-    def third(self, zz):
+    def third_y(self, zz):
+        self.take("y3", zz)
+        self.copy("cy", zz).start()
+
+    def third_x(self, zz):
         self.take("x3", zz)
         self.copy("cx", zz).start()
-        self.take("y3", zz)
-        self.copy("cy", zz).start()
         self.take("x2", zz)
         self.take("y2", zz)
         self.copy("cxy", zz).start()
 
-    def arrived(self, zz):
-        for site in ("c0", "cx", "cy", "cxy"):
-            self.take(site, zz)
+    def arrived_y(self, zz):
+        self.take("c0", zz)
+        self.take("cy", zz)
+
+    def arrived_x(self, zz):
+        self.take("cx", zz)
+        self.take("cxy", zz)
 
     def finish(self, zs, z_zs):
         for zz in zs:
@@ -484,25 +486,26 @@
 
     if depth == 4 and heads == 4:
         perform(
-            (v_step, 0), (o_begin,), (k_step, 0), (q_step, 0), (o_step, 0), (q_step, 1),
-            (q_step, 2), (v_step, 1), (v_step, 2), (q_step, 3), (k_step, 1), (k_step, 2),
-            (v_step, 3), (k_step, 3), (q_step, 4), (o_step, 1), (v_step, 4), (q_step, 5),
-            (k_step, 4), (o_step, 2), (q_step, 6), (rows_in,), (k_step, 5), (v_step, 5),
-            (v_step, 6), (project_with, 0), (k_step, 6), (g_first,), (o_step, 3), (o_step, 4),
-            (project_with, 1), (grads.own_along_z,), (project_with, 2), (head, 0), (grads.second, p.z),
-            (head, 1), (head, 2), (grads.third, p.z), (o_step, 5), (head, 3), (o_step, 6), (branch,),
-            (grads.arrived, p.z),
+            (o_begin,), (v_step, 0), (q_step, 0), (k_step, 0), (q_step, 1), (q_step, 2),
+            (q_step, 3), (v_step, 1), (k_step, 1), (k_step, 2), (q_step, 4), (k_step, 3),
+            (v_step, 2), (q_step, 5), (rows_in,), (v_step, 3), (q_step, 6), (k_step, 4),
+            (o_step, 0), (v_step, 4), (k_step, 5), (o_step, 1), (v_step, 5), (o_step, 2),
+            (k_step, 6), (project_with, 0), (v_step, 6), (project_with, 1), (g_first,),
+            (o_step, 3), (o_step, 4), (project_with, 2), (head, 0), (grads.second, p.z),
+            (head, 1), (head, 2), (head, 3), (o_step, 5), (o_step, 6), (branch,),
+            (grads.third_y, p.z), (grads.third_x, p.z),
+            (grads.arrived_y, p.z), (grads.arrived_x, p.z),
         )
     else:
         perform((o_begin,), (g_first,), *every(steps, q_step, k_step, v_step, o_step), (rows_in,))
-        perform((grads.second, p.z), (grads.third, p.z), *every(3, project_with))
-        perform(*every(heads, head), (branch,), (grads.own_along_z,), (grads.arrived, p.z))
-    pl.when(p.can_down)(lambda: grads.take_z(p.z - 1))
-    pl.when(p.can_up)(lambda: grads.take_z(p.z + 1))
+        perform((grads.second, p.z), (grads.third_y, p.z), (grads.third_x, p.z))
+        perform(*every(3, project_with))
+        perform(*every(heads, head), (branch,))
+        perform((grads.arrived_y, p.z), (grads.arrived_x, p.z))
     kept.wait()
     for copy in saves:
         copy.wait()
-    grads.finish([p.z], [p.z])
+    grads.finish([p.z], [])
     net.finish()
 
 
@@ -621,8 +624,11 @@
     places = lax.broadcasted_iota(jnp.int32, (capacity, rows), 0).astype(F32)
     slots = blocks * capacity
 
+    def blocks_of(zz, j):
+        return (zz * 2 + (1 - p.x if j else p.x)) * blocks
+
     def loads(zz, j):
-        at = pl.ds((zz * 2 + j) * blocks, blocks)
+        at = pl.ds(blocks_of(zz, j), blocks)
         return [
             pltpu.make_async_copy(act_all.at[at], act_in.at[j], load_sems.at[j, 0]),
             pltpu.make_async_copy(grad_all.at[at], grad_in.at[j], load_sems.at[j, 1]),
@@ -630,12 +636,12 @@
 
     def save(zz, j, k):
         if k < 5:
-            where = pl.ds(pl.multiple_of((zz * 2 + j) * slots, 16), slots)
+            where = pl.ds(pl.multiple_of(blocks_of(zz, j) * capacity, 16), slots)
             src = (x_rows, g_rows, hid, gl, ul)[k]
             dst = (x_hbm, g_hbm, hid_hbm, gl_hbm, ul_hbm)[k].at[:, where]
         else:
             src = (out, back)[k - 5]
-            dst = (out_hbm, back_hbm)[k - 5].at[pl.ds((zz * 2 + j) * blocks, blocks)]
+            dst = (out_hbm, back_hbm)[k - 5].at[pl.ds(blocks_of(zz, j), blocks)]
         return pltpu.make_async_copy(src, dst, save_sems.at[k])
 
     def one_hot(j, b):
@@ -729,57 +735,69 @@
             save(zz, j, k).start()
         serve(5)
 
-    def load(i):
-        if i == 0:
+    def load(i, j):
+        if i == j == 0:
             kept[0].wait()
             for copy in weights:
                 copy.wait()
-        for copy in loads(p.near[i], 0):
+        for copy in loads(p.near[i], j):
             copy.start()
 
     near = p.near
-    g1, g2, g3 = grads.first, grads.second, grads.third
-    a1, a2, a3 = acts.first, acts.second, acts.third
+    g1, g2, g3y, g3x = grads.first, grads.second, grads.third_y, grads.third_x
+    a1, a2, a3y, a3x = acts.first, acts.second, acts.third_y, acts.third_x
     if depth == 4:
         perform(
-            (grads.along_z, near[1], False), (along_y,), (g1, near[1]),
-            (grads.along_z, near[2], False), (norm,), (acts.own_along_z,), (a1, p.z, True),
-            (acts.along_z, near[1]), (a2, p.z), (g2, near[1]), (a1, near[1]),
-            (acts.along_z, near[2]), (a3, p.z), (a1, near[2]), (acts.arrived, p.z), (load, 0),
+            (grads.own_along_z,), (along_y,), (grads.along_z, near[1]), (g1, near[1]), (norm,),
+            (acts.own_along_z,), (a1, p.z, True), (a2, p.z), (acts.along_z, near[1]), (a3y, p.z),
+            (a1, near[1]), (acts.arrived_y, p.z), (load, 0, 0), (g2, near[1]),
+            (grads.along_z, near[2]), (g1, near[2]),
         )
         service = {
-            (0, 0, 0): [(g3, near[1])],
-            (0, 0, 1): [(acts.along_z, near[3])],
-            (0, 0, 3): [(a2, near[1]), (g1, near[2])],
-            (0, 1, 1): [(grads.along_z, near[3], False)],
-            (0, 1, 2): [(a3, near[1]), (a2, near[2])],
-            (0, 1, 4): [(acts.arrived, near[1])],
-            (0, 1, 5): [(g2, near[2]), (grads.arrived, near[1]), (load, 1)],
-            (1, 0, 4): [(a1, near[3])],
-            (1, 0, 5): [(g3, near[2])],
-            (1, 1, 1): [(grads.arrived, near[2])],
-            (1, 1, 2): [(a3, near[2]), (a2, near[3])],
-            (1, 1, 4): [(acts.arrived, near[2]), (load, 2)],
-            (2, 0, 0): [(g1, near[3])],
-            (2, 0, 1): [(a3, near[3])],
-            (2, 0, 5): [(g2, near[3])],
-            (2, 1, 3): [(g3, near[3])],
-            (2, 1, 5): [(acts.arrived, near[3]), (grads.arrived, near[3]), (load, 3)],
+            (0, 0, 1): [(a3x, p.z)],
+            (0, 0, 3): [(acts.arrived_x, p.z), (load, 0, 1)],
+            (0, 0, 4): [(acts.along_z, near[2])],
+            (0, 0, 5): [(a2, near[1])],
+            (0, 1, 0): [(a1, near[2]), (g3y, near[1])],
+            (0, 1, 2): [(a3y, near[1])],
+            (0, 1, 3): [
+                (acts.arrived_y, near[1]), (grads.along_z, near[3]), (grads.arrived_y, near[1]),
+                (load, 1, 0),
+            ],
+            (1, 0, 0): [(g2, near[2])],
+            (1, 0, 1): [(g3x, near[1]), (g3y, near[2])],
+            (1, 0, 2): [(g1, near[3])],
+            (1, 0, 3): [(a3x, near[1])],
+            (1, 0, 4): [
+                (acts.along_z, near[3]), (a2, near[2]), (a3y, near[2]), (acts.arrived_x, near[1]),
+                (grads.arrived_x, near[1]), (load, 1, 1),
+            ],
+            (1, 0, 5): [(g3x, near[2])],
+            (1, 1, 3): [(grads.arrived_y, near[2]), (acts.arrived_y, near[2]), (load, 2, 0)],
+            (1, 1, 4): [(a1, near[3])],
+            (2, 0, 0): [(a3x, near[2])],
+            (2, 0, 3): [(g2, near[3]), (grads.arrived_x, near[2])],
+            (2, 0, 4): [(g3y, near[3]), (a2, near[3]), (acts.arrived_x, near[2]), (load, 2, 1)],
+            (2, 0, 5): [(a3y, near[3])],
+            (2, 1, 1): [(acts.arrived_y, near[3]), (grads.arrived_y, near[3]), (load, 3, 0)],
+            (3, 0, 0): [(a3x, near[3])],
+            (3, 0, 1): [(g3x, near[3])],
+            (3, 0, 4): [(grads.arrived_x, near[3]), (acts.arrived_x, near[3]), (load, 3, 1)],
         }
     else:
-        perform((along_y,), (norm,), (acts.own_along_z,))
+        perform((along_y,), (norm,), (acts.own_along_z,), (grads.own_along_z,))
         for i, zz in enumerate(near):
             if i:
-                perform((acts.along_z, zz), (grads.along_z, zz, False))
-                perform((g1, zz), (g2, zz), (g3, zz), (grads.arrived, zz))
-            perform((a1, zz, i == 0), (a2, zz), (a3, zz), (acts.arrived, zz))
-        load(0)
-        service = {(g, 1, 4): [(load, g + 1)] for g in range(depth - 1)}
+                perform((acts.along_z, zz), (grads.along_z, zz), (g1, zz), (g2, zz))
+                perform((g3y, zz), (g3x, zz), (grads.arrived_y, zz), (grads.arrived_x, zz))
+            perform((a1, zz, i == 0), (a2, zz), (a3y, zz), (a3x, zz))
+            perform((acts.arrived_y, zz), (acts.arrived_x, zz))
+        load(0, 0)
+        service = {(g, 0, 0): [(load, g, 1)] for g in range(depth)}
+        service.update({(g, 1, 4): [(load, g + 1, 0)] for g in range(depth - 1)})
 
     def group(g, carry):
         zz = p.nearest(g)
-        for copy in loads(zz, 1):
-            copy.start()
 
         def serve(j, k):
             for (at, half, place), steps in service.items():
@@ -794,7 +812,7 @@
     for k in range(7):
         save(0, 1, k).wait()
     acts.finish(range(depth), range(depth))
-    grads.finish(near[1:], near[1:])
+    grads.finish(near[1:], near)
     net.finish()
 
 

time: 588 us -> 577 us (0.981)
  Pallas kernels: 542 us -> 531 us
    pallas_call x1, Pallas kernels: 189 us -> 180 us  [run_moe(): pl.pallas_call(functools.partial(moe_kernel, depth, capacity, experts, bl...]
where the time goes in v4:
time: 577 us; the launch traced here: 569 us
  Pallas kernels  531 us (92%)
  other arithmetic  25.1 us (4%)
  local copies, waits for them, and re-layouts  8.22 us (1%)
    pallas_call x1, Pallas kernels, run_moe(): pl.pallas_call(functools.partial(moe_kernel, depth, capacity, experts, bl...  180 us
    pallas_call x1, Pallas kernels, first_gather(): pl.pallas_call(functools.partial(first_kernel, depth), out_shape=[shape((...  101 us
    pallas_call x1, Pallas kernels, attend_back(): pl.pallas_call(functools.partial(attend_back_kernel, depth), out_shape=[s...  89.7 us
    pallas_call x1, Pallas kernels, last_reduce(): pl.pallas_call(functools.partial(last_kernel, depth), out_shape=[shape((w...  80.3 us
    pallas_call x1, Pallas kernels, reduce_back(): pl.pallas_call(functools.partial(back_kernel, depth), out_shape=[shape((r...  79.9 us

profile of v4, /device:TPU:2, one launch (start us, length us, event | category | flops | bytes accessed | tf_op | source)
XLA Modules:
  0.0 568.5 jit_solution(16235334899907989723)
XLA Ops:
  0.7 0.1 pad.12.clone
  0.7 0.7 fusion.7
  1.4 0.1 copy.60
  1.6 0.1 convolution_select_fusion
  1.7 0.1 copy.58
  1.8 0.8 maximum_maximum_fusion
  2.6 101.5 %first_gather.1 = (bf16[3,8,256,512]{3,2,1,0:T(8,128)(2,1)}, bf16[512,2048]{1,0:T(8,128)(2,1)}, bf16[4,128,2048]{2,1,0:T(8,128)(2,1)}, bf16[512,2048]{1,0:T(8,12...) custom-call(bf16[256,512]{1,0:T(8,128)(2,1)} %wq.1, ...), custom_call_target="tpu_custom_call" | custom-call | tf_op jit(solution)/shard_map/first_gather/pallas_call | solution.py:519
  104.1 179.9 %moe.1 = (f32[128,2048]{1,0:T(8,128)}, f32[128,128]{1,0:T(8,128)}, bf16[32,128,2176]{2,1,0:T(8,128)(2,1)}, bf16[32,128,2048]{2,1,0:T(8,128)(2,1)}, bf16[32,128,2...) custom-call(bf16[2,2,128,2048]{3,2,1,0:T(8,128)(2,1)} %bitcast.24, ...), custom_call_target="tpu_custom_call", output_to_operand_aliasing={{3}: (10, {})} | custom-call | tf_op jit(solution)/shard_map/moe/pallas_call | solution.py:833
  283.9 0.0 copy-start.1
  283.9 0.0 copy-start.6
  284.0 0.0 copy-start.7
  284.0 0.0 copy-start.9
  284.0 79.9 %reduce_back.1 = (f32[128,2176]{1,0:T(8,128)}, bf16[4,2,2,128,2048]{4,3,2,1,0:T(8,128)(2,1)}, bf16[4,2048,256]{2,1,0:T(8,128)(2,1)}, bf16[4,2048,256]{2,1,0:T(8,128)(2,1)}, bf16[4,256,2048]{2,1,0:T(8,128)(2,1)}) custom-call(bf16[4,2,2,2,128,2176]{5,4,3,2,1,0:T(8,128)(2,1)} %bitcast.20, bf16[4,2,2,2,128,2048]{5,4,3,2,1,0:T(8,128)(2,1)} %bitcast.18, ...), custom_call_target="tpu_custom_call" | custom-call | tf_op jit(solution)/shard_map/reduce_back/pallas_call | solution.py:1130
  363.9 0.0 copy-start.2
  363.9 0.0 copy-done.1
  363.9 0.2 multiply_reduce_fusion.2
  364.1 0.9 slice.20
  365.0 0.1 copy.62
  365.1 0.1 copy.64
  365.2 0.0 copy-done.6
  365.2 0.1 multiply_reduce_fusion.3
  365.3 0.0 copy-done.7
  365.3 0.0 copy-done.9
  365.3 2.1 multiply_reduce_fusion
  367.4 0.5 convolution_convert_fusion
  367.9 0.3 copy.70
  368.2 1.8 concatenate.28
  370.0 0.0 copy-done.2
  370.0 1.5 fusion.8
  371.5 89.7 %attend_back.1 = (bf16[8,256,1536]{2,1,0:T(8,128)(2,1)}, bf16[512,2048]{1,0:T(8,128)(2,1)}, f32[1,2048]{1,0:T(1,128)}, f32[256,256]{1,0:T(8,128)}, bf16[256,2048]{1,0:T(8,128)(2,1)}, /*index=5*/f32[128,2048]{1,0:T(8,128)}) custom-call(bf16[128,2048]{1,0:T(8,128)(2,1)} %get-tuple-element.144.mine, bf16[512,2048]{1,0:T(8,128)(2,1)} %get-tuple-element.58.act_hbm, ...), custom_call_target="tpu_custom_call" | custom-call | tf_op jit(solution)/shard_map/attend_back/pallas_call | solution.py:1359
  461.3 0.0 copy-start
  461.3 2.5 add_convert_fusion
  463.8 0.7 convert_reduce_fusion
  464.5 1.0 concatenate.27
  465.5 1.6 fusion.4
  467.2 0.0 copy-done
  467.2 0.0 copy-start.5
  467.2 0.0 copy-start.8
  467.2 80.3 %last_reduce.1 = (f32[256,512]{1,0:T(8,128)S(1)}, f32[256,512]{1,0:T(8,128)S(1)}, f32[256,512]{1,0:T(8,128)S(1)}, f32[128,2048]{1,0:T(8,128)S(1)}, f32[64,128]{1,0:T(8,128)S(1)}, /*index=5*/f32[256,256]{1,0:T(8,128)S(1)}) custom-call(bf16[4,2,2,2,64,128]{5,4,3,2,1,0:T(8,128)(2,1)S(1)} %bitcast.16, bf16[4,2,256,1536]{3,2,1,0:T(8,128)(2,1)} %bitcast.21, ...), custom_call_target="tpu_custom_call" | custom-call | tf_op jit(solution)/shard_map/last_reduce/pallas_call | solution.py:1528
  547.5 0.0 copy-done.5
  547.5 1.1 add.33
  548.6 0.7 slice_reduce_fusion
  549.3 0.7 copy.68
  550.0 0.0 copy-done.8
  550.0 0.8 pad_maximum_fusion
  550.8 0.0 copy-start.4
  550.9 6.5 %convert_element_type.36 = f32[4,2048,256]{2,1,0:T(8,128)} convert(bf16[4,2048,256]{2,1,0:T(8,128)(2,1)} %get-tuple-element.77) | non-fusion elementwise | flops 2097152 | bytes 12582912 | tf_op jit(solution)/shard_map/convert_element_type | solution.py:1665
  557.3 0.0 copy-done.4
  557.3 0.0 copy-start.3
  557.3 4.1 convert_element_type.37
  561.5 0.0 copy-done.3
  561.5 4.4 convert_element_type.38
  565.9 0.8 copy.76
  566.7 0.8 copy.77
  567.5 0.8 copy.78
  (6 shorter events, 0.0 us)
Async XLA Ops:
  283.9 80.0 %copy-start.1 = (f32[128,2048]{1,0:T(8,128)S(1)}, f32[128,2048]{1,0:T(8,128)}, u32[]{:S(2)}) copy-start(f32[128,2048]{1,0:T(8,128)} %get-tuple-element.48) | copy-start | bytes 3145732
  283.9 81.2 %copy-start.6 = (f32[128,128]{1,0:T(8,128)S(1)}, f32[128,128]{1,0:T(8,128)}, u32[]{:S(2)}) copy-start(f32[128,128]{1,0:T(8,128)} %get-tuple-element.57) | copy-start | bytes 196612
  284.0 81.3 %copy-start.7 = (bf16[2048,32]{0,1:T(8,128)(2,1)S(1)}, bf16[2048,32]{0,1:T(8,128)(2,1)}, u32[]{:S(2)}) copy-start(bf16[2048,32]{0,1:T(8,128)(2,1)} %param.24) | copy-start | bytes 393220
  284.0 81.3 %copy-start.9 = (f32[2048]{0:T(1024)S(1)}, f32[2048]{0:T(1024)}, u32[]{:S(2)}) copy-start(f32[2048]{0:T(1024)} %param.23) | copy-start | bytes 24580
  363.9 6.1 %copy-start.2 = (bf16[128,2048]{1,0:T(8,128)(2,1)S(1)}, bf16[128,2048]{1,0:T(8,128)(2,1)}, u32[]{:S(2)}) copy-start(bf16[128,2048]{1,0:T(8,128)(2,1)} %og.3) | copy-start | bytes 1572868
  461.3 5.9 %copy-start = (bf16[256,2048]{1,0:T(8,128)(2,1)S(1)}, bf16[256,2048]{1,0:T(8,128)(2,1)}, u32[]{:S(2)}) copy-start(bf16[256,2048]{1,0:T(8,128)(2,1)} %get-tuple-element.69.o_part) | copy-start | bytes 3145732
  467.2 80.3 %copy-start.5 = (f32[128,2048]{1,0:T(8,128)S(1)}, f32[128,2048]{1,0:T(8,128)}, u32[]{:S(2)}) copy-start(f32[128,2048]{1,0:T(8,128)} %get-tuple-element.145) | copy-start | bytes 3145732
  467.2 82.8 %copy-start.8 = (f32[256,256]{1,0:T(8,128)S(1)}, f32[256,256]{1,0:T(8,128)}, u32[]{:S(2)}) copy-start(f32[256,256]{1,0:T(8,128)} %get-tuple-element.75) | copy-start | bytes 786436
  550.8 6.5 %copy-start.4 = (bf16[4,2048,256]{2,1,0:T(8,128)(2,1)S(1)}, bf16[4,2048,256]{2,1,0:T(8,128)(2,1)}, u32[]{:S(2)}) copy-start(bf16[4,2048,256]{2,1,0:T(8,128)(2,1)} %get-tuple-element.78) | copy-start | bytes 12582916
  557.3 4.1 copy-start.3

commit v5 on v4

--- a/solution.py
+++ b/solution.py
@@ -316,7 +316,16 @@
         self.each_z(p.z, start)
 
     def take_z(self, zz):
-        self.z_copy(zz, True).wait_recv()
+        ref = self.ref(zz, 0, 0, 0, None)
+        at = len(NAMES) * self.place.depth + zz
+        pltpu.make_async_remote_copy(
+            src_ref=ref,
+            dst_ref=ref,
+            send_sem=self.sends.at[at],
+            recv_sem=self.recvs.at[at],
+            device_id=self.place.to["c"],
+            device_id_type=MESH,
+        ).wait_recv()
 
     def along_z(self, zz):
         self.take_z(zz)
@@ -553,7 +562,7 @@
     part, inp, og, gain, router, mask, rank, gate_hbm, up_hbm, down_hbm, grad_in_hbm,
     resid, gates_out, act_all, grad_all, out_hbm, back_hbm, x_hbm, g_hbm, hid_hbm, gl_hbm, ul_hbm,
     acc, rc, ry, own, w_gate, w_up, w_down, act_in, grad_in, x_rows, g_rows, tails, hid, gl, ul,
-    o_keep, r_keep, out, back,
+    keep, out, back,
     act_send, act_recv, og_send, og_recv, send, recv, local, load_sems, save_sems,
 ):
     p = Place(depth)
@@ -668,19 +677,31 @@
 
         settle((0, 1))
 
-        def gather(b, carry):
-            hot = one_hot(j, b)
-            picked = jnp.dot(hot, act_in[j, b], preferred_element_type=F32)
-            pulled = jnp.dot(hot, grad_in[j, b], preferred_element_type=F32).astype(BF16)
-            at = pl.ds(pl.multiple_of(b * capacity, 16), capacity)
-            for e in range(local_experts):
-                piece = picked[e * capacity : (e + 1) * capacity]
-                x_rows[e, at, :] = piece[:, :width].astype(BF16)
-                tails[e, at, :] = piece[:, width:]
-                g_rows[e, at, :] = pulled[e * capacity : (e + 1) * capacity]
+        def gather(pair, carry):
+            b = pair * 2
+            blank = jnp.zeros((local_experts * capacity, rows), BF16)
+            hot = jnp.concatenate(
+                [
+                    jnp.concatenate([one_hot(j, b), blank], axis=1),
+                    jnp.concatenate([blank, one_hot(j, b + 1)], axis=1),
+                ],
+                axis=0,
+            )
+            acts_two = act_in[j, pl.ds(b, 2)].reshape(2 * rows, width + LANES)
+            grads_two = grad_in[j, pl.ds(b, 2)].reshape(2 * rows, width)
+            picked = jnp.dot(hot, acts_two, preferred_element_type=F32)
+            pulled = jnp.dot(hot, grads_two, preferred_element_type=F32).astype(BF16)
+            for k in range(2):
+                at = pl.ds(pl.multiple_of((b + k) * capacity, 16), capacity)
+                for e in range(local_experts):
+                    first = (k * local_experts + e) * capacity
+                    piece = picked[first : first + capacity]
+                    x_rows[e, at, :] = piece[:, :width].astype(BF16)
+                    tails[e, at, :] = piece[:, width:]
+                    g_rows[e, at, :] = pulled[first : first + capacity]
             return carry
 
-        lax.fori_loop(0, blocks, gather, 0)
+        lax.fori_loop(0, blocks // 2, gather, 0)
         for k in (0, 1):
             save(zz, j, k).start()
         serve(0)
@@ -712,9 +733,9 @@
             for b in range(blocks):
                 at = slice(b * capacity, (b + 1) * capacity)
                 to = slice(e * capacity, (e + 1) * capacity)
-                o_keep[b, to, :] = o_rows[at]
-                r_keep[b, to, pl.ds(0, width)] = r_rows[at]
-                r_keep[b, to, pl.ds(width, LANES)] = r_tail[at]
+                keep[b, to, pl.ds(0, width)] = o_rows[at]
+                keep[b, to, pl.ds(width, width)] = r_rows[at]
+                keep[b, to, pl.ds(2 * width, LANES)] = r_tail[at]
             serve(1 + e)
         for k in (2, 3, 4):
             save(zz, j, k).start()
@@ -722,12 +743,9 @@
 
         def combine(b, carry):
             hot = one_hot(j, b)
-            out[b] = lax.dot_general(
-                hot, o_keep[b], CONTRACT_FIRST, preferred_element_type=F32
-            ).astype(BF16)
-            back[b] = lax.dot_general(
-                hot, r_keep[b], CONTRACT_FIRST, preferred_element_type=F32
-            ).astype(BF16)
+            found = lax.dot_general(hot, keep[b], CONTRACT_FIRST, preferred_element_type=F32)
+            out[b] = found[:, :width].astype(BF16)
+            back[b] = found[:, width:].astype(BF16)
             return carry
 
         lax.fori_loop(0, blocks, combine, 0)
@@ -860,8 +878,7 @@
             pltpu.VMEM((local_experts, slots, hidden), BF16),
             pltpu.VMEM((local_experts, slots, hidden), BF16),
             pltpu.VMEM((local_experts, slots, hidden), BF16),
-            pltpu.VMEM((blocks, local_experts * capacity, width), BF16),
-            pltpu.VMEM((blocks, local_experts * capacity, wide), BF16),
+            pltpu.VMEM((blocks, local_experts * capacity, width + wide), BF16),
             pltpu.VMEM((blocks, rows, width), BF16),
             pltpu.VMEM((blocks, rows, wide), BF16),
         ]
@@ -1159,15 +1176,15 @@
 
 
 def attend_back_kernel(
-    depth, mine, act_hbm, wqkv_hbm, wo_hbm, qkv_hbm, att_hbm, whole_hbm, seg_row, gain, out_part, out_other,
-    qkv_part, whole_part, gain_part, o_sum, o_rest, out_sum,
+    depth, mine, act_hbm, wqkv_hbm, wo_hbm, qkv_hbm, att_hbm, whole_hbm, seg_row, gain, resid, out_part, out_other,
+    qkv_part, whole_part, gain_part, o_sum, o_rest, output,
     acc, ya, xa, xb, yb, inbox, z_inbox, xc, yc, other, bg, act, wqkv, wo, qkv, att, ag, low, o_acc, o_inbox, o_rx,
     whole, act_grad, send, recv, local, other_sems,
 ):
     p = Place(depth)
     net = Net(p, send, recv, local)
     x, y, c = p.x, p.y, p.c
-    rows, width = out_sum.shape
+    rows, width = output.shape
     seq = act.shape[0]
     cols = wo.shape[0]
     heads = cols // HEAD
@@ -1323,19 +1340,26 @@
     one, two, three, along_z = flow.one, flow.two, flow.three, flow.along_z
     if depth == 4 and heads == 4:
         perform(
-            (one, 0), (one, 1), (one, 2), (along_z, 0), (along_z, 1), (rows_in,),
-            (attended_grad,), (o_terms,), (o_step, 0), (along_z, 2), (two, 0), (head, 0),
-            (two, 1), (one, 3), (o_step, 1), (o_step, 2), (head, 1), (head, 2), (head, 3),
-            (two, 2), (three, 0), (w_piece, 0), (o_step, 3), (w_piece, 1), (along_z, 3),
-            (flow.then_x,), (o_along_x,), (w_piece, 2), (three, 1), (three, 2), (flow.then_y,),
-            (w_piece, 3), (norm_piece, 0), (norm_piece, 1), (two, 3), (norm_piece, 2), (flow.end,), (norm_piece, 3), (three, 3),
+            (one, 0), (along_z, 0), (one, 1), (along_z, 1), (rows_in,), (attended_grad,),
+            (o_terms,), (o_step, 0), (two, 0), (one, 2), (along_z, 2), (head, 0), (head, 1),
+            (o_step, 1), (o_step, 2), (two, 1), (head, 2), (head, 3), (one, 3), (along_z, 3),
+            (three, 0), (w_piece, 0), (two, 2), (o_step, 3), (flow.then_x,), (w_piece, 1),
+            (three, 1), (three, 2), (o_along_x,), (two, 3), (w_piece, 2), (flow.then_y,),
+            (w_piece, 3), (norm_piece, 0), (norm_piece, 1), (norm_piece, 2), (three, 3),
+            (norm_piece, 3), (flow.end,),
         )
     else:
         perform(*every(depth, one), (rows_in,), (attended_grad,), (o_terms,))
         perform(*every(heads, head), *every(pieces, w_piece, norm_piece))
         perform(*every(depth, two, three, along_z, o_step), (o_along_x,))
         perform((flow.then_x,), (flow.then_y,), (flow.end,))
-    widen(out_sum, acc.at[p.z, x, y], rows)
+
+    def add_resid(i, carry):
+        at = pl.ds(pl.multiple_of(i * 16, 16), 16)
+        output[at, :] = (resid[at, :] + acc[p.z, x, y, at, :].astype(F32)).astype(BF16)
+        return carry
+
+    lax.fori_loop(0, rows // 16, add_resid, 0)
     net.got(o_rx, ("ox",))
     at_o = pl.ds(pl.multiple_of((p.z * 2 + x) * o_cols, LANES), o_cols)
 
@@ -1349,7 +1373,7 @@
 
 
 def attend_back(
-    depth, mine, act, wqkv, wo, qkv, att, whole, segments, gain, out_part, out_other, o_cols
+    depth, mine, act, wqkv, wo, qkv, att, whole, segments, gain, resid, out_part, out_other, o_cols
 ):
     rows, width = mine.shape
     seq, cols = att.shape
@@ -1364,9 +1388,9 @@
             shape((1, width), F32),
             shape((cols // 2, o_cols), F32),
             shape((cols // 2, width), BF16),
-            shape((rows, width), F32),
+            shape((rows, width), BF16),
         ],
-        in_specs=[ANY] * 7 + [VMEM] * 2 + [ANY] * 2,
+        in_specs=[ANY] * 7 + [VMEM] * 3 + [ANY] * 2,
         out_specs=[VMEM] * 6,
         scratch_shapes=reduce_scratch(
             depth, rows, width, [tile_rows(rows, 0.375), tile_rows(rows, 0.5)]
@@ -1392,7 +1416,7 @@
         compiler_params=comm_params(4, 63),
         name="attend_back",
     )(
-        mine, act, wqkv, wo, qkv, att, whole, segments[None, :], gain[None, :],
+        mine, act, wqkv, wo, qkv, att, whole, segments[None, :], gain[None, :], resid,
         out_part.reshape(depth, 2, 2, 2, rows, width), out_other,
     )
 
@@ -1636,9 +1660,10 @@
     )
     resid_part, gain_two_part = norm_back(resid, inverse_two, moe_gain, act_two_grad)
     resid_grad = out_grad.astype(F32) + resid_part
-    qkv_part, whole_part, gain_one_part, o_first, o_rest, out_sum = attend_back(
+    qkv_part, whole_part, gain_one_part, o_first, o_rest, output = attend_back(
         depth, resid_grad.astype(BF16), act_one, qkv_full, full_output, qkv, attended,
-        whole.reshape(seq, width), segments, attn_gain, out_part, out_other, w_output.shape[1],
+        whole.reshape(seq, width), segments, attn_gain, resid, out_part, out_other,
+        w_output.shape[1],
     )
     count = fsdp * tp
     piece = width // count
@@ -1649,7 +1674,6 @@
         depth, tail, qkv_part, whole_part.reshape(tp, rows, width), o_rest
     )
     o_sum = jnp.concatenate([o_first, o_second], axis=0)
-    output = (resid + out_sum).astype(BF16)
     input_grad = resid_grad + row_sum
     side = side[:piece]
     return (

time: 577 us -> 573 us (level)
  no operation moved by 1% of the time
where the time goes in v5:
time: 573 us; the launch traced here: 566 us
  Pallas kernels  529 us (92%)
  other arithmetic  22.6 us (4%)
  local copies, waits for them, and re-layouts  10.2 us (2%)
    pallas_call x1, Pallas kernels, run_moe(): pl.pallas_call(functools.partial(moe_kernel, depth, capacity, experts, bl...  179 us
    pallas_call x1, Pallas kernels, first_gather(): pl.pallas_call(functools.partial(first_kernel, depth), out_shape=[shape((...  101 us
    pallas_call x1, Pallas kernels, attend_back(): pl.pallas_call(functools.partial(attend_back_kernel, depth), out_shape=[s...  87.9 us
    pallas_call x1, Pallas kernels, last_reduce(): pl.pallas_call(functools.partial(last_kernel, depth), out_shape=[shape((w...  81 us
    pallas_call x1, Pallas kernels, reduce_back(): pl.pallas_call(functools.partial(back_kernel, depth), out_shape=[shape((r...  79.9 us

profile of v5, /device:TPU:2, one launch (start us, length us, event | category | flops | bytes accessed | tf_op | source)
XLA Modules:
  0.0 565.5 jit_solution(7801398685554477310)
XLA Ops:
  0.7 0.1 pad.12.clone
  0.7 0.7 fusion.7
  1.4 0.1 copy.60
  1.6 0.1 convolution_select_fusion
  1.7 0.1 copy.58
  1.8 0.8 maximum_maximum_fusion
  2.6 101.5 %first_gather.1 = (bf16[3,8,256,512]{3,2,1,0:T(8,128)(2,1)}, bf16[512,2048]{1,0:T(8,128)(2,1)}, bf16[4,128,2048]{2,1,0:T(8,128)(2,1)}, bf16[512,2048]{1,0:T(8,12...) custom-call(bf16[256,512]{1,0:T(8,128)(2,1)} %wq.1, ...), custom_call_target="tpu_custom_call" | custom-call | tf_op jit(solution)/shard_map/first_gather/pallas_call | solution.py:528
  104.1 178.7 %moe.1 = (f32[128,2048]{1,0:T(8,128)}, f32[128,128]{1,0:T(8,128)}, bf16[32,128,2176]{2,1,0:T(8,128)(2,1)}, bf16[32,128,2048]{2,1,0:T(8,128)(2,1)}, bf16[32,128,2...) custom-call(bf16[2,2,128,2048]{3,2,1,0:T(8,128)(2,1)} %bitcast.24, ...), custom_call_target="tpu_custom_call", output_to_operand_aliasing={{3}: (10, {})} | custom-call | tf_op jit(solution)/shard_map/moe/pallas_call | solution.py:851
  282.8 0.0 copy-start.1
  282.8 0.0 copy-start.6
  282.8 0.0 copy-start.7
  282.8 0.0 copy-start.10
  282.8 79.9 %reduce_back.1 = (f32[128,2176]{1,0:T(8,128)}, bf16[4,2,2,128,2048]{4,3,2,1,0:T(8,128)(2,1)}, bf16[4,2048,256]{2,1,0:T(8,128)(2,1)}, bf16[4,2048,256]{2,1,0:T(8,128)(2,1)}, bf16[4,256,2048]{2,1,0:T(8,128)(2,1)}) custom-call(bf16[4,2,2,2,128,2176]{5,4,3,2,1,0:T(8,128)(2,1)} %bitcast.20, bf16[4,2,2,2,128,2048]{5,4,3,2,1,0:T(8,128)(2,1)} %bitcast.18, ...), custom_call_target="tpu_custom_call" | custom-call | tf_op jit(solution)/shard_map/reduce_back/pallas_call | solution.py:1147
  362.7 0.0 copy-start.2
  362.7 0.0 copy-done.1
  362.7 0.2 multiply_reduce_fusion.2
  362.9 0.9 slice.20
  363.8 0.1 copy.62
  363.9 0.1 copy.64
  364.0 0.0 copy-done.6
  364.0 0.1 multiply_reduce_fusion.3
  364.1 0.0 copy-done.7
  364.1 0.0 copy-done.10
  364.1 2.1 multiply_reduce_fusion
  366.2 0.5 convolution_convert_fusion
  366.7 0.3 copy.70
  367.0 1.8 concatenate.28
  368.8 0.0 copy-done.2
  368.8 1.5 fusion.8
  370.3 87.9 %attend_back.1 = (bf16[8,256,1536]{2,1,0:T(8,128)(2,1)}, bf16[512,2048]{1,0:T(8,128)(2,1)}, f32[1,2048]{1,0:T(1,128)}, f32[256,256]{1,0:T(8,128)}, bf16[256,2048]{1,0:T(8,128)(2,1)}, /*index=5*/bf16[128,2048]{1,0:T(8,128)(2,1)}) custom-call(bf16[128,2048]{1,0:T(8,128)(2,1)} %get-tuple-element.144.mine, bf16[512,2048]{1,0:T(8,128)(2,1)} %get-tuple-element.58.act_hbm, ...), custom_call_target="tpu_custom_call" | custom-call | tf_op jit(solution)/shard_map/attend_back/pallas_call | solution.py:1383
  458.2 0.7 convert_reduce_fusion
  458.9 1.0 concatenate.27
  459.9 1.6 fusion.4
  461.5 0.0 copy-start
  461.6 1.2 copy-done
  462.8 0.0 copy-start.5
  462.8 0.0 copy-start.9
  462.8 81.0 %last_reduce.1 = (f32[256,512]{1,0:T(8,128)S(1)}, f32[256,512]{1,0:T(8,128)S(1)}, f32[256,512]{1,0:T(8,128)S(1)}, f32[128,2048]{1,0:T(8,128)S(1)}, f32[64,128]{1,0:T(8,128)S(1)}, /*index=5*/f32[256,256]{1,0:T(8,128)S(1)}) custom-call(bf16[4,2,2,2,64,128]{5,4,3,2,1,0:T(8,128)(2,1)S(1)} %bitcast.16, bf16[4,2,256,1536]{3,2,1,0:T(8,128)(2,1)} %bitcast.21, ...), custom_call_target="tpu_custom_call" | custom-call | tf_op jit(solution)/shard_map/last_reduce/pallas_call | solution.py:1552
  543.7 0.0 copy-done.5
  543.8 1.1 add.29
  544.9 0.7 slice_reduce_fusion
  545.6 0.7 copy.68
  546.2 0.0 copy-done.9
  546.2 0.8 pad_maximum_fusion
  547.1 0.0 copy-start.4
  547.1 6.5 %convert_element_type.32 = f32[4,2048,256]{2,1,0:T(8,128)} convert(bf16[4,2048,256]{2,1,0:T(8,128)(2,1)} %get-tuple-element.77) | non-fusion elementwise | flops 2097152 | bytes 12582912 | tf_op jit(solution)/shard_map/convert_element_type | solution.py:1689
  553.5 0.0 copy-done.4
  553.5 0.0 copy-start.3
  553.5 4.1 convert_element_type.33
  557.7 0.0 copy-done.3
  557.7 0.0 copy-start.8
  557.7 4.4 convert_element_type.34
  562.1 0.0 copy-done.8
  562.1 0.8 copy.77
  562.9 0.8 copy.78
  563.7 0.8 copy.79
  564.5 0.8 copy.80
  (6 shorter events, 0.0 us)
Async XLA Ops:
  282.8 80.0 %copy-start.1 = (f32[128,2048]{1,0:T(8,128)S(1)}, f32[128,2048]{1,0:T(8,128)}, u32[]{:S(2)}) copy-start(f32[128,2048]{1,0:T(8,128)} %get-tuple-element.48.resid) | copy-start | bytes 3145732
  282.8 81.2 %copy-start.6 = (f32[128,128]{1,0:T(8,128)S(1)}, f32[128,128]{1,0:T(8,128)}, u32[]{:S(2)}) copy-start(f32[128,128]{1,0:T(8,128)} %get-tuple-element.57) | copy-start | bytes 196612
  282.8 81.3 %copy-start.7 = (bf16[2048,32]{0,1:T(8,128)(2,1)S(1)}, bf16[2048,32]{0,1:T(8,128)(2,1)}, u32[]{:S(2)}) copy-start(bf16[2048,32]{0,1:T(8,128)(2,1)} %param.24) | copy-start | bytes 393220
  282.8 81.3 %copy-start.10 = (f32[2048]{0:T(1024)S(1)}, f32[2048]{0:T(1024)}, u32[]{:S(2)}) copy-start(f32[2048]{0:T(1024)} %param.23) | copy-start | bytes 24580
  362.7 6.1 %copy-start.2 = (bf16[128,2048]{1,0:T(8,128)(2,1)S(1)}, bf16[128,2048]{1,0:T(8,128)(2,1)}, u32[]{:S(2)}) copy-start(bf16[128,2048]{1,0:T(8,128)(2,1)} %og.3) | copy-start | bytes 1572868
  461.5 1.2 copy-start
  462.8 81.0 %copy-start.5 = (f32[128,2048]{1,0:T(8,128)S(1)}, f32[128,2048]{1,0:T(8,128)}, u32[]{:S(2)}) copy-start(f32[128,2048]{1,0:T(8,128)} %get-tuple-element.145) | copy-start | bytes 3145732
  462.8 83.5 %copy-start.9 = (f32[256,256]{1,0:T(8,128)S(1)}, f32[256,256]{1,0:T(8,128)}, u32[]{:S(2)}) copy-start(f32[256,256]{1,0:T(8,128)} %get-tuple-element.75) | copy-start | bytes 786436
  547.1 6.5 %copy-start.4 = (bf16[4,2048,256]{2,1,0:T(8,128)(2,1)S(1)}, bf16[4,2048,256]{2,1,0:T(8,128)(2,1)}, u32[]{:S(2)}) copy-start(bf16[4,2048,256]{2,1,0:T(8,128)(2,1)} %get-tuple-element.78) | copy-start | bytes 12582916
  553.5 4.1 copy-start.3
  557.7 4.5 copy-start.8

commit v6 on v5

--- a/solution.py
+++ b/solution.py
@@ -341,6 +341,13 @@
         self.copy("x3", zz, part_b).start()
         self.copy("y3", zz, part_a).start()
         self.copy("c0", zz, whole).start()
+
+    def first_of_own(self, part):
+        zz, rows = self.place.z, self.own.at[pl.ds(part * self.half, self.half)]
+        self.copy("y1" if part else "x1", zz, rows).start()
+        self.copy("x3" if part else "y3", zz, rows).start()
+        if part:
+            self.copy("c0", zz, self.own).start()
 
     def second(self, zz):
         self.take("x1", zz)
@@ -581,20 +588,25 @@
     net.put(part.at[:, 1 - p.c], rc, "c", ("rc",))
     far = 1 - p.y
 
+    half = rows // 2
+
     def along_y():
         part_in.wait()
         net.got(rc, ("rc",))
-        add_rows(acc.at[far], rc.at[far], rows)
-        net.put(acc.at[far], ry, "y", ("ry",))
+        for i in range(2):
+            at = pl.ds(i * half, half)
+            add_rows(acc.at[far, at], rc.at[far, at], half)
+            net.put(acc.at[far, at], ry.at[at], "y", ("ry", i))
         add_rows(acc.at[p.y], rc.at[p.y], rows)
 
     kept = []
 
-    def norm():
-        net.got(ry, ("ry",))
+    def norm(part_of):
+        here = pl.ds(part_of * half, half)
+        net.got(ry.at[here], ("ry", part_of))
 
         def body(i, carry):
-            at = pl.ds(pl.multiple_of(i * 16, 16), 16)
+            at = pl.ds(pl.multiple_of(part_of * half + i * 16, 16), 16)
             branch = acc[p.y, at, :].astype(F32) + ry[at, :].astype(F32)
             values = inp[at, :].astype(F32) + branch
             resid[at, :] = values
@@ -602,26 +614,27 @@
             own[at, pl.ds(0, width)] = (values * inverse * gain[...]).astype(BF16)
             return carry
 
-        lax.fori_loop(0, rows // 16, body, 0)
+        lax.fori_loop(0, half // 16, body, 0)
         twice = jnp.concatenate(
             [router[...]] * 2 + [jnp.zeros((LANES - 2 * experts, width), BF16)], axis=0
         )
         logits = lax.dot_general(
-            own[:, pl.ds(0, width)], twice, CONTRACT_LAST, preferred_element_type=F32
+            own[here, pl.ds(0, width)], twice, CONTRACT_LAST, preferred_element_type=F32
         )
-        chosen = mask[...] > 0.0
+        chosen = mask[here, :] > 0.0
         peak = jnp.max(jnp.where(chosen, logits, -1e30), axis=1, keepdims=True)
         expo = jnp.where(chosen, jnp.exp(jnp.minimum(logits - peak, 0.0)), 0.0)
         lane = lax.broadcasted_iota(jnp.int32, expo.shape, 1)
         total = jnp.sum(jnp.where(lane < experts, expo, 0.0), axis=1, keepdims=True)
         gates = expo / total
-        gates_out[...] = gates
+        gates_out[here, :] = gates
         high = gates.astype(BF16).astype(F32)
         tail = jnp.where(
-            lane < experts, high, jnp.where(lane < 2 * experts, gates - high, rank[...])
+            lane < experts, high, jnp.where(lane < 2 * experts, gates - high, rank[here, :])
         )
-        own[:, pl.ds(width, LANES)] = tail.astype(BF16)
-        kept.append(net.local(own, acts.ref(p.z, 0, 0, 0, None)))
+        own[here, pl.ds(width, LANES)] = tail.astype(BF16)
+        if part_of == 1:
+            kept.append(net.local(own, acts.ref(p.z, 0, 0, 0, None)))
 
     first_expert = p.f * local_experts
     tp_lane = p.t * experts + first_expert
@@ -766,44 +779,40 @@
     a1, a2, a3y, a3x = acts.first, acts.second, acts.third_y, acts.third_x
     if depth == 4:
         perform(
-            (grads.own_along_z,), (along_y,), (grads.along_z, near[1]), (g1, near[1]), (norm,),
-            (acts.own_along_z,), (a1, p.z, True), (a2, p.z), (acts.along_z, near[1]), (a3y, p.z),
-            (a1, near[1]), (acts.arrived_y, p.z), (load, 0, 0), (g2, near[1]),
-            (grads.along_z, near[2]), (g1, near[2]),
+            (along_y,), (grads.own_along_z,), (norm, 0), (acts.first_of_own, 0), (norm, 1),
+            (acts.own_along_z,), (acts.first_of_own, 1), (grads.along_z, near[1]), (g1, near[1]),
+            (a2, p.z), (a3y, p.z), (grads.along_z, near[2]), (acts.arrived_y, p.z), (load, 0, 0),
+            (acts.along_z, near[1]), (a1, near[1]), (g2, near[1]),
         )
         service = {
-            (0, 0, 1): [(a3x, p.z)],
-            (0, 0, 3): [(acts.arrived_x, p.z), (load, 0, 1)],
-            (0, 0, 4): [(acts.along_z, near[2])],
-            (0, 0, 5): [(a2, near[1])],
-            (0, 1, 0): [(a1, near[2]), (g3y, near[1])],
-            (0, 1, 2): [(a3y, near[1])],
-            (0, 1, 3): [
-                (acts.arrived_y, near[1]), (grads.along_z, near[3]), (grads.arrived_y, near[1]),
-                (load, 1, 0),
-            ],
-            (1, 0, 0): [(g2, near[2])],
-            (1, 0, 1): [(g3x, near[1]), (g3y, near[2])],
-            (1, 0, 2): [(g1, near[3])],
-            (1, 0, 3): [(a3x, near[1])],
-            (1, 0, 4): [
-                (acts.along_z, near[3]), (a2, near[2]), (a3y, near[2]), (acts.arrived_x, near[1]),
-                (grads.arrived_x, near[1]), (load, 1, 1),
-            ],
-            (1, 0, 5): [(g3x, near[2])],
-            (1, 1, 3): [(grads.arrived_y, near[2]), (acts.arrived_y, near[2]), (load, 2, 0)],
-            (1, 1, 4): [(a1, near[3])],
-            (2, 0, 0): [(a3x, near[2])],
-            (2, 0, 3): [(g2, near[3]), (grads.arrived_x, near[2])],
-            (2, 0, 4): [(g3y, near[3]), (a2, near[3]), (acts.arrived_x, near[2]), (load, 2, 1)],
-            (2, 0, 5): [(a3y, near[3])],
-            (2, 1, 1): [(acts.arrived_y, near[3]), (grads.arrived_y, near[3]), (load, 3, 0)],
-            (3, 0, 0): [(a3x, near[3])],
-            (3, 0, 1): [(g3x, near[3])],
-            (3, 0, 4): [(grads.arrived_x, near[3]), (acts.arrived_x, near[3]), (load, 3, 1)],
+            (0, 0, 0): [(g1, near[2])],
+            (0, 0, 3): [(acts.along_z, near[2])],
+            (0, 0, 4): [(a3x, p.z), (acts.arrived_x, p.z), (load, 0, 1)],
+            (0, 1, 1): [(grads.along_z, near[3])],
+            (0, 1, 2): [(a2, near[1])],
+            (0, 1, 3): [(a3y, near[1]), (g3y, near[1]), (a1, near[2])],
+            (0, 1, 4): [(grads.arrived_y, near[1]), (acts.arrived_y, near[1]), (load, 1, 0)],
+            (1, 0, 0): [(g1, near[3]), (g3x, near[1])],
+            (1, 0, 2): [(acts.along_z, near[3])],
+            (1, 0, 3): [(g2, near[2]), (a3x, near[1]), (grads.arrived_x, near[1])],
+            (1, 0, 4): [(a2, near[2]), (acts.arrived_x, near[1]), (load, 1, 1)],
+            (1, 1, 0): [(a3y, near[2])],
+            (1, 1, 2): [(g3y, near[2])],
+            (1, 1, 3): [(acts.arrived_y, near[2])],
+            (1, 1, 4): [(grads.arrived_y, near[2]), (load, 2, 0)],
+            (2, 0, 1): [(a1, near[3]), (g3x, near[2]), (g2, near[3])],
+            (2, 0, 2): [(g3y, near[3])],
+            (2, 0, 3): [(a3x, near[2]), (grads.arrived_x, near[2])],
+            (2, 0, 4): [(acts.arrived_x, near[2]), (load, 2, 1)],
+            (2, 1, 2): [(a2, near[3])],
+            (2, 1, 3): [(a3y, near[3])],
+            (2, 1, 4): [(acts.arrived_y, near[3]), (grads.arrived_y, near[3]), (load, 3, 0)],
+            (3, 0, 0): [(g3x, near[3])],
+            (3, 0, 2): [(grads.arrived_x, near[3]), (a3x, near[3])],
+            (3, 0, 4): [(acts.arrived_x, near[3]), (load, 3, 1)],
         }
     else:
-        perform((along_y,), (norm,), (acts.own_along_z,), (grads.own_along_z,))
+        perform((along_y,), (norm, 0), (norm, 1), (acts.own_along_z,), (grads.own_along_z,))
         for i, zz in enumerate(near):
             if i:
                 perform((acts.along_z, zz), (grads.along_z, zz), (g1, zz), (g2, zz))

time: 573 us -> 567 us (0.990)
  Pallas kernels: 529 us -> 522 us
    pallas_call x1, Pallas kernels: 179 us -> 172 us  [run_moe(): pl.pallas_call(functools.partial(moe_kernel, depth, capacity, experts, bl...]
where the time goes in v6:
time: 567 us; the launch traced here: 558 us
  Pallas kernels  522 us (92%)
  other arithmetic  22.6 us (4%)
  local copies, waits for them, and re-layouts  10.2 us (2%)
    pallas_call x1, Pallas kernels, run_moe(): pl.pallas_call(functools.partial(moe_kernel, depth, capacity, experts, bl...  172 us
    pallas_call x1, Pallas kernels, first_gather(): pl.pallas_call(functools.partial(first_kernel, depth), out_shape=[shape((...  101 us
    pallas_call x1, Pallas kernels, attend_back(): pl.pallas_call(functools.partial(attend_back_kernel, depth), out_shape=[s...  86.8 us
    pallas_call x1, Pallas kernels, last_reduce(): pl.pallas_call(functools.partial(last_kernel, depth), out_shape=[shape((w...  82.5 us
    pallas_call x1, Pallas kernels, reduce_back(): pl.pallas_call(functools.partial(back_kernel, depth), out_shape=[shape((r...  79.2 us

profile of v6, /device:TPU:2, one launch (start us, length us, event | category | flops | bytes accessed | tf_op | source)
XLA Modules:
  0.0 558.1 jit_solution(8006586198260784623)
XLA Ops:
  0.7 0.1 pad.12.clone
  0.7 0.7 fusion.7
  1.4 0.1 copy.60
  1.6 0.1 convolution_select_fusion
  1.7 0.1 copy.58
  1.8 0.8 maximum_maximum_fusion
  2.6 101.5 %first_gather.1 = (bf16[3,8,256,512]{3,2,1,0:T(8,128)(2,1)}, bf16[512,2048]{1,0:T(8,128)(2,1)}, bf16[4,128,2048]{2,1,0:T(8,128)(2,1)}, bf16[512,2048]{1,0:T(8,12...) custom-call(bf16[256,512]{1,0:T(8,128)(2,1)} %wq.1, ...), custom_call_target="tpu_custom_call" | custom-call | tf_op jit(solution)/shard_map/first_gather/pallas_call | solution.py:535
  104.1 171.6 %moe.1 = (f32[128,2048]{1,0:T(8,128)}, f32[128,128]{1,0:T(8,128)}, bf16[32,128,2176]{2,1,0:T(8,128)(2,1)}, bf16[32,128,2048]{2,1,0:T(8,128)(2,1)}, bf16[32,128,2...) custom-call(bf16[2,2,128,2048]{3,2,1,0:T(8,128)(2,1)} %bitcast.24, ...), custom_call_target="tpu_custom_call", output_to_operand_aliasing={{3}: (10, {})} | custom-call | tf_op jit(solution)/shard_map/moe/pallas_call | solution.py:860
  275.6 0.0 copy-start.1
  275.6 0.0 copy-start.6
  275.7 0.0 copy-start.7
  275.7 0.0 copy-start.10
  275.7 79.2 %reduce_back.1 = (f32[128,2176]{1,0:T(8,128)}, bf16[4,2,2,128,2048]{4,3,2,1,0:T(8,128)(2,1)}, bf16[4,2048,256]{2,1,0:T(8,128)(2,1)}, bf16[4,2048,256]{2,1,0:T(8,128)(2,1)}, bf16[4,256,2048]{2,1,0:T(8,128)(2,1)}) custom-call(bf16[4,2,2,2,128,2176]{5,4,3,2,1,0:T(8,128)(2,1)} %bitcast.20, bf16[4,2,2,2,128,2048]{5,4,3,2,1,0:T(8,128)(2,1)} %bitcast.18, ...), custom_call_target="tpu_custom_call" | custom-call | tf_op jit(solution)/shard_map/reduce_back/pallas_call | solution.py:1156
  354.9 0.0 copy-start.2
  354.9 0.0 copy-done.1
  354.9 0.2 multiply_reduce_fusion.2
  355.1 0.9 slice.20
  355.9 0.1 copy.62
  356.0 0.1 copy.64
  356.1 0.0 copy-done.6
  356.1 0.1 multiply_reduce_fusion.3
  356.3 0.0 copy-done.7
  356.3 0.0 copy-done.10
  356.3 2.1 multiply_reduce_fusion
  358.4 0.5 convolution_convert_fusion
  358.9 0.3 copy.70
  359.2 1.8 concatenate.28
  361.0 0.0 copy-done.2
  361.0 1.5 fusion.8
  362.5 86.8 %attend_back.1 = (bf16[8,256,1536]{2,1,0:T(8,128)(2,1)}, bf16[512,2048]{1,0:T(8,128)(2,1)}, f32[1,2048]{1,0:T(1,128)}, f32[256,256]{1,0:T(8,128)}, bf16[256,2048]{1,0:T(8,128)(2,1)}, /*index=5*/bf16[128,2048]{1,0:T(8,128)(2,1)}) custom-call(bf16[128,2048]{1,0:T(8,128)(2,1)} %get-tuple-element.144.mine, bf16[512,2048]{1,0:T(8,128)(2,1)} %get-tuple-element.58.act_hbm, ...), custom_call_target="tpu_custom_call" | custom-call | tf_op jit(solution)/shard_map/attend_back/pallas_call | solution.py:1392
  449.3 0.7 convert_reduce_fusion
  450.0 1.0 concatenate.27
  451.0 1.6 fusion.4
  452.6 0.0 copy-start
  452.6 1.2 copy-done
  453.9 0.0 copy-start.5
  453.9 0.0 copy-start.9
  453.9 82.5 %last_reduce.1 = (f32[256,512]{1,0:T(8,128)S(1)}, f32[256,512]{1,0:T(8,128)S(1)}, f32[256,512]{1,0:T(8,128)S(1)}, f32[128,2048]{1,0:T(8,128)S(1)}, f32[64,128]{1,0:T(8,128)S(1)}, /*index=5*/f32[256,256]{1,0:T(8,128)S(1)}) custom-call(bf16[4,2,2,2,64,128]{5,4,3,2,1,0:T(8,128)(2,1)S(1)} %bitcast.16, bf16[4,2,256,1536]{3,2,1,0:T(8,128)(2,1)} %bitcast.21, ...), custom_call_target="tpu_custom_call" | custom-call | tf_op jit(solution)/shard_map/last_reduce/pallas_call | solution.py:1561
  536.4 0.0 copy-done.5
  536.4 1.1 add.29
  537.5 0.7 slice_reduce_fusion
  538.2 0.7 copy.68
  538.8 0.0 copy-done.9
  538.8 0.8 pad_maximum_fusion
  539.7 0.0 copy-start.4
  539.7 6.5 %convert_element_type.32 = f32[4,2048,256]{2,1,0:T(8,128)} convert(bf16[4,2048,256]{2,1,0:T(8,128)(2,1)} %get-tuple-element.77) | non-fusion elementwise | flops 2097152 | bytes 12582912 | tf_op jit(solution)/shard_map/convert_element_type | solution.py:1698
  546.1 0.0 copy-done.4
  546.1 0.0 copy-start.3
  546.1 4.1 convert_element_type.33
  550.3 0.0 copy-done.3
  550.3 0.0 copy-start.8
  550.3 4.4 convert_element_type.34
  554.7 0.0 copy-done.8
  554.7 0.8 copy.77
  555.5 0.8 copy.78
  556.3 0.8 copy.79
  557.1 0.8 copy.80
  (6 shorter events, 0.0 us)
Async XLA Ops:
  275.6 79.3 %copy-start.1 = (f32[128,2048]{1,0:T(8,128)S(1)}, f32[128,2048]{1,0:T(8,128)}, u32[]{:S(2)}) copy-start(f32[128,2048]{1,0:T(8,128)} %get-tuple-element.48.resid) | copy-start | bytes 3145732
  275.6 80.5 %copy-start.6 = (f32[128,128]{1,0:T(8,128)S(1)}, f32[128,128]{1,0:T(8,128)}, u32[]{:S(2)}) copy-start(f32[128,128]{1,0:T(8,128)} %get-tuple-element.57) | copy-start | bytes 196612
  275.7 80.6 %copy-start.7 = (bf16[2048,32]{0,1:T(8,128)(2,1)S(1)}, bf16[2048,32]{0,1:T(8,128)(2,1)}, u32[]{:S(2)}) copy-start(bf16[2048,32]{0,1:T(8,128)(2,1)} %param.24) | copy-start | bytes 393220
  275.7 80.6 %copy-start.10 = (f32[2048]{0:T(1024)S(1)}, f32[2048]{0:T(1024)}, u32[]{:S(2)}) copy-start(f32[2048]{0:T(1024)} %param.23) | copy-start | bytes 24580
  354.9 6.1 %copy-start.2 = (bf16[128,2048]{1,0:T(8,128)(2,1)S(1)}, bf16[128,2048]{1,0:T(8,128)(2,1)}, u32[]{:S(2)}) copy-start(bf16[128,2048]{1,0:T(8,128)(2,1)} %og.3) | copy-start | bytes 1572868
  452.6 1.2 copy-start
  453.9 82.5 %copy-start.5 = (f32[128,2048]{1,0:T(8,128)S(1)}, f32[128,2048]{1,0:T(8,128)}, u32[]{:S(2)}) copy-start(f32[128,2048]{1,0:T(8,128)} %get-tuple-element.145) | copy-start | bytes 3145732
  453.9 85.0 %copy-start.9 = (f32[256,256]{1,0:T(8,128)S(1)}, f32[256,256]{1,0:T(8,128)}, u32[]{:S(2)}) copy-start(f32[256,256]{1,0:T(8,128)} %get-tuple-element.75) | copy-start | bytes 786436
  539.7 6.5 %copy-start.4 = (bf16[4,2048,256]{2,1,0:T(8,128)(2,1)S(1)}, bf16[4,2048,256]{2,1,0:T(8,128)(2,1)}, u32[]{:S(2)}) copy-start(bf16[4,2048,256]{2,1,0:T(8,128)(2,1)} %get-tuple-element.78) | copy-start | bytes 12582916
  546.1 4.1 copy-start.3
  550.3 4.5 copy-start.8
